TPU v7x, 256 devices: a whole 4x4x8 slice. The times are simulated.
256 devices in a mesh: fsdp: 32 (over x, y, core), tensor: 8 (over z).
Axes of the slice: x: 4, y: 4, z: 8, core: 2. Of those that a mesh axis runs over, the one named last changes fastest.
Arguments:
- weight_q: bfloat16 [16384, 16384], P('fsdp', 'tensor'), may hold values from -6 to 6
- momentum_q: bfloat16 [16384, 16384], P('fsdp', 'tensor'), may hold values from -6 to 6
- grad_q: bfloat16 [16384, 16384], P('fsdp', 'tensor'), may hold values from -12 to 12
- basis_q: float32 [16384, 128], P(('tensor', 'fsdp')), may hold values from -0.046875 to 0.046875
- weight_k: bfloat16 [16384, 1024], P('fsdp', 'tensor'), may hold values from -6 to 6
- momentum_k: bfloat16 [16384, 1024], P('fsdp', 'tensor'), may hold values from -6 to 6
- grad_k: bfloat16 [16384, 1024], P('fsdp', 'tensor'), may hold values from -12 to 12
- basis_k: float32 [1024, 128], P(('tensor', 'fsdp')), may hold values from -0.1875 to 0.1875
- weight_v: bfloat16 [16384, 1024], P('fsdp', 'tensor'), may hold values from -6 to 6
- momentum_v: bfloat16 [16384, 1024], P('fsdp', 'tensor'), may hold values from -6 to 6
- grad_v: bfloat16 [16384, 1024], P('fsdp', 'tensor'), may hold values from -12 to 12
- basis_v: float32 [1024, 128], P(('tensor', 'fsdp')), may hold values from -0.1875 to 0.1875
Outputs:
- new_weight_q: bfloat16 [16384, 16384], P('fsdp', 'tensor')
- new_momentum_q: bfloat16 [16384, 16384], P('fsdp', 'tensor')
- new_basis_q: float32 [16384, 128], P(('tensor', 'fsdp'))
- new_weight_k: bfloat16 [16384, 1024], P('fsdp', 'tensor')
- new_momentum_k: bfloat16 [16384, 1024], P('fsdp', 'tensor')
- new_basis_k: float32 [1024, 128], P(('tensor', 'fsdp'))
- new_weight_v: bfloat16 [16384, 1024], P('fsdp', 'tensor')
- new_momentum_v: bfloat16 [16384, 1024], P('fsdp', 'tensor')
- new_basis_v: float32 [1024, 128], P(('tensor', 'fsdp'))
All inputs are finite; a program needn't handle non-finite values.
Results may differ from a plain program's by a relative error of at most 0.0017.
Values sent between devices are 32-bit elements; how exact they have to be, the bound alone decides.
No kernel may reach another device: no remote copies, remote signals or barrier semaphores. Data moves between devices by JAX's collectives and lax.ppermute only.
A program may use at most 64 MiB of HBM per device.

v0:
```python
import math

import jax
import jax.numpy as jnp
from jax import lax
from jax.sharding import PartitionSpec as P

RANK = 128


HIGH = lax.Precision.HIGHEST


def orthonormal(projected, gram):
    lower = jnp.linalg.cholesky(gram)
    return jax.scipy.linalg.solve_triangular(lower, projected.T, lower=True).T


def right_share(blend, ortho):
    return lax.psum_scatter(
        jnp.dot(blend.T, ortho, precision=HIGH), "fsdp", scatter_dimension=0, tiled=True
    )


def body(
    weight_q,
    momentum_q,
    grad_q,
    basis_q,
    weight_k,
    momentum_k,
    grad_k,
    basis_k,
    weight_v,
    momentum_v,
    grad_v,
    basis_v,
):
    weights = (weight_q, weight_k, weight_v)
    moments = (momentum_q, momentum_k, momentum_v)
    grads = (grad_q, grad_k, grad_v)
    bases = (
        lax.all_gather(basis_q, "fsdp", axis=0, tiled=True),
        lax.all_gather(basis_k, "fsdp", axis=0, tiled=True),
        lax.all_gather(basis_v, "fsdp", axis=0, tiled=True),
    )
    blends = [m.astype(jnp.float32) + g.astype(jnp.float32) for m, g in zip(moments, grads)]
    partial_rows = tuple((jnp.dot(b, q, precision=HIGH) for b, q in zip(blends, bases)))
    projected = lax.psum(partial_rows, "tensor")
    local_grams = tuple((jnp.dot(p.T, p, precision=HIGH) for p in projected))
    grams = lax.psum(local_grams, "fsdp")
    orthos = [orthonormal(p, g) for p, g in zip(projected, grams)]
    shares = [right_share(b, o) for b, o in zip(blends, orthos)]
    squares = lax.psum(tuple((jnp.sum(s * s, axis=0) for s in shares)), ("fsdp", "tensor"))
    inverses = [lax.rsqrt(s + 1e-06) for s in squares]
    new_bases = [s * inv for s, inv in zip(shares, inverses)]
    rights = lax.all_gather(tuple(shares), "fsdp", axis=0, tiled=True)
    results = []
    for w, b, o, r, inv, nb in zip(weights, blends, orthos, rights, inverses, new_bases):
        new_momentum = (b - 0.5 * jnp.dot(o, r.T, precision=HIGH)).astype(jnp.bfloat16)
        rows_all = w.shape[0] * lax.axis_size("fsdp")
        cols_all = w.shape[1] * lax.axis_size("tensor")
        factor = 0.25 * math.sqrt(rows_all * cols_all / RANK)
        update = jnp.dot(o, (r * inv).T, precision=HIGH)
        new_weight = (w.astype(jnp.float32) - factor * update).astype(jnp.bfloat16)
        results.extend([new_weight, new_momentum, nb])
    return tuple(results)


def solution(mesh):
    placed = (
        P("fsdp", "tensor"),
        P("fsdp", "tensor"),
        P("fsdp", "tensor"),
        P(("tensor", "fsdp"), None),
        P("fsdp", "tensor"),
        P("fsdp", "tensor"),
        P("fsdp", "tensor"),
        P(("tensor", "fsdp"), None),
        P("fsdp", "tensor"),
        P("fsdp", "tensor"),
        P("fsdp", "tensor"),
        P(("tensor", "fsdp"), None),
    )
    return jax.shard_map(
        body,
        mesh=mesh,
        in_specs=placed,
        out_specs=(
            P("fsdp", "tensor"),
            P("fsdp", "tensor"),
            P(("tensor", "fsdp"), None),
            P("fsdp", "tensor"),
            P("fsdp", "tensor"),
            P(("tensor", "fsdp"), None),
            P("fsdp", "tensor"),
            P("fsdp", "tensor"),
            P(("tensor", "fsdp"), None),
        ),
        check_vma=False,
    )
```

profile of v0, /device:TPU:1, one launch (start us, length us, event | category | flops | bytes accessed | tf_op | source)
XLA Modules:
  0.0 696.9 jit_solution(5019335754920247637)
XLA Ops:
  8.0 25.8 %all-gather = f32[32,4,128]{2,1,0:T(4,128)S(1)} all-gather(f32[1,4,128]{2,1,0:T(4,128)} %bitcast.74), channel_id=1, replica_groups=mesh['fsdp'=32,'tensor'=8] {'fsdp'}, dimensions={0}, use_global_device_ids=true | all-gather | bytes 67584 | tf_op jit(solution)/shard_map/all_gather | solution.py:44
  33.8 23.5 %all-gather.2 = f32[32,4,128]{2,1,0:T(4,128)S(1)} all-gather(f32[1,4,128]{2,1,0:T(4,128)} %bitcast.75), channel_id=1, replica_groups=mesh['fsdp'=32,'tensor'=8] {'fsdp'}, dimensions={0}, use_global_device_ids=true | all-gather | bytes 67584 | tf_op jit(solution)/shard_map/all_gather | solution.py:45
  57.2 2.1 fusion.21
  59.3 2.0 fusion.19
  61.3 1.3 all-gather.7.cloned.1.call-done
  62.6 6.7 fusion.1
  69.5 69.7 %all-reduce.14.cloned.1.call-done = (f32[512,128]{1,0:T(8,128)}, f32[512,128]{1,0:T(8,128)}, f32[512,128]{1,0:T(8,128)}) async-done(((f32[512,128]{1,0:T(8,128)}, f32[512,128]{1,0:T(8,128)}, f32[512,128]{1,0:T(8,128)}), (f32[512,128]{1,0:T(8,128)}, f32[512,128]{1,0:T(8,128)}, f32[512,128]{1,0:T(8,128)})) %all-reduce.14.cloned.1.call-update) | async-done | bytes 786448 | tf_op jit(solution)/shard_map/psum | solution.py:49
  139.2 2.3 fusion.36
  141.5 2.3 fusion.37
  144.3 2.3 fusion.35
  146.6 109.9 %all-reduce.12.cloned.1.call-done = (f32[128,128]{0,1:T(8,128)}, f32[128,128]{0,1:T(8,128)}) async-done(((f32[128,128]{0,1:T(8,128)}, f32[128,128]{0,1:T(8,128)}), (f32[128,128]{0,1:T(8,128)}, f32[128,128]{0,1:T(8,128)})) %all-reduce.12.cloned.1.call-update) | async-done | bytes 131088 | tf_op jit(solution)/shard_map/psum | solution.py:51
  258.3 1.5 fusion.26
  259.9 11.7 %cholesky.81 = f32[128,128]{1,0:T(8,128)S(1)} custom-call(f32[128,128]{1,0:T(8,128)S(1)} %get-tuple-element.26), custom_call_target="Cholesky" | custom-call | tf_op jit(solution)/shard_map/jit(cholesky)/cholesky | solution.py:15
  272.9 10.4 %custom-call.9 = f32[1,128,128]{1,2,0:T(8,128)} custom-call(f32[1,128,128]{2,1,0:T(8,128)S(1)} %fusion.24), custom_call_target="InvertDiagBlocksLowerTriangular" | custom-call | tf_op jit(solution)/shard_map/jit(_solve_triangular)/triangular_solve | solution.py:16
  284.6 12.6 %cholesky.70 = f32[128,128]{1,0:T(8,128)S(1)} custom-call(f32[128,128]{1,0:T(8,128)} %get-tuple-element.27), custom_call_target="Cholesky" | custom-call | tf_op jit(solution)/shard_map/jit(cholesky)/cholesky | solution.py:15
  298.5 10.6 %custom-call.8 = f32[1,128,128]{1,2,0:T(8,128)} custom-call(f32[1,128,128]{2,1,0:T(8,128)S(1)} %fusion.23), custom_call_target="InvertDiagBlocksLowerTriangular" | custom-call | tf_op jit(solution)/shard_map/jit(_solve_triangular)/triangular_solve | solution.py:16
  309.1 1.3 fusion.14
  311.6 2.1 fusion.20
  313.8 109.9 %all-reduce.10.cloned.1.call-done = (f32[128,128]{0,1:T(8,128)}, f32[128,128]{1,0:T(8,128)}, f32[128,128]{1,0:T(8,128)}) async-done(((f32[128,128]{0,1:T(8,128)}, f32[128,128]{1,0:T(8,128)}, f32[128,128]{1,0:T(8,128)}), (f32[128,128]{0,1:T(8,128)}, f32[128,128]{1,0:T(8,128)}, f32[128,128]{1,0:T(8,128)})) %all-reduce.10.cloned.1.call-update) | async-done | bytes 196624 | tf_op jit(solution)/shard_map/psum | solution.py:51
  425.6 11.7 %cholesky.59 = f32[128,128]{1,0:T(8,128)S(1)} custom-call(f32[128,128]{1,0:T(8,128)S(1)} %fusion.30), custom_call_target="Cholesky" | custom-call | tf_op jit(solution)/shard_map/jit(cholesky)/cholesky | solution.py:15
  438.6 10.4 %custom-call.7 = f32[1,128,128]{1,2,0:T(8,128)} custom-call(f32[1,128,128]{2,1,0:T(8,128)S(1)} %fusion.22), custom_call_target="InvertDiagBlocksLowerTriangular" | custom-call | tf_op jit(solution)/shard_map/jit(_solve_triangular)/triangular_solve | solution.py:16
  450.4 9.5 %fusion = f32[2048,128]{1,0:T(8,128)} fusion(f32[128,512]{1,0:T(8,128)S(1)} %fusion.16, bf16[512,2048]{1,0:T(8,128)(2,1)S(1)} %copy-done, bf16[512,2048]{1,0:T(8,128)(2,1)} %param.16), kind=kOutput, calls=%fused_computation.3 | convolution fusion | flops 1613758464 | bytes 5505024 | tf_op jit(solution)/shard_map/dot_general | solution.py:21
  462.6 80.1 %reduce-scatter.2.cloned.1.call-done = f32[64,128]{1,0:T(8,128)} async-done(((f32[2048,128]{1,0:T(8,128)}), f32[64,128]{1,0:T(8,128)}) %reduce-scatter.2.cloned.1.call-update) | async-done | bytes 32784 | tf_op jit(solution)/shard_map/reduce_scatter | solution.py:20
  543.5 77.2 %all-reduce.2 = (f32[128]{0:T(128)S(1)}, f32[128]{0:T(128)}, f32[128]{0:T(128)}) all-reduce(f32[128]{0:T(128)S(1)} %multiply_reduce_fusion, f32[128]{0:T(128)S(1)} %multiply_reduce_fusion.2, f32[128]{0:T(128)S(1)} %multiply_reduce_fusion.1), channel_id=1, replica_groups=mesh['fsdp'=32,'tensor'=8] {'fsdp','tensor'}, use_global_device_ids=true, to_apply=%region_6.0 | all-reduce | flops 384 | bytes 3072 | tf_op jit(solution)/shard_map/psum | solution.py:54
  621.4 1.3 dynamic-slice_multiply_fusion
  622.6 22.1 %all-gather.3 = f32[32,4,128]{2,1,0:T(4,128)S(1)} all-gather(f32[1,4,128]{2,1,0:T(4,128)S(1)} %get-tuple-element.23), channel_id=1, replica_groups=mesh['fsdp'=32,'tensor'=8] {'fsdp'}, dimensions={0}, use_global_device_ids=true | all-gather | bytes 67584 | tf_op jit(solution)/shard_map/all_gather | solution.py:57
  645.4 1.3 dynamic-slice_multiply_fusion.1
  646.7 24.2 %all-gather.1 = f32[32,4,128]{2,1,0:T(4,128)S(1)} all-gather(f32[1,4,128]{2,1,0:T(4,128)S(1)} %get-tuple-element.25), channel_id=1, replica_groups=mesh['fsdp'=32,'tensor'=8] {'fsdp'}, dimensions={0}, use_global_device_ids=true | all-gather | bytes 67584 | tf_op jit(solution)/shard_map/all_gather | solution.py:57
  670.9 1.4 broadcast_multiply_fusion
  673.6 2.2 fusion.8
  678.2 6.8 subtract_convert_fusion
  685.0 4.8 subtract_convert_fusion.1
  (63 shorter events, 20.7 us)
Async XLA Ops:
  7.2 55.5 %all-gather.7.cloned.1.call-start = ((), (), s32[]{:S(2)}) async-start(), calls=%async_computation.1 | async-start | bytes 1081344 | tf_op jit(solution)/shard_map/all_gather | solution.py:43
  7.9 131.3 %all-reduce.14.cloned.1.call-start = ((), (), s32[]{:S(2)}) async-start(), calls=%async_computation.6 | async-start | bytes 1572864 | tf_op jit(solution)/shard_map/psum | solution.py:49
  69.4 241.0 %copy-start.6 = (bf16[512,128]{1,0:T(8,128)(2,1)S(1)}, bf16[512,128]{1,0:T(8,128)(2,1)}, u32[]{:S(2)}) copy-start(bf16[512,128]{1,0:T(8,128)(2,1)} %param.21) | copy-start | bytes 393220
  69.4 241.0 %copy-start.7 = (bf16[512,128]{1,0:T(8,128)(2,1)S(1)}, bf16[512,128]{1,0:T(8,128)(2,1)}, u32[]{:S(2)}) copy-start(bf16[512,128]{1,0:T(8,128)(2,1)} %param.20) | copy-start | bytes 393220
  69.4 187.0 %all-reduce.12.cloned.1.call-start = ((), (), s32[]{:S(2)}) async-start(), calls=%async_computation.5 | async-start | bytes 262144 | tf_op jit(solution)/shard_map/psum | solution.py:51
  139.2 144.2 %copy-start.4 = (f32[512,128]{1,0:T(8,128)S(1)}, f32[512,128]{1,0:T(8,128)}, u32[]{:S(2)}) copy-start(f32[512,128]{1,0:T(8,128)} %get-tuple-element.21) | copy-start | bytes 786436
  139.2 169.9 %copy-start.3 = (f32[512,128]{1,0:T(8,128)S(1)}, f32[512,128]{1,0:T(8,128)}, u32[]{:S(2)}) copy-start(f32[512,128]{1,0:T(8,128)} %get-tuple-element.20) | copy-start | bytes 786436
  141.5 170.1 %copy-start.8 = (bf16[512,128]{1,0:T(8,128)(2,1)S(1)}, bf16[512,128]{1,0:T(8,128)(2,1)}, u32[]{:S(2)}) copy-start(bf16[512,128]{1,0:T(8,128)(2,1)} %param.25) | copy-start | bytes 393220
  143.8 279.9 %all-reduce.10.cloned.1.call-start = ((), (), s32[]{:S(2)}) async-start(), calls=%async_computation.4 | async-start | bytes 393216 | tf_op jit(solution)/shard_map/psum | solution.py:51
  146.6 302.5 %copy-start.2 = (f32[512,128]{1,0:T(8,128)S(1)}, f32[512,128]{1,0:T(8,128)}, u32[]{:S(2)}) copy-start(f32[512,128]{1,0:T(8,128)} %get-tuple-element.19) | copy-start | bytes 786436
  259.9 190.5 %copy-start = (bf16[512,2048]{1,0:T(8,128)(2,1)S(1)}, bf16[512,2048]{1,0:T(8,128)(2,1)}, u32[]{:S(2)}) copy-start(bf16[512,2048]{1,0:T(8,128)(2,1)} %param.17) | copy-start | bytes 6291460
  313.8 228.9 %reduce-scatter.2.cloned.1.call-start = ((), (), s32[]{:S(2)}) async-start(), calls=%async_computation.2 | async-start | bytes 1081344 | tf_op jit(solution)/shard_map/reduce_scatter | solution.py:20
  450.3 9.6 %copy-start.11 = (u32[256]{0:T(256)S(1)}, u32[256]{0:T(256)}, u32[]{:S(2)}) copy-start(u32[256]{0:T(256)} %constant.47) | copy-start | bytes 3076
  450.4 222.0 %copy-start.10 = (bf16[512,128]{1,0:T(8,128)(2,1)S(1)}, bf16[512,128]{1,0:T(8,128)(2,1)}, u32[]{:S(2)}) copy-start(bf16[512,128]{1,0:T(8,128)(2,1)} %param.19) | copy-start | bytes 393220
  459.9 217.1 %copy-start.9 = (bf16[512,128]{1,0:T(8,128)(2,1)S(1)}, bf16[512,128]{1,0:T(8,128)(2,1)}, u32[]{:S(2)}) copy-start(bf16[512,128]{1,0:T(8,128)(2,1)} %param.24) | copy-start | bytes 393220
  459.9 218.3 %all-gather.9.cloned.1.call-start = ((), (), s32[]{:S(2)}) async-start(), calls=%async_computation.3 | async-start | bytes 1081344 | tf_op jit(solution)/shard_map/all_gather | solution.py:57
  678.2 6.8 copy-start.1
  678.2 6.8 copy-start.5
Sparse Core Ops, SparseCore 0:
  10.6 52.0 all-gather.6
  69.5 69.6 all-reduce.13
  143.9 112.4 all-reduce.11
  313.9 109.8 all-reduce.9
  460.0 82.6 reduce-scatter.1
  621.5 44.8 all-gather.8
where the time goes:
time: 703 us; the launch traced here: 697 us
  waiting for transfers between devices  372 us (53%)
  blocking collectives  173 us (25%)
  other arithmetic  81.2 us (12%)
  matrix products  51.9 us (7%)
  between operations  15.2 us (2%)
    psum x2, waiting for transfers between devices, body(): grams = lax.psum(local_grams, 'fsdp')  220 us
    reduce_scatter x1, waiting for transfers between devices, right_share(): lax.psum_scatter(jnp.dot(blend.T, ortho, precision=HIGH), 'fsdp', scatter...  80.1 us
    psum x1, blocking collectives, body(): lax.psum(tuple((jnp.sum(s * s, axis=0) for s in shares)), ('fsdp', 'tenso...  77.2 us
    psum x1, waiting for transfers between devices, body(): projected = lax.psum(partial_rows, 'tensor')  69.7 us
    all_gather x2, blocking collectives, body(): rights = lax.all_gather(tuple(shares), 'fsdp', axis=0, tiled=True)  46.4 us
    another operation x9, other arithmetic, orthonormal(): lower = jnp.linalg.cholesky(gram)  38 us
    another operation x6, other arithmetic, orthonormal(): return jax.scipy.linalg.solve_triangular(lower, projected.T, lower=True).T  33.4 us
    all_gather x1, blocking collectives, body(): lax.all_gather(basis_k, 'fsdp', axis=0, tiled=True)  25.8 us
  transfers between devices with their start and end apart: 6, of which 5 were waited for; matrix products, arithmetic and copies ran while one was open for 3% of the time, Pallas kernels for 0%

commit v1 on v0

v1 whole, which is shorter than its diff:
```python
import math

import jax
import jax.numpy as jnp
from jax import lax
from jax.sharding import PartitionSpec as P

RANK = 128
HIGH = lax.Precision.HIGHEST
PLANE = [[2 * i + c for i in range(16)] for c in range(2)]
SIBLING = [(i, i ^ 1) for i in range(32)]


def swap_core(x):
    return lax.ppermute(x, "fsdp", SIBLING)


def plane_exchange(x):
    return lax.all_to_all(x, "fsdp", 0, 0, tiled=True, axis_index_groups=PLANE)


def tensor_exchange(x):
    return lax.all_to_all(x, "tensor", 0, 0, tiled=True)


def gather_fsdp(x, core):
    mine = plane_exchange(jnp.broadcast_to(x[None], (16,) + x.shape))
    other = swap_core(mine)
    low = jnp.where(core == 0, mine, other)
    high = jnp.where(core == 0, other, mine)
    return jnp.stack([low, high], axis=1)


def scatter_fsdp(x, core):
    keep = jnp.where(core == 0, x[:, 0], x[:, 1])
    send = jnp.where(core == 0, x[:, 1], x[:, 0])
    paired = keep + swap_core(send)
    return jnp.sum(plane_exchange(paired), axis=0)


def body(
    weight_q,
    momentum_q,
    grad_q,
    basis_q,
    weight_k,
    momentum_k,
    grad_k,
    basis_k,
    weight_v,
    momentum_v,
    grad_v,
    basis_v,
):
    weights = (weight_q, weight_k, weight_v)
    moments = (momentum_q, momentum_k, momentum_v)
    grads = (grad_q, grad_k, grad_v)
    fsdp = lax.axis_index("fsdp")
    core = lax.rem(fsdp, 2)

    packed = jnp.concatenate([basis_q, basis_k, basis_v], axis=0)
    bases = gather_fsdp(packed, core).reshape(32, 72, RANK)
    bases = (
        bases[:, :64].reshape(2048, RANK),
        bases[:, 64:68].reshape(128, RANK),
        bases[:, 68:].reshape(128, RANK),
    )
    blends = [m.astype(jnp.float32) + g.astype(jnp.float32) for m, g in zip(moments, grads)]
    partial_rows = jnp.concatenate(
        [jnp.dot(b, q, precision=HIGH).reshape(8, 64, RANK) for b, q in zip(blends, bases)], axis=1
    )
    own_rows = jnp.sum(tensor_exchange(partial_rows), axis=0)
    rows = lax.all_gather(own_rows, "tensor", axis=0)
    projected = [rows[:, 64 * i : 64 * i + 64].reshape(512, RANK) for i in range(3)]

    rights = [jnp.dot(b.T, p, precision=HIGH) for b, p in zip(blends, projected)]
    grams = [jnp.dot(p.T, p, precision=HIGH) for p in projected]
    pad = jnp.zeros((128, RANK), jnp.float32)
    full = jnp.concatenate(rights + grams + [pad], axis=0)
    share = scatter_fsdp(full.reshape(16, 2, 88, RANK), core)
    full = gather_fsdp(share, core).reshape(2816, RANK)
    rights = (full[:2048], full[2048:2176], full[2176:2304])
    grams = full[2304:2688].reshape(3, RANK, RANK)

    lowers = jnp.linalg.cholesky(grams)
    eye = jnp.broadcast_to(jnp.eye(RANK, dtype=jnp.float32), grams.shape)
    inverse_lowers = jax.scipy.linalg.solve_triangular(lowers, eye, lower=True)
    orthos = [jnp.dot(p, li.T, precision=HIGH) for p, li in zip(projected, inverse_lowers)]
    rights = [jnp.dot(r, li.T, precision=HIGH) for r, li in zip(rights, inverse_lowers)]
    squares = jnp.stack([jnp.sum(r * r, axis=0) for r in rights])
    squares = jnp.sum(tensor_exchange(jnp.broadcast_to(squares[None], (8, 3, RANK))), axis=0)
    inverses = lax.rsqrt(squares + 1e-06)
    results = []
    for i in range(3):
        w, b, o, r = weights[i], blends[i], orthos[i], rights[i]
        new_momentum = (b - 0.5 * jnp.dot(o, r.T, precision=HIGH)).astype(jnp.bfloat16)
        rows_all = w.shape[0] * lax.axis_size("fsdp")
        cols_all = w.shape[1] * lax.axis_size("tensor")
        factor = 0.25 * math.sqrt(rows_all * cols_all / RANK)
        basis = r * inverses[i]
        update = jnp.dot(o, basis.T, precision=HIGH)
        new_weight = (w.astype(jnp.float32) - factor * update).astype(jnp.bfloat16)
        own = basis.shape[0] // 32
        results.extend([new_weight, new_momentum, lax.dynamic_slice_in_dim(basis, fsdp * own, own)])
    return tuple(results)


def solution(mesh):
    placed = (
        P("fsdp", "tensor"),
        P("fsdp", "tensor"),
        P("fsdp", "tensor"),
        P(("tensor", "fsdp"), None),
    ) * 3
    return jax.shard_map(
        body,
        mesh=mesh,
        in_specs=placed,
        out_specs=(
            P("fsdp", "tensor"),
            P("fsdp", "tensor"),
            P(("tensor", "fsdp"), None),
        )
        * 3,
        check_vma=False,
    )
```

time: 703 us -> 247 us (0.35)
  waiting for transfers between devices: 372 us -> 11.6 us
  blocking collectives: 173 us -> 82.9 us
  starting transfers between devices: 0.71 us -> 22.4 us
  between operations: 15.2 us -> 1.09 us
  matrix products: 51.9 us -> 42 us
    psum x3 -> x0, waiting for transfers between devices: 290 us -> none  [the longest x2 220 us: body(): grams = lax.psum(local_grams, 'fsdp')]
    reduce_scatter x1 -> x0, waiting for transfers between devices: 80.1 us -> none  [right_share(): lax.psum_scatter(jnp.dot(blend.T, ortho, precision=HIGH), 'fsdp', scatter...]
    psum x1 -> x0, blocking collectives: 77.2 us -> none  [body(): lax.psum(tuple((jnp.sum(s * s, axis=0) for s in shares)), ('fsdp', 'tenso...]
    all_gather x4 -> x1, blocking collectives: 95.6 us -> 20.6 us  [body(): rows = lax.all_gather(own_rows, 'tensor', axis=0)]
    all_to_all x0 -> x3, blocking collectives: none -> 62.3 us  [the longest x1 31.6 us: tensor_exchange(): return lax.all_to_all(x, 'tensor', 0, 0, tiled=True)]
    ppermute x0 -> x3, starting transfers between devices: none -> 11.3 us  [swap_core(): return lax.ppermute(x, 'fsdp', SIBLING)]
    all_to_all x0 -> x2, starting transfers between devices: none -> 11.2 us  [the longest x1 7.58 us: plane_exchange(): return lax.all_to_all(x, 'fsdp', 0, 0, tiled=True, axis_index_groups=PLANE)]
    all_to_all x0 -> x2, waiting for transfers between devices: none -> 9.26 us  [the longest x1 9.25 us: plane_exchange(): return lax.all_to_all(x, 'fsdp', 0, 0, tiled=True, axis_index_groups=PLANE)]
  transfers between devices with their start and end apart: 6 -> 5, of which waited for: 5 -> 3; matrix products, arithmetic and copies ran while one was open for 3% -> 6% of each run, Pallas kernels for 0% -> 0%
where the time goes in v1:
time: 247 us; the launch traced here: 246 us
  blocking collectives  82.9 us (34%)
  other arithmetic  79.2 us (32%)
  matrix products  42 us (17%)
  starting transfers between devices  22.4 us (9%)
  waiting for transfers between devices  11.6 us (5%)
  local copies, waits for them, and re-layouts  6.81 us (3%)
    another operation x4, other arithmetic, body(): lowers = jnp.linalg.cholesky(grams)  38.3 us
    another operation x3, other arithmetic, body(): inverse_lowers = jax.scipy.linalg.solve_triangular(lowers, eye, lower=True)  32.6 us
    all_to_all x1, blocking collectives, tensor_exchange(): return lax.all_to_all(x, 'tensor', 0, 0, tiled=True)  31.6 us
    all_to_all x2, blocking collectives, plane_exchange(): return lax.all_to_all(x, 'fsdp', 0, 0, tiled=True, axis_index_groups=PLANE)  30.7 us
    all_gather x1, blocking collectives, body(): rows = lax.all_gather(own_rows, 'tensor', axis=0)  20.6 us
    ppermute x3, starting transfers between devices, swap_core(): return lax.ppermute(x, 'fsdp', SIBLING)  11.3 us
    dot_general x3, matrix products, body(): jnp.dot(o, r.T, precision=HIGH)  9.3 us
    all_to_all x1, waiting for transfers between devices, plane_exchange(): return lax.all_to_all(x, 'fsdp', 0, 0, tiled=True, axis_index_groups=PLANE)  9.25 us
  transfers between devices with their start and end apart: 5, of which 3 were waited for; matrix products, arithmetic and copies ran while one was open for 6% of the time, Pallas kernels for 0%

profile of v1, /device:TPU:1, one launch (start us, length us, event | category | flops | bytes accessed | tf_op | source)
XLA Modules:
  0.0 246.1 jit_solution(1873026335989151887)
XLA Ops:
  2.5 7.6 %all-to-all-start = ((f32[16,72,128]{2,1,0:T(8,128)}), f32[16,72,128]{2,1,0:T(8,128)S(1)}, u32[]{:S(2)}, u32[]{:S(2)}) async-start(f32[16,72,128]{2,1,0:T(8,128)} %broadcast_in_dim.14), calls=%async_computation | async-start | bytes 1179648 | tf_op jit(solution)/shard_map/all_to_all | solution.py:19
  10.1 1.7 convert_add_fusion.2
  11.8 9.3 %all-to-all-done = f32[16,72,128]{2,1,0:T(8,128)S(1)} async-done(((f32[16,72,128]{2,1,0:T(8,128)}), f32[16,72,128]{2,1,0:T(8,128)S(1)}, u32[]{:S(2)}, u32[]{:S(2)}) %all-to-all-start) | async-done | bytes 589856 | tf_op jit(solution)/shard_map/all_to_all | solution.py:19
  21.1 1.9 collective-permute-start
  22.9 2.4 convert_add_fusion
  27.1 3.4 %fusion.32 = f32[8,64,128]{2,1,0:T(8,128)S(1)} fusion(f32[8,64,2048]{2,1,0:T(8,128)S(1)} %bitcast.122, f32[2048,128,1]{1,0,2:T(8,128)S(1)} %bitcast.135), kind=kOutput, calls=%fused_computation.81 | convolution fusion | flops 1610612736 | bytes 5505024 | tf_op jit(solution)/shard_map/dot_general | solution.py:70
  30.6 31.6 %all_to_all.25 = f32[8,192,128]{2,1,0:T(8,128)S(1)} all-to-all(f32[8,192,128]{2,1,0:T(8,128)S(1)} %pad_maximum_fusion.2), channel_id=1, replica_groups=mesh['fsdp'=32,'tensor'=8] {'tensor'}, dimensions={0} | all-to-all | bytes 1572864 | tf_op jit(solution)/shard_map/all_to_all | solution.py:23
  62.3 20.6 %all-gather = f32[1536,128]{1,0:T(8,128)S(1)} all-gather(f32[192,128]{1,0:T(8,128)S(1)} %reduce_sum.54), channel_id=2, replica_groups=mesh['fsdp'=32,'tensor'=8] {'tensor'}, dimensions={0}, use_global_device_ids=true | all-gather | bytes 884736 | tf_op jit(solution)/shard_map/all_gather | solution.py:73
  83.0 7.0 %convolution_dynamic-update-slice_fusion = f32[2816,128]{1,0:T(8,128)S(1)} fusion(f32[512,128]{1,0:T(8,128)S(1)} %bitcast.140, bf16[512,2048]{1,0:T(8,128)(2,1)S(1)} %copy-done, bf16[512,2048]{1,0:T(8,128)(2,1)S(1)} %copy-done.1), kind=kOutput, calls=%fused_computation.3 | convolution fusion | flops 1613758464 | bytes 5505024 | tf_op jit(solution)/shard_map/dot_general | solution.py:76
  93.1 6.4 %collective-permute-start.1 = (f32[16,88,128]{2,1,0:T(8,128)S(1)}, f32[16,88,128]{2,1,0:T(8,128)S(1)}, u32[]{:S(2)}, u32[]{:S(2)}) collective-permute-start(f32[16,88,128]{2,1,0:T(8,128)S(1)} %select_bitcast_fusion.2), channel_id=1, source_target_pairs={{0,8},{8,0},{16,24},{24,16},{32,40},{40,32},{48,56},{56,48},{64,72... | collective-permute-start | bytes 2162696 | tf_op jit(solution)/shard_map/ppermute | solution.py:15
  99.6 1.8 collective-permute-done.1
  101.5 15.8 %all_to_all.26 = f32[16,88,128]{2,1,0:T(8,128)S(1)} all-to-all(f32[16,88,128]{2,1,0:T(8,128)S(1)} %fusion.14), channel_id=1, replica_groups={{0,16,32,48,64,80,96,112,128,144,160,176,192,208,224,240},{8,24,40,56,7..., dimensions={0} | all-to-all | bytes 1441792 | tf_op jit(solution)/shard_map/all_to_all | solution.py:19
  117.4 14.9 %all_to_all.27 = f32[16,88,128]{2,1,0:T(8,128)S(1)} all-to-all(f32[16,88,128]{2,1,0:T(8,128)S(1)} %broadcast_in_dim.16), channel_id=1, replica_groups={{0,16,32,48,64,80,96,112,128,144,160,176,192,208,224,240},{8,24,40,56,7..., dimensions={0} | all-to-all | bytes 1441792 | tf_op jit(solution)/shard_map/all_to_all | solution.py:19
  132.3 3.0 %collective-permute-start.2 = (f32[16,88,128]{2,1,0:T(8,128)S(1)}, f32[16,88,128]{2,1,0:T(8,128)S(1)}, u32[]{:S(2)}, u32[]{:S(2)}) collective-permute-start(f32[16,88,128]{2,1,0:T(8,128)S(1)} %all_to_all.27), channel_id=1, source_target_pairs={{0,8},{8,0},{16,24},{24,16},{32,40},{40,32},{48,56},{56,48},{64,72... | collective-permute-start | bytes 2162696 | tf_op jit(solution)/shard_map/ppermute | solution.py:15
  138.1 1.7 copy.50
  139.9 1.7 fusion.17
  141.6 36.6 %custom-call.8 = f32[3,128,128]{2,1,0:T(8,128)} custom-call(f32[3,128,128]{2,1,0:T(8,128)} %fusion.17), custom_call_target="Cholesky" | custom-call | tf_op jit(solution)/shard_map/jit(cholesky)/cholesky | solution.py:85
  178.2 1.0 select_reduce_fusion
  179.3 1.7 select_bitcast_fusion.5
  181.0 30.9 %custom-call.9 = f32[3,1,128,128]{2,3,1,0:T(8,128)} custom-call(f32[3,1,128,128]{3,2,1,0:T(8,128)} %select_bitcast_fusion.5), custom_call_target="InvertDiagBlocksLowerTriangular" | custom-call | tf_op jit(solution)/shard_map/jit(_solve_triangular)/vmap()/triangular_solve | solution.py:87
  211.9 1.5 fusion.15
  213.4 2.0 fusion.25
  217.2 2.3 multiply_reduce_fusion
  219.5 1.1 fusion.24
  220.6 1.1 fusion.23
  222.3 3.6 %all-to-all-start.4 = ((f32[8,3,128]{2,1,0:T(4,128)}), f32[8,3,128]{2,1,0:T(4,128)S(1)}, u32[]{:S(2)}, u32[]{:S(2)}) async-start(f32[8,3,128]{2,1,0:T(4,128)} %broadcast_in_dim.32), calls=%async_computation.4 | async-start | bytes 32768 | tf_op jit(solution)/shard_map/all_to_all | solution.py:23
  225.9 2.0 fusion.7
  228.0 6.2 %subtract_convert_fusion = bf16[512,2048]{1,0:T(8,128)(2,1)} fusion(f32[512,128]{1,0:T(8,128)} %fusion.23, f32[2048,128]{1,0:T(8,128)S(1)} %get-tuple-element.26, bf16[512,2048]{1,0:T(8,128)(2,1)S(1)} %copy-done, bf16[512,2048]{1,0:T(8,128)(2,1)} %param.13), kind=kOutput, calls=%fused_computation | convolution fusion | flops 1616904192 | bytes 7602176 | tf_op jit(solution)/shard_map/dot_general | solution.py:96
  234.2 1.0 fusion.5
  235.3 2.1 fusion.6
  238.6 2.0 fusion.4
  240.7 4.7 %subtract_convert_fusion.1 = bf16[512,2048]{1,0:T(8,128)(2,1)} fusion(bf16[512,2048]{1,0:T(8,128)(2,1)S(1)} %copy-done.11, f32[512,128]{1,0:T(8,128)S(1)} %copy-done.10, f32[2048,128]{1,0:T(8,128)S(1)} %broadcast_multiply_fusion), kind=kOutput, calls=%fused_computation.1 | convolution fusion | flops 1614807040 | bytes 5505024 | tf_op jit(solution)/shard_map/dot_general | solution.py:101
  (86 shorter events, 14.3 us)
Async XLA Ops:
  0.6 11.1 %copy-start.13 = (bf16[512,128]{1,0:T(8,128)(2,1)S(1)}, bf16[512,128]{1,0:T(8,128)(2,1)}, u32[]{:S(2)}) copy-start(bf16[512,128]{1,0:T(8,128)(2,1)} %param.21) | copy-start | bytes 393220
  0.7 11.1 %copy-start.12 = (bf16[512,128]{1,0:T(8,128)(2,1)S(1)}, bf16[512,128]{1,0:T(8,128)(2,1)}, u32[]{:S(2)}) copy-start(bf16[512,128]{1,0:T(8,128)(2,1)} %param.22) | copy-start | bytes 393220
  0.7 22.3 %copy-start = (bf16[512,2048]{1,0:T(8,128)(2,1)S(1)}, bf16[512,2048]{1,0:T(8,128)(2,1)}, u32[]{:S(2)}) copy-start(bf16[512,2048]{1,0:T(8,128)(2,1)} %param.14) | copy-start | bytes 6291460
  2.5 18.6 %all-to-all-start = ((f32[16,72,128]{2,1,0:T(8,128)}), f32[16,72,128]{2,1,0:T(8,128)S(1)}, u32[]{:S(2)}, u32[]{:S(2)}) async-start(f32[16,72,128]{2,1,0:T(8,128)} %broadcast_in_dim.14), calls=%async_computation | async-start | bytes 1179648 | tf_op jit(solution)/shard_map/all_to_all | solution.py:19
  21.1 4.3 %collective-permute-start = (f32[16,72,128]{2,1,0:T(8,128)S(1)}, f32[16,72,128]{2,1,0:T(8,128)S(1)}, u32[]{:S(2)}, u32[]{:S(2)}) collective-permute-start(f32[16,72,128]{2,1,0:T(8,128)S(1)} %all-to-all-done), channel_id=1, source_target_pairs={{0,8},{8,0},{16,24},{24,16},{32,40},{40,32},{48,56},{56,48},{64,72... | collective-permute-start | bytes 1769480 | tf_op jit(solution)/shard_map/ppermute | solution.py:15
  25.4 1.0 copy-start.18
  62.2 20.7 %copy-start.1 = (bf16[512,2048]{1,0:T(8,128)(2,1)S(1)}, bf16[512,2048]{1,0:T(8,128)(2,1)}, u32[]{:S(2)}) copy-start(bf16[512,2048]{1,0:T(8,128)(2,1)} %param.13) | copy-start | bytes 6291460
  83.0 7.0 %copy-start.8 = (f32[8,64,128]{2,1,0:T(8,128)}, f32[8,64,128]{2,1,0:T(8,128)S(1)}, u32[]{:S(2)}) copy-start(f32[8,64,128]{2,1,0:T(8,128)S(1)} %get-tuple-element.17) | copy-start | bytes 786436
  83.0 7.0 %copy-start.3 = (f32[8,64,128]{2,1,0:T(8,128)}, f32[8,64,128]{2,1,0:T(8,128)S(1)}, u32[]{:S(2)}) copy-start(f32[8,64,128]{2,1,0:T(8,128)S(1)} %get-tuple-element.16) | copy-start | bytes 786436
  83.0 7.7 %copy-start.5 = (f32[8,64,128]{2,1,0:T(8,128)}, f32[8,64,128]{2,1,0:T(8,128)S(1)}, u32[]{:S(2)}) copy-start(f32[8,64,128]{2,1,0:T(8,128)S(1)} %get-tuple-element.15) | copy-start | bytes 786436
  83.0 7.0 %copy-start.14 = (bf16[512,128]{1,0:T(8,128)(2,1)S(1)}, bf16[512,128]{1,0:T(8,128)(2,1)}, u32[]{:S(2)}) copy-start(bf16[512,128]{1,0:T(8,128)(2,1)} %param.18) | copy-start | bytes 393220
  83.0 7.0 %copy-start.16 = (bf16[512,128]{1,0:T(8,128)(2,1)S(1)}, bf16[512,128]{1,0:T(8,128)(2,1)}, u32[]{:S(2)}) copy-start(bf16[512,128]{1,0:T(8,128)(2,1)} %param.17) | copy-start | bytes 393220
  93.1 8.2 %collective-permute-start.1 = (f32[16,88,128]{2,1,0:T(8,128)S(1)}, f32[16,88,128]{2,1,0:T(8,128)S(1)}, u32[]{:S(2)}, u32[]{:S(2)}) collective-permute-start(f32[16,88,128]{2,1,0:T(8,128)S(1)} %select_bitcast_fusion.2), channel_id=1, source_target_pairs={{0,8},{8,0},{16,24},{24,16},{32,40},{40,32},{48,56},{56,48},{64,72... | collective-permute-start | bytes 2162696 | tf_op jit(solution)/shard_map/ppermute | solution.py:15
  132.3 4.8 %collective-permute-start.2 = (f32[16,88,128]{2,1,0:T(8,128)S(1)}, f32[16,88,128]{2,1,0:T(8,128)S(1)}, u32[]{:S(2)}, u32[]{:S(2)}) collective-permute-start(f32[16,88,128]{2,1,0:T(8,128)S(1)} %all_to_all.27), channel_id=1, source_target_pairs={{0,8},{8,0},{16,24},{24,16},{32,40},{40,32},{48,56},{56,48},{64,72... | collective-permute-start | bytes 2162696 | tf_op jit(solution)/shard_map/ppermute | solution.py:15
  137.3 79.0 %copy-start.2 = (f32[16,2,88,128]{3,2,1,0:T(8,128)}, f32[16,2,88,128]{3,2,1,0:T(8,128)S(1)}, u32[]{:S(2)}) copy-start(f32[16,2,88,128]{3,2,1,0:T(8,128)S(1)} %pad_maximum_fusion) | copy-start | bytes 4325380
  211.9 7.6 %copy-start.4 = (f32[8,64,128]{2,1,0:T(8,128)S(1)}, f32[8,64,128]{2,1,0:T(8,128)}, u32[]{:S(2)}) copy-start(f32[8,64,128]{2,1,0:T(8,128)} %copy-done.3) | copy-start | bytes 786436
  211.9 8.7 %copy-start.9 = (f32[8,64,128]{2,1,0:T(8,128)S(1)}, f32[8,64,128]{2,1,0:T(8,128)}, u32[]{:S(2)}) copy-start(f32[8,64,128]{2,1,0:T(8,128)} %copy-done.8) | copy-start | bytes 786436
  217.2 8.7 %copy-start.6 = (f32[512,128]{1,0:T(8,128)S(1)}, f32[512,128]{1,0:T(8,128)}, u32[]{:S(2)}) copy-start(f32[512,128]{1,0:T(8,128)} %fusion.25) | copy-start | bytes 786436
  217.2 8.7 %copy-start.19 = (f32[128,128]{1,0:T(8,128)S(1)}, f32[128,128]{1,0:T(8,128)}, u32[]{:S(2)}) copy-start(f32[128,128]{1,0:T(8,128)} %get-tuple-element.22) | copy-start | bytes 196612
  222.3 13.0 %all-to-all-start.4 = ((f32[8,3,128]{2,1,0:T(4,128)}), f32[8,3,128]{2,1,0:T(4,128)S(1)}, u32[]{:S(2)}, u32[]{:S(2)}) async-start(f32[8,3,128]{2,1,0:T(4,128)} %broadcast_in_dim.32), calls=%async_computation.4 | async-start | bytes 32768 | tf_op jit(solution)/shard_map/all_to_all | solution.py:23
  227.9 6.3 %copy-start.7 = (f32[512,128]{1,0:T(8,128)S(1)}, f32[512,128]{1,0:T(8,128)}, u32[]{:S(2)}) copy-start(f32[512,128]{1,0:T(8,128)} %fusion.24) | copy-start | bytes 786436
  227.9 6.3 %copy-start.15 = (bf16[512,128]{1,0:T(8,128)(2,1)S(1)}, bf16[512,128]{1,0:T(8,128)(2,1)}, u32[]{:S(2)}) copy-start(bf16[512,128]{1,0:T(8,128)(2,1)} %param.18) | copy-start | bytes 393220
  227.9 6.3 %copy-start.17 = (bf16[512,128]{1,0:T(8,128)(2,1)S(1)}, bf16[512,128]{1,0:T(8,128)(2,1)}, u32[]{:S(2)}) copy-start(bf16[512,128]{1,0:T(8,128)(2,1)} %param.17) | copy-start | bytes 393220
  227.9 6.3 %copy-start.20 = (f32[128,128]{1,0:T(8,128)S(1)}, f32[128,128]{1,0:T(8,128)}, u32[]{:S(2)}) copy-start(f32[128,128]{1,0:T(8,128)} %get-tuple-element.24) | copy-start | bytes 196612
  234.2 6.5 %copy-start.10 = (f32[512,128]{1,0:T(8,128)S(1)}, f32[512,128]{1,0:T(8,128)}, u32[]{:S(2)}) copy-start(f32[512,128]{1,0:T(8,128)} %fusion.23) | copy-start | bytes 786436
  235.3 5.4 %copy-start.11 = (bf16[512,2048]{1,0:T(8,128)(2,1)S(1)}, bf16[512,2048]{1,0:T(8,128)(2,1)}, u32[]{:S(2)}) copy-start(bf16[512,2048]{1,0:T(8,128)(2,1)} %param.12) | copy-start | bytes 6291460

commit v2 on v1

v2 whole, which is shorter than its diff:
```python
import functools
import math

import jax
import jax.numpy as jnp
from jax import lax
from jax.experimental import pallas as pl
from jax.experimental.pallas import tpu as pltpu
from jax.sharding import PartitionSpec as P

RANK = 128
HIGHEST = lax.Precision.HIGHEST
F32 = jnp.float32
BF16 = jnp.bfloat16
PLANE = [[2 * i + c for i in range(16)] for c in range(2)]
SIBLING = [(i, i ^ 1) for i in range(32)]
STEPS = 4
BLOCKS = 22
HALF = BLOCKS // 2


def swap_core(x):
    return lax.ppermute(x, "fsdp", SIBLING)


def plane_exchange(x):
    return lax.all_to_all(x, "fsdp", 0, 0, tiled=True, axis_index_groups=PLANE)


def plane_gather(x):
    return plane_exchange(jnp.broadcast_to(x[None], (16,) + x.shape))


def tensor_exchange(x):
    return lax.all_to_all(x, "tensor", 0, 0, tiled=True)


def tensor_shift(x, distance):
    return lax.ppermute(x, "tensor", [(i, (i + distance) % 8) for i in range(8)])


def dot(a, b, contract=(1, 0)):
    dims = (((contract[0],), (contract[1],)), ((), ()))
    return lax.dot_general(a, b, dims, preferred_element_type=F32)


def split(x):
    high = x.astype(BF16)
    return high, (x - high.astype(F32)).astype(BF16)


def blend_of(moment_ref, grad_ref):
    return moment_ref[...].astype(F32) + grad_ref[...].astype(F32)


def full_spec(shape):
    return pl.BlockSpec(shape, lambda i: (0,) * len(shape))


def column_spec(rows):
    return pl.BlockSpec((rows, 2048 // STEPS), lambda i: (0, i))


SMEM = pl.BlockSpec(memory_space=pltpu.SMEM)


def rows_kernel(
    place, mq, gq, mine, other, mk, gk, mv, gv, out, rows, small
):
    step = pl.program_id(0)
    chips = 16 // STEPS
    first = place[2] == 0
    a, b = mine[...], other[...]
    low, high = jnp.where(first, a, b), jnp.where(first, b, a)

    def times(blend, basis):
        bh, bl = split(blend)
        qh, ql = split(basis)
        both = dot(bh, jnp.concatenate([qh, ql], axis=1))
        return both[:, :RANK] + both[:, RANK:] + dot(bl, qh)

    pieces = []
    for i in range(chips):
        pieces += [low[i, :64], high[i, :64]]
        at = pl.multiple_of((step * chips + i) * 8, 8)
        small[0, pl.ds(at, 8)] = jnp.concatenate([low[i, 64:68], high[i, 64:68]], axis=0)
        small[1, pl.ds(at, 8)] = jnp.concatenate([low[i, 68:72], high[i, 68:72]], axis=0)
    part = times(blend_of(mq, gq), jnp.concatenate(pieces, axis=0))

    @pl.when(step == 0)
    def _():
        rows[0] = part

    @pl.when(step > 0)
    def _():
        rows[0] += part

    @pl.when(step == STEPS - 1)
    def _():
        rows[1] = times(blend_of(mk, gk), small[0])
        rows[2] = times(blend_of(mv, gv), small[1])
        for d in range(8):
            for m in range(3):
                out[d, 64 * m : 64 * m + 64] = rows[m, 64 * d : 64 * d + 64]


def partial_rows(place, moments, grads, mine, other):
    tall = full_spec((512, RANK))
    gathered = pl.BlockSpec((16 // STEPS, 72, RANK), lambda i: (i, 0, 0))
    return pl.pallas_call(
        rows_kernel,
        grid=(STEPS,),
        in_specs=[SMEM, column_spec(512), column_spec(512), gathered, gathered] + [tall] * 4,
        out_specs=full_spec((8, 192, RANK)),
        out_shape=jax.ShapeDtypeStruct((8, 192, RANK), F32),
        scratch_shapes=[pltpu.VMEM((3, 512, RANK), F32), pltpu.VMEM((2, RANK, RANK), F32)],
        cost_estimate=pl.CostEstimate(
            flops=6 * 512 * 2304 * RANK, bytes_accessed=7_000_000, transcendentals=0
        ),
        name="partial_rows",
    )(place, moments[0], grads[0], mine, other, moments[1], grads[1], moments[2], grads[2])


def right_kernel(
    place, mq, gq, mk, gk, mv, gv, r0, r1, r2, r3, r4, r5, r6, r7, keep, send, projected, lhs
):
    step = pl.program_id(0)
    core = place[2]

    def put(half, at, value):
        @pl.when(half == core)
        def _():
            keep[at] = value

        @pl.when(half != core)
        def _():
            send[at] = value

    def times(m, blend):
        bh, bl = split(blend)
        both = dot(lhs[m], bh)
        return both[:RANK] + both[RANK:] + dot(lhs[m, :RANK], bl)

    @pl.when(step == 0)
    def _():
        for d, rows in enumerate((r0, r1, r2, r3, r4, r5, r6, r7)):
            at = pl.multiple_of(lax.rem(place[0] + (8 - d), 8) * 64, 64)
            for m in range(3):
                projected[m, pl.ds(at, 64)] = rows[64 * m : 64 * m + 64]
        for m in range(3):
            p = projected[m]
            turned = p.T
            high, low = split(turned)
            lhs[m, :RANK] = high
            lhs[m, RANK:] = low
            gram = jnp.dot(turned, p, precision=HIGHEST, preferred_element_type=F32)
            put(1, 18 + m - HALF, gram)
        put(1, 16 - HALF, times(1, blend_of(mk, gk)))
        put(1, 17 - HALF, times(2, blend_of(mv, gv)))
        put(1, 21 - HALF, jnp.zeros((RANK, RANK), F32))

    right = times(0, blend_of(mq, gq))
    for i in range(16 // STEPS):
        at = step * (16 // STEPS) + i
        put(at // HALF, lax.rem(at, HALF), right[:, RANK * i : RANK * i + RANK])


def right_parts(place, moments, grads, rows):
    tall = full_spec((512, RANK))
    half = (HALF, RANK, RANK)
    return pl.pallas_call(
        right_kernel,
        grid=(STEPS,),
        in_specs=[SMEM, column_spec(512), column_spec(512)] + [tall] * 4 + [full_spec((192, RANK))] * 8,
        out_specs=[full_spec(half), full_spec(half), full_spec((3, 512, RANK))],
        out_shape=[
            jax.ShapeDtypeStruct(half, F32),
            jax.ShapeDtypeStruct(half, F32),
            jax.ShapeDtypeStruct((3, 512, RANK), F32),
        ],
        scratch_shapes=[pltpu.VMEM((3, 2 * RANK, 512), BF16)],
        cost_estimate=pl.CostEstimate(
            flops=6 * 512 * 2304 * RANK, bytes_accessed=8_000_000, transcendentals=0
        ),
        name="right_parts",
    )(place, moments[0], grads[0], moments[1], grads[1], moments[2], grads[2], *rows)


def eliminate(work):
    sub = lax.broadcasted_iota(jnp.int32, (8, RANK), 0)
    for p in range(16):
        lo = 8 * p
        for m in range(3):
            panel = work[m, lo : lo + 8, :]
            if p > 0:
                coef = work[m, :lo, :RANK][:, lo : lo + 8]
                panel = panel - lax.dot_general(
                    coef,
                    work[m, :lo, :],
                    (((0,), (0,)), ((), ())),
                    precision=HIGHEST,
                    preferred_element_type=F32,
                )
            cols = [jnp.broadcast_to(panel[:, lo + k : lo + k + 1], (8, RANK)) for k in range(8)]
            left, right = panel[:, :RANK], panel[:, RANK:]
            for j in range(8):
                inv = lax.rsqrt(jnp.broadcast_to(cols[j][j : j + 1, :], (8, RANK)))
                row_left = jnp.broadcast_to(left[j : j + 1, :], (8, RANK)) * inv
                row_right = jnp.broadcast_to(right[j : j + 1, :], (8, RANK)) * inv
                below = jnp.where(sub > j, cols[j] * inv, 0.0)
                for k in range(j + 1, 8):
                    cols[k] = cols[k] - below * (jnp.broadcast_to(cols[k][j : j + 1, :], (8, RANK)) * inv)
                left = jnp.where(sub == j, row_left, left - below * row_left)
                right = jnp.where(sub == j, row_right, right - below * row_right)
            work[m, lo : lo + 8, :RANK] = left
            work[m, lo : lo + 8, RANK:] = right


def factor_kernel(
    place, mine, other, projected, ortho, right_high, right_low, squares, sq, sk, sv, work, turned
):
    core = place[2]
    fsdp = place[1]

    def block(j):
        return jnp.where(core == j // HALF, mine[j % HALF], other[j % HALF])

    row = lax.broadcasted_iota(jnp.int32, (RANK, RANK), 0)
    col = lax.broadcasted_iota(jnp.int32, (RANK, RANK), 1)
    for m in range(3):
        work[m, :, :RANK] = block(18 + m)
        work[m, :, RANK:] = jnp.where(row == col, 1.0, 0.0).astype(F32)
    eliminate(work)
    for m, blocks in enumerate((range(16), (16,), (17,))):
        inverse = work[m, :, RANK:]
        ih, il = split(inverse)
        ph, plow = split(projected[m])
        ortho[m] = dot(ph, ih, (1, 1)) + dot(ph, il, (1, 1)) + dot(plow, ih, (1, 1))
        stacked = jnp.concatenate([ih, il], axis=0)
        total = jnp.zeros((RANK, RANK), F32)
        for j in blocks:
            zh, zl = split(block(j))
            both = dot(stacked, zh)
            right = both[:RANK] + both[RANK:] + dot(ih, zl)
            total += right * right
            high, low = split(right)
            right_high[:, RANK * j : RANK * j + RANK] = high
            right_low[:, RANK * j : RANK * j + RANK] = low
            if m == 0:
                @pl.when(lax.div(fsdp, 2) == j)
                def _():
                    turned[0] = right.T
            else:
                turned[m] = right.T
        sums = jnp.sum(total.T, axis=0, keepdims=True)
        for d in range(8):
            squares[d, m : m + 1, :] = sums
    for d in range(8):
        squares[d, 3:, :] = jnp.zeros((5, RANK), F32)
    odd = lax.rem(fsdp, 2)
    sq[...] = turned[0, pl.ds(pl.multiple_of(odd * 64, 64), 64)]
    for m, out in ((1, sk), (2, sv)):
        tile = turned[m, pl.ds(pl.multiple_of(lax.div(fsdp, 2) * 8, 8), 8)]
        out[...] = jnp.where(odd == 0, tile[:4], tile[4:])


def factor_and_rotate(place, mine, other, projected):
    vmem = pl.BlockSpec(memory_space=pltpu.VMEM)
    return pl.pallas_call(
        factor_kernel,
        in_specs=[SMEM, vmem, vmem, vmem],
        out_specs=[vmem] * 7,
        out_shape=[
            jax.ShapeDtypeStruct((3, 512, RANK), F32),
            jax.ShapeDtypeStruct((RANK, 2304), BF16),
            jax.ShapeDtypeStruct((RANK, 2304), BF16),
            jax.ShapeDtypeStruct((8, 8, RANK), F32),
            jax.ShapeDtypeStruct((64, RANK), F32),
            jax.ShapeDtypeStruct((4, RANK), F32),
            jax.ShapeDtypeStruct((4, RANK), F32),
        ],
        scratch_shapes=[pltpu.VMEM((3, RANK, 2 * RANK), F32), pltpu.VMEM((3, RANK, RANK), F32)],
        name="factor_and_rotate",
    )(place, mine, other, projected)


def store_split(lhs, m, value):
    high, low = split(value)
    lhs[m, :, :RANK] = high
    lhs[m, :, RANK:] = low


def minus_product(base, lhs, m, high, low):
    product = dot(lhs[m], jnp.concatenate([high, high], axis=0)) + dot(lhs[m, :, :RANK], low)
    return (base - product).astype(BF16)


def momentum_kernel(
    mq, gq, mk, gk, mv, gv, ortho, hq, lq, hs, ls, out_q, out_k, out_v, lhs
):
    @pl.when(pl.program_id(0) == 0)
    def _():
        for m in range(3):
            store_split(lhs, m, 0.5 * ortho[m])
        out_k[...] = minus_product(blend_of(mk, gk), lhs, 1, hs[:, :RANK], ls[:, :RANK])
        out_v[...] = minus_product(blend_of(mv, gv), lhs, 2, hs[:, RANK:], ls[:, RANK:])

    out_q[...] = minus_product(blend_of(mq, gq), lhs, 0, hq[...], lq[...])


def weight_kernel(
    factors, wq, wk, wv, ortho, hq, lq, hs, ls, squares, sq, sk, sv,
    out_q, out_k, out_v, bq, bk, bv, lhs,
):
    @pl.when(pl.program_id(0) == 0)
    def _():
        inverse = lax.rsqrt(jnp.sum(squares[...], axis=0) + 1e-06)
        for m in range(3):
            store_split(lhs, m, ortho[m] * (factors[m] * inverse[m : m + 1]))
        for m, share, out in ((0, sq, bq), (1, sk, bk), (2, sv, bv)):
            out[...] = share[...] * inverse[m : m + 1]
        out_k[...] = minus_product(wk[...].astype(F32), lhs, 1, hs[:, :RANK], ls[:, :RANK])
        out_v[...] = minus_product(wv[...].astype(F32), lhs, 2, hs[:, RANK:], ls[:, RANK:])

    out_q[...] = minus_product(wq[...].astype(F32), lhs, 0, hq[...], lq[...])


TALL = full_spec((512, RANK))
ORTHO = full_spec((3, 512, RANK))
SMALL_RIGHT = pl.BlockSpec((RANK, 2 * RANK), lambda i: (0, 8))
WIDE_OUT = [
    jax.ShapeDtypeStruct((512, 2048), BF16),
    jax.ShapeDtypeStruct((512, RANK), BF16),
    jax.ShapeDtypeStruct((512, RANK), BF16),
]
COST = pl.CostEstimate(flops=6 * 512 * 2304 * RANK, bytes_accessed=9_000_000, transcendentals=0)


def new_momenta(moments, grads, ortho, high, low):
    wide = column_spec(512)
    return pl.pallas_call(
        momentum_kernel,
        grid=(STEPS,),
        in_specs=[wide, wide] + [TALL] * 4 + [ORTHO, column_spec(RANK), column_spec(RANK), SMALL_RIGHT, SMALL_RIGHT],
        out_specs=[wide, TALL, TALL],
        out_shape=WIDE_OUT,
        scratch_shapes=[pltpu.VMEM((3, 512, 2 * RANK), BF16)],
        cost_estimate=COST,
        name="new_momenta",
    )(moments[0], grads[0], moments[1], grads[1], moments[2], grads[2], ortho, high, low, high, low)


def new_weights(factors, weights, ortho, high, low, squares, shares):
    wide = column_spec(512)
    share_specs = [full_spec((64, RANK)), full_spec((4, RANK)), full_spec((4, RANK))]
    return pl.pallas_call(
        functools.partial(weight_kernel, factors),
        grid=(STEPS,),
        in_specs=[wide, TALL, TALL, ORTHO, column_spec(RANK), column_spec(RANK), SMALL_RIGHT, SMALL_RIGHT]
        + [full_spec((8, 8, RANK))]
        + share_specs,
        out_specs=[wide, TALL, TALL] + share_specs,
        out_shape=WIDE_OUT + [jax.ShapeDtypeStruct(s.block_shape, F32) for s in share_specs],
        scratch_shapes=[pltpu.VMEM((3, 512, 2 * RANK), BF16)],
        cost_estimate=COST,
        name="new_weights",
    )(*weights, ortho, high, low, high, low, squares, *shares)


def body(
    weight_q,
    momentum_q,
    grad_q,
    basis_q,
    weight_k,
    momentum_k,
    grad_k,
    basis_k,
    weight_v,
    momentum_v,
    grad_v,
    basis_v,
):
    weights = (weight_q, weight_k, weight_v)
    moments = (momentum_q, momentum_k, momentum_v)
    grads = (grad_q, grad_k, grad_v)
    fsdp = lax.axis_index("fsdp")
    place = jnp.stack([lax.axis_index("tensor"), fsdp, lax.rem(fsdp, 2)]).astype(jnp.int32)
    factors = [
        0.25 * math.sqrt(w.shape[0] * lax.axis_size("fsdp") * w.shape[1] * lax.axis_size("tensor") / RANK)
        for w in weights
    ]

    mine = plane_gather(jnp.concatenate([basis_q, basis_k, basis_v], axis=0))
    chunks = partial_rows(place, moments, grads, mine, swap_core(mine))
    own = jnp.sum(tensor_exchange(chunks), axis=0)
    rows = [own] + [tensor_shift(own, d) for d in range(1, 8)]
    keep, send, projected = right_parts(place, moments, grads, rows)

    paired = (keep + swap_core(send)).reshape(16, 88, RANK)
    mine = plane_gather(jnp.sum(plane_exchange(paired), axis=0)).reshape(HALF, RANK, RANK)
    ortho, high, low, squares, *shares = factor_and_rotate(place, mine, swap_core(mine), projected)
    squares = tensor_exchange(squares)
    momenta = new_momenta(moments, grads, ortho, high, low)
    new_w = new_weights(factors, weights, ortho, high, low, squares, shares)
    return tuple(x for i in range(3) for x in (new_w[i], momenta[i], new_w[3 + i]))


def solution(mesh):
    placed = (
        P("fsdp", "tensor"),
        P("fsdp", "tensor"),
        P("fsdp", "tensor"),
        P(("tensor", "fsdp"), None),
    ) * 3
    return jax.shard_map(
        body,
        mesh=mesh,
        in_specs=placed,
        out_specs=(
            P("fsdp", "tensor"),
            P("fsdp", "tensor"),
            P(("tensor", "fsdp"), None),
        )
        * 3,
        check_vma=False,
    )
```

time: 247 us -> 168 us (0.68)
  other arithmetic: 79.2 us -> 2.62 us
  matrix products: 42 us -> 0 us
  Pallas kernels: 0 us -> 39.3 us
  waiting for transfers between devices: 11.6 us -> 22.2 us
  local copies, waits for them, and re-layouts: 6.81 us -> 3.07 us
  blocking collectives: 82.9 us -> 79.3 us
  starting transfers between devices: 22.4 us -> 19.7 us
    another operation x12 -> x1, other arithmetic: 71.3 us -> 0.55 us  [body(): jnp.stack([lax.axis_index('tensor'), fsdp, lax.rem(fsdp, 2)])]
    dot_general x21 -> x0, matrix products: 40.5 us -> none  [the longest x3 9.3 us: body(): jnp.dot(o, r.T, precision=HIGH)]
    pallas_call x0 -> x5, Pallas kernels: none -> 39.3 us  [the longest x1 14.2 us: factor_and_rotate(): pl.pallas_call(factor_kernel, in_specs=[SMEM, vmem, vmem, vmem], out_spec...]
    all_gather x1 -> x0, blocking collectives: 20.6 us -> none  [body(): rows = lax.all_gather(own_rows, 'tensor', axis=0)]
    all_to_all x2 -> x3, blocking collectives: 30.7 us -> 48.8 us  [plane_exchange(): return lax.all_to_all(x, 'fsdp', 0, 0, tiled=True, axis_index_groups=PLANE)]
    ppermute x0 -> x7, waiting for transfers between devices: none -> 16.4 us  [tensor_shift(): lax.ppermute(x, 'tensor', [(i, (i + distance) % 8) for i in range(8)])]
    ppermute x0 -> x7, starting transfers between devices: none -> 9.53 us  [tensor_shift(): lax.ppermute(x, 'tensor', [(i, (i + distance) % 8) for i in range(8)])]
    all_to_all x1 -> x0, waiting for transfers between devices: 9.25 us -> none  [plane_exchange(): return lax.all_to_all(x, 'fsdp', 0, 0, tiled=True, axis_index_groups=PLANE)]
  transfers between devices with their start and end apart: 5 -> 11, of which waited for: 3 -> 7; matrix products, arithmetic and copies ran while one was open for 6% -> 0% of each run, Pallas kernels for 0% -> 4%
where the time goes in v2:
time: 168 us; the launch traced here: 167 us
  blocking collectives  79.3 us (47%)
  Pallas kernels  39.3 us (23%)
  waiting for transfers between devices  22.2 us (13%)
  starting transfers between devices  19.7 us (12%)
  local copies, waits for them, and re-layouts  3.07 us (2%)
  other arithmetic  2.62 us (2%)
    all_to_all x3, blocking collectives, plane_exchange(): return lax.all_to_all(x, 'fsdp', 0, 0, tiled=True, axis_index_groups=PLANE)  48.8 us
    all_to_all x1, blocking collectives, tensor_exchange(): return lax.all_to_all(x, 'tensor', 0, 0, tiled=True)  30.5 us
    ppermute x7, waiting for transfers between devices, tensor_shift(): lax.ppermute(x, 'tensor', [(i, (i + distance) % 8) for i in range(8)])  16.4 us
    pallas_call x1, Pallas kernels, factor_and_rotate(): pl.pallas_call(factor_kernel, in_specs=[SMEM, vmem, vmem, vmem], out_spec...  14.2 us
    ppermute x7, starting transfers between devices, tensor_shift(): lax.ppermute(x, 'tensor', [(i, (i + distance) % 8) for i in range(8)])  9.53 us
    pallas_call x1, Pallas kernels, right_parts(): pl.pallas_call(right_kernel, grid=(STEPS,), in_specs=[SMEM, column_spec(5...  7.71 us
    pallas_call x1, Pallas kernels, new_momenta(): pl.pallas_call(momentum_kernel, grid=(STEPS,), in_specs=[wide, wide] + [T...  6.03 us
    ppermute x3, starting transfers between devices, swap_core(): return lax.ppermute(x, 'fsdp', SIBLING)  5.84 us
  transfers between devices with their start and end apart: 11, of which 7 were waited for; matrix products, arithmetic and copies ran while one was open for 0% of the time, Pallas kernels for 4%

profile of v2, /device:TPU:1, one launch (start us, length us, event | category | flops | bytes accessed | tf_op | source)
XLA Modules:
  0.0 167.0 jit_solution(16664883348361241621)
XLA Ops:
  0.6 0.8 pad_maximum_fusion
  1.5 18.4 %all_to_all.25.mine = f32[16,72,128]{2,1,0:T(8,128)S(1)} all-to-all(f32[16,72,128]{2,1,0:T(8,128)S(1)} %broadcast_in_dim.4), channel_id=1, replica_groups={{0,16,32,48,64,80,96,112,128,144,160,176,192,208,224,240},{8,24,40,56,7..., dimensions={0} | all-to-all | bytes 1179648 | tf_op jit(solution)/shard_map/all_to_all | solution.py:27
  19.8 2.2 %collective-permute-start = (f32[16,72,128]{2,1,0:T(8,128)S(1)}, f32[16,72,128]{2,1,0:T(8,128)S(1)}, u32[]{:S(2)}, u32[]{:S(2)}) collective-permute-start(f32[16,72,128]{2,1,0:T(8,128)S(1)} %all_to_all.25.mine), channel_id=1, source_target_pairs={{0,8},{8,0},{16,24},{24,16},{32,40},{40,32},{48,56},{56,48},{64,72... | collective-permute-start | bytes 1769480 | tf_op jit(solution)/shard_map/ppermute | solution.py:23
  22.0 0.6 pad_add_fusion.place
  22.6 1.1 collective-permute-done.other
  23.7 0.8 copy-done.3
  24.5 5.8 %partial_rows.1 = f32[8,192,128]{2,1,0:T(8,128)} custom-call(s32[3]{0:T(128)} %pad_add_fusion.place, bf16[512,2048]{1,0:T(8,128)(2,1)} %mq.5, bf16[512,2048]{1,0:T(8,128)(2,1)} %gq.5, f32[16,72,128]{2,1,0:T(8,128)} %copy-done.1, f32[16,72,128]{2,1,0:T(8,128)} %copy-done.3, bf16[512,128]{1,0:T(8,128)(2,1)} %mk.5, bf16[512,128]{1,0:T(8,128)(2,1)} %gk.5, ...), custom_call_target="tpu_custom_call" | custom-call | flops 905969664 | bytes 7000000 | tf_op jit(solution)/shard_map/partial_rows/pallas_call | solution.py:110
  30.3 30.5 %all_to_all.26 = f32[8,192,128]{2,1,0:T(8,128)S(1)} all-to-all(f32[8,192,128]{2,1,0:T(8,128)} %partial_rows.1), channel_id=1, replica_groups=mesh['fsdp'=32,'tensor'=8] {'tensor'}, dimensions={0} | all-to-all | bytes 1572864 | tf_op jit(solution)/shard_map/all_to_all | solution.py:35
  60.9 0.8 collective-permute-start.6
  61.7 1.9 %collective-permute-start.5 = (f32[192,128]{1,0:T(8,128)S(1)}, f32[192,128]{1,0:T(8,128)S(1)}, u32[]{:S(2)}, u32[]{:S(2)}) collective-permute-start(f32[192,128]{1,0:T(8,128)S(1)} %reduce_sum.18.r0), channel_id=1, source_target_pairs={{0,5},{1,6},{2,7},{3,0},{4,1},{5,2},{6,3},{7,4},{8,13},{9,14},{10,... | collective-permute-start | bytes 294920 | tf_op jit(solution)/shard_map/ppermute | solution.py:39
  63.6 3.6 %collective-permute-start.4 = (f32[192,128]{1,0:T(8,128)S(1)}, f32[192,128]{1,0:T(8,128)S(1)}, u32[]{:S(2)}, u32[]{:S(2)}) collective-permute-start(f32[192,128]{1,0:T(8,128)S(1)} %reduce_sum.18.r0), channel_id=1, source_target_pairs={{0,4},{1,5},{2,6},{3,7},{4,0},{5,1},{6,2},{7,3},{8,12},{9,13},{10,... | collective-permute-start | bytes 294920 | tf_op jit(solution)/shard_map/ppermute | solution.py:39
  67.3 0.5 collective-permute-start.3
  67.8 2.6 %collective-permute-start.2 = (f32[192,128]{1,0:T(8,128)S(1)}, f32[192,128]{1,0:T(8,128)S(1)}, u32[]{:S(2)}, u32[]{:S(2)}) collective-permute-start(f32[192,128]{1,0:T(8,128)S(1)} %reduce_sum.18.r0), channel_id=1, source_target_pairs={{0,2},{1,3},{2,4},{3,5},{4,6},{5,7},{6,0},{7,1},{8,10},{9,11},{10,... | collective-permute-start | bytes 294920 | tf_op jit(solution)/shard_map/ppermute | solution.py:39
  70.4 2.1 %collective-permute-done.5.r5 = f32[192,128]{1,0:T(8,128)S(1)} collective-permute-done((f32[192,128]{1,0:T(8,128)S(1)}, f32[192,128]{1,0:T(8,128)S(1)}, u32[]{:S(2)}, u32[]{:S(2)}) %collective-permute-start.5) | collective-permute-done | bytes 98336 | tf_op jit(solution)/shard_map/ppermute | solution.py:39
  72.5 8.8 %collective-permute-done.3.r3 = f32[192,128]{1,0:T(8,128)S(1)} collective-permute-done((f32[192,128]{1,0:T(8,128)S(1)}, f32[192,128]{1,0:T(8,128)S(1)}, u32[]{:S(2)}, u32[]{:S(2)}) %collective-permute-start.3) | collective-permute-done | bytes 98336 | tf_op jit(solution)/shard_map/ppermute | solution.py:39
  81.3 5.5 %collective-permute-done.1.r1 = f32[192,128]{1,0:T(8,128)S(1)} collective-permute-done((f32[192,128]{1,0:T(8,128)S(1)}, f32[192,128]{1,0:T(8,128)S(1)}, u32[]{:S(2)}, u32[]{:S(2)}) %collective-permute-start.1) | collective-permute-done | bytes 98336 | tf_op jit(solution)/shard_map/ppermute | solution.py:39
  86.9 0.6 copy-done.12
  87.5 7.7 %right_parts.1 = (f32[11,128,128]{2,1,0:T(8,128)}, f32[11,128,128]{2,1,0:T(8,128)}, f32[3,512,128]{2,1,0:T(8,128)}) custom-call(s32[3]{0:T(128)} %pad_add_fusion.place, bf16[512,2048]{1,0:T(8,128)(2,1)} %mq.5, bf16[512,2048]{1,0:T(8,128)(2,1)} %gq.5, bf16[512,128]{1,0:T(8,128)(2,1)} %mk.5, bf16[512,128]{1,0:T(8,128)(2,1)} %gk.5, bf16[512,128]{1,0:T(8,128)(2,1)} %mv.5, ...), custom_call_target="tpu_custom_call" | custom-call | flops 905969664 | bytes 8000000 | tf_op jit(solution)/shard_map/right_parts/pallas_call | solution.py:171
  95.2 0.7 collective-permute-start.8
  95.9 2.0 %collective-permute-done.8 = f32[11,128,128]{2,1,0:T(8,128)S(1)} collective-permute-done((f32[11,128,128]{2,1,0:T(8,128)}, f32[11,128,128]{2,1,0:T(8,128)S(1)}, u32[]{:S(2)}, u32[]{:S(2)}) %collective-permute-start.8) | collective-permute-done | bytes 720928 | tf_op jit(solution)/shard_map/ppermute | solution.py:23
  97.9 1.2 add.3
  99.1 15.5 %all_to_all.27 = f32[16,88,128]{2,1,0:T(8,128)S(1)} all-to-all(f32[16,88,128]{2,1,0:T(8,128)S(1)} %bitcast.7), channel_id=1, replica_groups={{0,16,32,48,64,80,96,112,128,144,160,176,192,208,224,240},{8,24,40,56,7..., dimensions={0} | all-to-all | bytes 1441792 | tf_op jit(solution)/shard_map/all_to_all | solution.py:27
  114.7 14.9 %all_to_all.28 = f32[16,88,128]{2,1,0:T(8,128)S(1)} all-to-all(f32[16,88,128]{2,1,0:T(8,128)S(1)} %broadcast_in_dim.5), channel_id=1, replica_groups={{0,16,32,48,64,80,96,112,128,144,160,176,192,208,224,240},{8,24,40,56,7..., dimensions={0} | all-to-all | bytes 1441792 | tf_op jit(solution)/shard_map/all_to_all | solution.py:27
  129.6 3.0 %collective-permute-start.9 = (f32[11,128,128]{2,1,0:T(8,128)S(1)}, f32[11,128,128]{2,1,0:T(8,128)S(1)}, u32[]{:S(2)}, u32[]{:S(2)}) collective-permute-start(f32[11,128,128]{2,1,0:T(8,128)S(1)} %bitcast.5), channel_id=1, source_target_pairs={{0,8},{8,0},{16,24},{24,16},{32,40},{40,32},{48,56},{56,48},{64,72... | collective-permute-start | bytes 2162696 | tf_op jit(solution)/shard_map/ppermute | solution.py:23
  132.6 1.8 %collective-permute-done.9.other = f32[11,128,128]{2,1,0:T(8,128)S(1)} collective-permute-done((f32[11,128,128]{2,1,0:T(8,128)S(1)}, f32[11,128,128]{2,1,0:T(8,128)S(1)}, u32[]{:S(2)}, u32[]{:S(2)}) %collective-permute-start.9) | collective-permute-done | bytes 720928 | tf_op jit(solution)/shard_map/ppermute | solution.py:23
  134.4 0.9 copy-done.2
  135.3 14.2 %factor_and_rotate.1 = (f32[3,512,128]{2,1,0:T(8,128)}, bf16[128,2304]{1,0:T(8,128)(2,1)}, bf16[128,2304]{1,0:T(8,128)(2,1)}, f32[8,8,128]{2,1,0:T(8,128)}, f32[...) custom-call(s32[3]{0:T(128)} %pad_add_fusion.place, f32[11,128,128]{2,1,0:T(8,128)} %bitcast.6, ...), custom_call_target="tpu_custom_call" | custom-call | tf_op jit(solution)/shard_map/factor_and_rotate/pallas_call | solution.py:269
  149.5 4.3 %all-to-all-start.4 = ((f32[8,8,128]{2,1,0:T(8,128)}), f32[8,8,128]{2,1,0:T(8,128)S(1)}, u32[]{:S(2)}, u32[]{:S(2)}) async-start(f32[8,8,128]{2,1,0:T(8,128)} %get-tuple-element.34), calls=%async_computation.4 | async-start | bytes 65536 | tf_op jit(solution)/shard_map/all_to_all | solution.py:35
  153.8 6.0 %new_momenta.1 = (bf16[512,2048]{1,0:T(8,128)(2,1)}, bf16[512,128]{1,0:T(8,128)(2,1)}, bf16[512,128]{1,0:T(8,128)(2,1)}) custom-call(bf16[512,2048]{1,0:T(8,128)(2,1)} %mq.5, bf16[512,2048]{1,0:T(8,128)(2,1)} %gq.5, bf16[512,128]{1,0:T(8,128)(2,1)} %mk.5, bf16[512,128]{1,0:T(8,128)(2,1)} %gk.5, bf16[512,128]{1,0:T(8,128)(2,1)} %mv.5, bf16[512,128]{1,0:T(8,128)(2,1)} %gv.5, ...), custom_call_target="tpu_custom_call" | custom-call | flops 905969664 | bytes 9000000 | tf_op jit(solution)/shard_map/new_momenta/pallas_call | solution.py:341
  159.9 0.9 all-to-all-done.4.squares
  160.8 0.6 copy-done.5
  161.4 5.6 %new_weights.1 = (bf16[512,2048]{1,0:T(8,128)(2,1)}, bf16[512,128]{1,0:T(8,128)(2,1)}, bf16[512,128]{1,0:T(8,128)(2,1)}, f32[64,128]{1,0:T(8,128)}, f32[4,128]{1,0:T(4,128)}, /*index=5*/f32[4,128]{1,0:T(4,128)}) custom-call(bf16[512,2048]{1,0:T(8,128)(2,1)} %wq.1, bf16[512,128]{1,0:T(8,128)(2,1)} %wk.1, bf16[512,128]{1,0:T(8,128)(2,1)} %wv.1, ...), custom_call_target="tpu_custom_call" | custom-call | flops 905969664 | bytes 9000000 | tf_op jit(solution)/shard_map/new_weights/pallas_call | solution.py:356
  (32 shorter events, 0.3 us)
Async XLA Ops:
  19.8 3.8 %copy-start.1 = (f32[16,72,128]{2,1,0:T(8,128)}, f32[16,72,128]{2,1,0:T(8,128)S(1)}, u32[]{:S(2)}) copy-start(f32[16,72,128]{2,1,0:T(8,128)S(1)} %all_to_all.25.mine) | copy-start | bytes 1769476
  19.8 3.8 %collective-permute-start = (f32[16,72,128]{2,1,0:T(8,128)S(1)}, f32[16,72,128]{2,1,0:T(8,128)S(1)}, u32[]{:S(2)}, u32[]{:S(2)}) collective-permute-start(f32[16,72,128]{2,1,0:T(8,128)S(1)} %all_to_all.25.mine), channel_id=1, source_target_pairs={{0,8},{8,0},{16,24},{24,16},{32,40},{40,32},{48,56},{56,48},{64,72... | collective-permute-start | bytes 1769480 | tf_op jit(solution)/shard_map/ppermute | solution.py:23
  23.7 0.8 copy-start.3
  60.8 26.0 %copy-start.4 = (f32[192,128]{1,0:T(8,128)}, f32[192,128]{1,0:T(8,128)S(1)}, u32[]{:S(2)}) copy-start(f32[192,128]{1,0:T(8,128)S(1)} %reduce_sum.18.r0) | copy-start | bytes 294916
  60.8 6.9 %collective-permute-start.7 = (f32[192,128]{1,0:T(8,128)S(1)}, f32[192,128]{1,0:T(8,128)S(1)}, u32[]{:S(2)}, u32[]{:S(2)}) collective-permute-start(f32[192,128]{1,0:T(8,128)S(1)} %reduce_sum.18.r0), channel_id=1, source_target_pairs={{0,7},{1,0},{2,1},{3,2},{4,3},{5,4},{6,5},{7,6},{8,15},{9,8},{10,9... | collective-permute-start | bytes 294920 | tf_op jit(solution)/shard_map/ppermute | solution.py:39
  60.9 9.5 %collective-permute-start.6 = (f32[192,128]{1,0:T(8,128)S(1)}, f32[192,128]{1,0:T(8,128)S(1)}, u32[]{:S(2)}, u32[]{:S(2)}) collective-permute-start(f32[192,128]{1,0:T(8,128)S(1)} %reduce_sum.18.r0), channel_id=1, source_target_pairs={{0,6},{1,7},{2,0},{3,1},{4,2},{5,3},{6,4},{7,5},{8,14},{9,15},{10,... | collective-permute-start | bytes 294920 | tf_op jit(solution)/shard_map/ppermute | solution.py:39
  61.7 10.8 %collective-permute-start.5 = (f32[192,128]{1,0:T(8,128)S(1)}, f32[192,128]{1,0:T(8,128)S(1)}, u32[]{:S(2)}, u32[]{:S(2)}) collective-permute-start(f32[192,128]{1,0:T(8,128)S(1)} %reduce_sum.18.r0), channel_id=1, source_target_pairs={{0,5},{1,6},{2,7},{3,0},{4,1},{5,2},{6,3},{7,4},{8,13},{9,14},{10,... | collective-permute-start | bytes 294920 | tf_op jit(solution)/shard_map/ppermute | solution.py:39
  63.6 8.9 %collective-permute-start.4 = (f32[192,128]{1,0:T(8,128)S(1)}, f32[192,128]{1,0:T(8,128)S(1)}, u32[]{:S(2)}, u32[]{:S(2)}) collective-permute-start(f32[192,128]{1,0:T(8,128)S(1)} %reduce_sum.18.r0), channel_id=1, source_target_pairs={{0,4},{1,5},{2,6},{3,7},{4,0},{5,1},{6,2},{7,3},{8,12},{9,13},{10,... | collective-permute-start | bytes 294920 | tf_op jit(solution)/shard_map/ppermute | solution.py:39
  67.3 14.1 %collective-permute-start.3 = (f32[192,128]{1,0:T(8,128)S(1)}, f32[192,128]{1,0:T(8,128)S(1)}, u32[]{:S(2)}, u32[]{:S(2)}) collective-permute-start(f32[192,128]{1,0:T(8,128)S(1)} %reduce_sum.18.r0), channel_id=1, source_target_pairs={{0,3},{1,4},{2,5},{3,6},{4,7},{5,0},{6,1},{7,2},{8,11},{9,12},{10,... | collective-permute-start | bytes 294920 | tf_op jit(solution)/shard_map/ppermute | solution.py:39
  67.8 19.0 %copy-start.6 = (f32[192,128]{1,0:T(8,128)}, f32[192,128]{1,0:T(8,128)S(1)}, u32[]{:S(2)}) copy-start(f32[192,128]{1,0:T(8,128)S(1)} %collective-permute-done.7.r7) | copy-start | bytes 294916
  67.8 13.6 %collective-permute-start.2 = (f32[192,128]{1,0:T(8,128)S(1)}, f32[192,128]{1,0:T(8,128)S(1)}, u32[]{:S(2)}, u32[]{:S(2)}) collective-permute-start(f32[192,128]{1,0:T(8,128)S(1)} %reduce_sum.18.r0), channel_id=1, source_target_pairs={{0,2},{1,3},{2,4},{3,5},{4,6},{5,7},{6,0},{7,1},{8,10},{9,11},{10,... | collective-permute-start | bytes 294920 | tf_op jit(solution)/shard_map/ppermute | solution.py:39
  70.4 16.4 %copy-start.7 = (f32[192,128]{1,0:T(8,128)}, f32[192,128]{1,0:T(8,128)S(1)}, u32[]{:S(2)}) copy-start(f32[192,128]{1,0:T(8,128)S(1)} %collective-permute-done.6.r6) | copy-start | bytes 294916
  70.4 16.4 %collective-permute-start.1 = (f32[192,128]{1,0:T(8,128)S(1)}, f32[192,128]{1,0:T(8,128)S(1)}, u32[]{:S(2)}, u32[]{:S(2)}) collective-permute-start(f32[192,128]{1,0:T(8,128)S(1)} %reduce_sum.18.r0), channel_id=1, source_target_pairs={{0,1},{1,2},{2,3},{3,4},{4,5},{5,6},{6,7},{7,0},{8,9},{9,10},{10,1... | collective-permute-start | bytes 294920 | tf_op jit(solution)/shard_map/ppermute | solution.py:39
  72.5 14.3 %copy-start.8 = (f32[192,128]{1,0:T(8,128)}, f32[192,128]{1,0:T(8,128)S(1)}, u32[]{:S(2)}) copy-start(f32[192,128]{1,0:T(8,128)S(1)} %collective-permute-done.5.r5) | copy-start | bytes 294916
  72.5 14.3 %copy-start.9 = (f32[192,128]{1,0:T(8,128)}, f32[192,128]{1,0:T(8,128)S(1)}, u32[]{:S(2)}) copy-start(f32[192,128]{1,0:T(8,128)S(1)} %collective-permute-done.4.r4) | copy-start | bytes 294916
  81.3 5.5 %copy-start.10 = (f32[192,128]{1,0:T(8,128)}, f32[192,128]{1,0:T(8,128)S(1)}, u32[]{:S(2)}) copy-start(f32[192,128]{1,0:T(8,128)S(1)} %collective-permute-done.3.r3) | copy-start | bytes 294916
  81.3 5.5 %copy-start.11 = (f32[192,128]{1,0:T(8,128)}, f32[192,128]{1,0:T(8,128)S(1)}, u32[]{:S(2)}) copy-start(f32[192,128]{1,0:T(8,128)S(1)} %collective-permute-done.2.r2) | copy-start | bytes 294916
  86.8 0.6 copy-start.12
  95.2 2.7 %collective-permute-start.8 = (f32[11,128,128]{2,1,0:T(8,128)}, f32[11,128,128]{2,1,0:T(8,128)S(1)}, u32[]{:S(2)}, u32[]{:S(2)}) collective-permute-start(f32[11,128,128]{2,1,0:T(8,128)} %get-tuple-element.29), channel_id=1, source_target_pairs={{0,8},{8,0},{16,24},{24,16},{32,40},{40,32},{48,56},{56,48},{64,72... | collective-permute-start | bytes 2162696 | tf_op jit(solution)/shard_map/ppermute | solution.py:23
  129.6 4.8 %copy-start = (f32[16,88,128]{2,1,0:T(8,128)}, f32[16,88,128]{2,1,0:T(8,128)S(1)}, u32[]{:S(2)}) copy-start(f32[16,88,128]{2,1,0:T(8,128)S(1)} %all_to_all.28) | copy-start | bytes 2162692
  129.6 4.8 %collective-permute-start.9 = (f32[11,128,128]{2,1,0:T(8,128)S(1)}, f32[11,128,128]{2,1,0:T(8,128)S(1)}, u32[]{:S(2)}, u32[]{:S(2)}) collective-permute-start(f32[11,128,128]{2,1,0:T(8,128)S(1)} %bitcast.5), channel_id=1, source_target_pairs={{0,8},{8,0},{16,24},{24,16},{32,40},{40,32},{48,56},{56,48},{64,72... | collective-permute-start | bytes 2162696 | tf_op jit(solution)/shard_map/ppermute | solution.py:23
  134.4 0.9 copy-start.2
  149.5 11.3 %all-to-all-start.4 = ((f32[8,8,128]{2,1,0:T(8,128)}), f32[8,8,128]{2,1,0:T(8,128)S(1)}, u32[]{:S(2)}, u32[]{:S(2)}) async-start(f32[8,8,128]{2,1,0:T(8,128)} %get-tuple-element.34), calls=%async_computation.4 | async-start | bytes 65536 | tf_op jit(solution)/shard_map/all_to_all | solution.py:35
  160.8 0.6 copy-start.5

commit v3 on v2

v3 whole, which is shorter than its diff:
```python
import functools
import math

import jax
import jax.numpy as jnp
from jax import lax
from jax.experimental import pallas as pl
from jax.experimental.pallas import tpu as pltpu
from jax.sharding import PartitionSpec as P

RANK = 128
HIGHEST = lax.Precision.HIGHEST
F32 = jnp.float32
BF16 = jnp.bfloat16
PLANE = [[2 * i + c for i in range(16)] for c in range(2)]
SIBLING = [(i, i ^ 1) for i in range(32)]
STEPS = 4
BLOCKS = 22
HALF = BLOCKS // 2
VMEM_LIMIT = 24 * 1024 * 1024


def swap_core(x):
    return lax.ppermute(x, "fsdp", SIBLING)


def plane_exchange(x):
    return lax.all_to_all(x, "fsdp", 0, 0, tiled=True, axis_index_groups=PLANE)


def plane_gather(x):
    return plane_exchange(jnp.broadcast_to(x[None], (16,) + x.shape))


def tensor_exchange(x):
    return lax.all_to_all(x, "tensor", 0, 0, tiled=True)


def tensor_shift(x, distance):
    return lax.ppermute(x, "tensor", [(i, (i + distance) % 8) for i in range(8)])


def dot(a, b, contract=(1, 0)):
    dims = (((contract[0],), (contract[1],)), ((), ()))
    return lax.dot_general(a, b, dims, preferred_element_type=F32)


def split(x):
    high = x.astype(BF16)
    return high, (x - high.astype(F32)).astype(BF16)


def blend_of(moment_ref, grad_ref):
    return moment_ref[...].astype(F32) + grad_ref[...].astype(F32)


def full_spec(shape):
    return pl.BlockSpec(shape, lambda i: (0,) * len(shape))


def column_spec(rows):
    return pl.BlockSpec((rows, 2048 // STEPS), lambda i: (0, i))


VMEM = pl.BlockSpec(memory_space=pltpu.VMEM)


def blend_kernel(mq, gq, mk, gk, mv, gv, high, low):
    for at, moment, grad in ((0, mq, gq), (2048, mk, gk), (2048 + RANK, mv, gv)):
        h, l = split(moment[...].astype(F32) + grad[...].astype(F32))
        span = slice(at, at + h.shape[1])
        high[:, span] = h
        low[:, span] = l


def blend_terms(moments, grads):
    def rows(width):
        return pl.BlockSpec((128, width), lambda i: (i, 0))

    return pl.pallas_call(
        blend_kernel,
        grid=(4,),
        in_specs=[rows(2048)] * 2 + [rows(RANK)] * 4,
        out_specs=[rows(2304)] * 2,
        out_shape=[jax.ShapeDtypeStruct((512, 2304), BF16)] * 2,
        compiler_params=pltpu.CompilerParams(vmem_limit_bytes=VMEM_LIMIT),
        cost_estimate=pl.CostEstimate(
            flops=4 * 512 * 2304, bytes_accessed=9_400_000, transcendentals=0
        ),
        name="blend_terms",
    )(*(x for group in zip(moments, grads) for x in group))


def small_kernel(kernel, shape, name, *operands):
    return pl.pallas_call(
        kernel,
        in_specs=[VMEM] * len(operands),
        out_specs=VMEM,
        out_shape=jax.ShapeDtypeStruct(shape, F32),
        compiler_params=pltpu.CompilerParams(vmem_limit_bytes=VMEM_LIMIT),
        name=name,
    )(*operands)


def total_kernel(parts, out):
    out[...] = jnp.sum(parts[...], axis=0)


def repeat_total_kernel(parts, out):
    total = jnp.sum(parts[...], axis=0)
    for i in range(16):
        out[i] = total


def pair_kernel(a, b, out):
    out[...] = a[...] + b[...]


def rows_kernel(high, low, mine, other, out, basis, small):
    first = lax.rem(lax.axis_index("fsdp"), 2) == 0
    for i in range(16):
        a, b = mine[i], other[i]
        pair = (jnp.where(first, a, b), jnp.where(first, b, a))
        for c in range(2):
            at = 128 * i + 64 * c
            qh, ql = split(pair[c][:64])
            basis[at : at + 64, :RANK] = qh
            basis[at : at + 64, RANK:] = ql
        for n in range(2):
            piece = [x[64 + 4 * n : 68 + 4 * n] for x in pair]
            small[n, 8 * i : 8 * i + 8] = jnp.concatenate(piece, axis=0)
    for n in range(2):
        qh, ql = split(small[n])
        basis[2048 + RANK * n : 2048 + RANK * n + RANK, :RANK] = qh
        basis[2048 + RANK * n : 2048 + RANK * n + RANK, RANK:] = ql
    for m, (lo, hi) in enumerate(((0, 2048), (2048, 2176), (2176, 2304))):
        for half in range(2):
            at = slice(256 * half, 256 * half + 256)
            both = dot(high[at, lo:hi], basis[lo:hi])
            rows = both[:, :RANK] + both[:, RANK:] + dot(low[at, lo:hi], basis[lo:hi, :RANK])
            for d in range(4):
                out[4 * half + d, 64 * m : 64 * m + 64] = rows[64 * d : 64 * d + 64]


def partial_rows(high, low, mine, other):
    return pl.pallas_call(
        rows_kernel,
        in_specs=[VMEM] * 4,
        out_specs=VMEM,
        out_shape=jax.ShapeDtypeStruct((8, 192, RANK), F32),
        scratch_shapes=[pltpu.VMEM((2304, 2 * RANK), BF16), pltpu.VMEM((2, RANK, RANK), F32)],
        compiler_params=pltpu.CompilerParams(vmem_limit_bytes=VMEM_LIMIT),
        cost_estimate=pl.CostEstimate(
            flops=6 * 512 * 2304 * RANK, bytes_accessed=7_000_000, transcendentals=0
        ),
        name="partial_rows",
    )(high, low, mine, other)


def right_kernel(
    high, low, r0, r1, r2, r3, r4, r5, r6, r7, keep, send, projected, lhs
):
    core = lax.rem(lax.axis_index("fsdp"), 2)
    tensor = lax.axis_index("tensor")

    def put(at, value):
        @pl.when(core == at // HALF)
        def _():
            keep[at % HALF] = value

        @pl.when(core != at // HALF)
        def _():
            send[at % HALF] = value

    def times(m, lo, hi):
        both = dot(lhs[m], high[:, lo:hi])
        return both[:RANK] + both[RANK:] + dot(lhs[m, :RANK], low[:, lo:hi])

    for d, rows in enumerate((r0, r1, r2, r3, r4, r5, r6, r7)):
        at = pl.multiple_of(lax.rem(tensor + (8 - d), 8) * 64, 64)
        for m in range(3):
            projected[m, pl.ds(at, 64)] = rows[64 * m : 64 * m + 64]
    for m in range(3):
        p = projected[m]
        turned = p.T
        h, l = split(turned)
        lhs[m, :RANK] = h
        lhs[m, RANK:] = l
        put(18 + m, jnp.dot(turned, p, precision=HIGHEST, preferred_element_type=F32))
    for lo in range(0, 2048, 512):
        right = times(0, lo, lo + 512)
        for i in range(4):
            put(lo // RANK + i, right[:, RANK * i : RANK * i + RANK])
    put(16, times(1, 2048, 2176))
    put(17, times(2, 2176, 2304))
    put(21, jnp.zeros((RANK, RANK), F32))


def right_parts(high, low, rows):
    half = (HALF, RANK, RANK)
    return pl.pallas_call(
        right_kernel,
        in_specs=[VMEM] * 10,
        out_specs=[VMEM] * 3,
        out_shape=[
            jax.ShapeDtypeStruct(half, F32),
            jax.ShapeDtypeStruct(half, F32),
            jax.ShapeDtypeStruct((3, 512, RANK), F32),
        ],
        scratch_shapes=[pltpu.VMEM((3, 2 * RANK, 512), BF16)],
        compiler_params=pltpu.CompilerParams(vmem_limit_bytes=VMEM_LIMIT),
        cost_estimate=pl.CostEstimate(
            flops=6 * 512 * 2304 * RANK, bytes_accessed=8_000_000, transcendentals=0
        ),
        name="right_parts",
    )(high, low, *rows)


def eliminate(work):
    sub = lax.broadcasted_iota(jnp.int32, (8, RANK), 0)
    for p in range(16):
        lo = 8 * p
        for m in range(3):
            panel = work[m, lo : lo + 8, :]
            if p > 0:
                coef = work[m, :lo, :RANK][:, lo : lo + 8]
                panel = panel - lax.dot_general(
                    coef,
                    work[m, :lo, :],
                    (((0,), (0,)), ((), ())),
                    precision=HIGHEST,
                    preferred_element_type=F32,
                )
            cols = [jnp.broadcast_to(panel[:, lo + k : lo + k + 1], (8, RANK)) for k in range(8)]
            left, right = panel[:, :RANK], panel[:, RANK:]
            for j in range(8):
                inv = lax.rsqrt(jnp.broadcast_to(cols[j][j : j + 1, :], (8, RANK)))
                row_left = jnp.broadcast_to(left[j : j + 1, :], (8, RANK)) * inv
                row_right = jnp.broadcast_to(right[j : j + 1, :], (8, RANK)) * inv
                below = jnp.where(sub > j, cols[j] * inv, 0.0)
                for k in range(j + 1, 8):
                    cols[k] = cols[k] - below * (jnp.broadcast_to(cols[k][j : j + 1, :], (8, RANK)) * inv)
                left = jnp.where(sub == j, row_left, left - below * row_left)
                right = jnp.where(sub == j, row_right, right - below * row_right)
            work[m, lo : lo + 8, :RANK] = left
            work[m, lo : lo + 8, RANK:] = right


def factor_kernel(
    mine, other, projected, ortho, right_high, right_low, squares, sq, sk, sv, work, turned
):
    fsdp = lax.axis_index("fsdp")
    core = lax.rem(fsdp, 2)

    def block(j):
        return jnp.where(core == j // HALF, mine[j % HALF], other[j % HALF])

    row = lax.broadcasted_iota(jnp.int32, (RANK, RANK), 0)
    col = lax.broadcasted_iota(jnp.int32, (RANK, RANK), 1)
    for m in range(3):
        work[m, :, :RANK] = block(18 + m)
        work[m, :, RANK:] = jnp.where(row == col, 1.0, 0.0).astype(F32)
    eliminate(work)
    for m, blocks in enumerate((range(16), (16,), (17,))):
        inverse = work[m, :, RANK:]
        ih, il = split(inverse)
        ph, plow = split(projected[m])
        ortho[m] = dot(ph, ih, (1, 1)) + dot(ph, il, (1, 1)) + dot(plow, ih, (1, 1))
        stacked = jnp.concatenate([ih, il], axis=0)
        total = jnp.zeros((RANK, RANK), F32)
        for j in blocks:
            zh, zl = split(block(j))
            both = dot(stacked, zh)
            right = both[:RANK] + both[RANK:] + dot(ih, zl)
            total += right * right
            high, low = split(right)
            right_high[:, RANK * j : RANK * j + RANK] = high
            right_low[:, RANK * j : RANK * j + RANK] = low
            if m == 0:
                @pl.when(lax.div(fsdp, 2) == j)
                def _():
                    turned[0] = right.T
            else:
                turned[m] = right.T
        sums = jnp.sum(total.T, axis=0, keepdims=True)
        for d in range(8):
            squares[d, m : m + 1, :] = sums
    for d in range(8):
        squares[d, 3:, :] = jnp.zeros((5, RANK), F32)
    odd = lax.rem(fsdp, 2)
    sq[...] = turned[0, pl.ds(pl.multiple_of(odd * 64, 64), 64)]
    for m, out in ((1, sk), (2, sv)):
        tile = turned[m, pl.ds(pl.multiple_of(lax.div(fsdp, 2) * 8, 8), 8)]
        out[...] = jnp.where(odd == 0, tile[:4], tile[4:])


def factor_and_rotate(mine, other, projected):
    return pl.pallas_call(
        factor_kernel,
        in_specs=[VMEM, VMEM, VMEM],
        out_specs=[VMEM] * 7,
        out_shape=[
            jax.ShapeDtypeStruct((3, 512, RANK), F32),
            jax.ShapeDtypeStruct((RANK, 2304), BF16),
            jax.ShapeDtypeStruct((RANK, 2304), BF16),
            jax.ShapeDtypeStruct((8, 8, RANK), F32),
            jax.ShapeDtypeStruct((64, RANK), F32),
            jax.ShapeDtypeStruct((4, RANK), F32),
            jax.ShapeDtypeStruct((4, RANK), F32),
        ],
        scratch_shapes=[pltpu.VMEM((3, RANK, 2 * RANK), F32), pltpu.VMEM((3, RANK, RANK), F32)],
        compiler_params=pltpu.CompilerParams(vmem_limit_bytes=VMEM_LIMIT),
        name="factor_and_rotate",
    )(mine, other, projected)


def store_split(lhs, m, value):
    high, low = split(value)
    lhs[m, :, :RANK] = high
    lhs[m, :, RANK:] = low


def minus_product(base, lhs, m, high, low):
    product = dot(lhs[m], jnp.concatenate([high, high], axis=0)) + dot(lhs[m, :, :RANK], low)
    return (base - product).astype(BF16)


def update_kernel(
    factors, high, low, wq, wk, wv, ortho, rh, rl, squares, sq, sk, sv,
    mq, mk, mv, out_q, out_k, out_v, bq, bk, bv, half, scaled,
):
    step = pl.program_id(0)

    def new(m, span, weight, moment_out, weight_out):
        base = high[:, span].astype(F32) + low[:, span].astype(F32)
        moment_out[...] = minus_product(base, half, m, rh[:, span], rl[:, span])
        weight_out[...] = minus_product(weight.astype(F32), scaled, m, rh[:, span], rl[:, span])

    @pl.when(step == 0)
    def _():
        inverse = lax.rsqrt(jnp.sum(squares[...], axis=0) + 1e-06)
        for m in range(3):
            store_split(half, m, 0.5 * ortho[m])
            store_split(scaled, m, ortho[m] * (factors[m] * inverse[m : m + 1]))
        for m, share, out in ((0, sq, bq), (1, sk, bk), (2, sv, bv)):
            out[...] = share[...] * inverse[m : m + 1]
        new(1, slice(2048, 2176), wk[...], mk, out_k)
        new(2, slice(2176, 2304), wv[...], mv, out_v)

    span = pl.ds(pl.multiple_of(step * WIDTH, WIDTH), WIDTH)
    new(0, span, wq[:, span], mq, out_q)


WIDTH = 2048 // STEPS
WIDE_SPECS = [column_spec(512), full_spec((512, RANK)), full_spec((512, RANK))]
WIDE_OUT = [
    jax.ShapeDtypeStruct((512, 2048), BF16),
    jax.ShapeDtypeStruct((512, RANK), BF16),
    jax.ShapeDtypeStruct((512, RANK), BF16),
]


def updates(factors, high, low, weights, ortho, rh, rl, squares, shares):
    share_specs = [full_spec((64, RANK)), full_spec((4, RANK)), full_spec((4, RANK))]
    return pl.pallas_call(
        functools.partial(update_kernel, factors),
        grid=(STEPS,),
        in_specs=[VMEM] * 12,
        out_specs=WIDE_SPECS + WIDE_SPECS + share_specs,
        out_shape=WIDE_OUT + WIDE_OUT + [jax.ShapeDtypeStruct(s.block_shape, F32) for s in share_specs],
        scratch_shapes=[pltpu.VMEM((3, 512, 2 * RANK), BF16)] * 2,
        compiler_params=pltpu.CompilerParams(vmem_limit_bytes=VMEM_LIMIT),
        cost_estimate=pl.CostEstimate(
            flops=12 * 512 * 2304 * RANK, bytes_accessed=16_000_000, transcendentals=0
        ),
        name="updates",
    )(high, low, *weights, ortho, rh, rl, squares, *shares)


def body(
    weight_q,
    momentum_q,
    grad_q,
    basis_q,
    weight_k,
    momentum_k,
    grad_k,
    basis_k,
    weight_v,
    momentum_v,
    grad_v,
    basis_v,
):
    weights = (weight_q, weight_k, weight_v)
    moments = (momentum_q, momentum_k, momentum_v)
    grads = (grad_q, grad_k, grad_v)
    factors = [
        0.25 * math.sqrt(w.shape[0] * lax.axis_size("fsdp") * w.shape[1] * lax.axis_size("tensor") / RANK)
        for w in weights
    ]

    high, low = blend_terms(moments, grads)
    mine = plane_gather(jnp.concatenate([basis_q, basis_k, basis_v], axis=0))
    mine, high, low = lax.optimization_barrier((mine, high, low))
    chunks = partial_rows(high, low, mine, swap_core(mine))
    own = small_kernel(total_kernel, (192, RANK), "own_rows", tensor_exchange(chunks))
    rows = [own] + [tensor_shift(own, d) for d in range(1, 8)]
    keep, send, projected = right_parts(high, low, rows)

    paired = small_kernel(pair_kernel, (HALF, RANK, RANK), "pair_sum", keep, swap_core(send))
    share = plane_exchange(paired.reshape(16, 88, RANK))
    share = small_kernel(repeat_total_kernel, (16, 88, RANK), "own_share", share)
    mine = plane_exchange(share).reshape(HALF, RANK, RANK)
    ortho, rh, rl, squares, *shares = factor_and_rotate(mine, swap_core(mine), projected)
    squares = tensor_exchange(squares)
    out = updates(factors, high, low, weights, ortho, rh, rl, squares, shares)
    return tuple(out[3 * j + i] for i in range(3) for j in (1, 0, 2))


def solution(mesh):
    placed = (
        P("fsdp", "tensor"),
        P("fsdp", "tensor"),
        P("fsdp", "tensor"),
        P(("tensor", "fsdp"), None),
    ) * 3
    return jax.shard_map(
        body,
        mesh=mesh,
        in_specs=placed,
        out_specs=(
            P("fsdp", "tensor"),
            P("fsdp", "tensor"),
            P(("tensor", "fsdp"), None),
        )
        * 3,
        check_vma=False,
    )
```

time: 168 us -> 154 us (0.917)
  Pallas kernels: 39.3 us -> 22.4 us
  local copies, waits for them, and re-layouts: 3.07 us -> 10.8 us
  blocking collectives: 79.3 us -> 73.1 us
  starting transfers between devices: 19.7 us -> 22.7 us
  other arithmetic: 2.62 us -> 0.8 us
    all_to_all x3 -> x2, blocking collectives: 48.8 us -> 31.7 us  [plane_exchange(): return lax.all_to_all(x, 'fsdp', 0, 0, tiled=True, axis_index_groups=PLANE)]
    pallas_call x5 -> x8, Pallas kernels: 39.3 us -> 22.4 us  [the longest x1 11.6 us: factor_and_rotate(): pl.pallas_call(factor_kernel, in_specs=[VMEM, VMEM, VMEM], out_specs=[VME...]
    all_to_all x1 -> x2, blocking collectives: 30.5 us -> 41.4 us  [tensor_exchange(): return lax.all_to_all(x, 'tensor', 0, 0, tiled=True)]
    unnamed x26 -> x24, local copies, waits for them, and re-layouts: 2.98 us -> 9.91 us
    all_to_all x1, starting transfers between devices: 4.32 us -> 7.58 us  [plane_exchange(): return lax.all_to_all(x, 'fsdp', 0, 0, tiled=True, axis_index_groups=PLANE)]
  transfers between devices with their start and end apart: 11 -> 11, of which waited for: 7 -> 7; matrix products, arithmetic and copies ran while one was open for 0% -> 0% of each run, Pallas kernels for 4% -> 1%
where the time goes in v3:
time: 154 us
  blocking collectives  73.1 us (47%)
  waiting for transfers between devices  23.3 us (15%)
  starting transfers between devices  22.7 us (15%)
  Pallas kernels  22.4 us (15%)
  local copies, waits for them, and re-layouts  10.8 us (7%)
    all_to_all x2, blocking collectives, tensor_exchange(): return lax.all_to_all(x, 'tensor', 0, 0, tiled=True)  41.4 us
    all_to_all x2, blocking collectives, plane_exchange(): return lax.all_to_all(x, 'fsdp', 0, 0, tiled=True, axis_index_groups=PLANE)  31.7 us
    ppermute x7, waiting for transfers between devices, tensor_shift(): lax.ppermute(x, 'tensor', [(i, (i + distance) % 8) for i in range(8)])  16.4 us
    pallas_call x1, Pallas kernels, factor_and_rotate(): pl.pallas_call(factor_kernel, in_specs=[VMEM, VMEM, VMEM], out_specs=[VME...  11.6 us
    unnamed x24, local copies, waits for them, and re-layouts  9.91 us
    ppermute x7, starting transfers between devices, tensor_shift(): lax.ppermute(x, 'tensor', [(i, (i + distance) % 8) for i in range(8)])  9.54 us
    all_to_all x1, starting transfers between devices, plane_exchange(): return lax.all_to_all(x, 'fsdp', 0, 0, tiled=True, axis_index_groups=PLANE)  7.58 us
    ppermute x3, starting transfers between devices, swap_core(): return lax.ppermute(x, 'fsdp', SIBLING)  5.6 us
  transfers between devices with their start and end apart: 11, of which 7 were waited for; matrix products, arithmetic and copies ran while one was open for 0% of the time, Pallas kernels for 1%

profile of v3, /device:TPU:1, one launch (start us, length us, event | category | flops | bytes accessed | tf_op | source)
XLA Modules:
  0.0 153.9 jit_solution(7444002254012787299)
XLA Ops:
  0.6 0.8 pad_maximum_fusion
  1.4 0.9 broadcast_in_dim.2
  2.3 7.6 %all-to-all-start = ((f32[16,72,128]{2,1,0:T(8,128)}), f32[16,72,128]{2,1,0:T(8,128)S(1)}, u32[]{:S(2)}, u32[]{:S(2)}) async-start(f32[16,72,128]{2,1,0:T(8,128)} %broadcast_in_dim.2), calls=%async_computation | async-start | bytes 1179648 | tf_op jit(solution)/shard_map/all_to_all | solution.py:28
  9.9 1.6 %copy-done.3 = bf16[512,2048]{1,0:T(8,128)(2,1)S(1)} copy-done((bf16[512,2048]{1,0:T(8,128)(2,1)S(1)}, bf16[512,2048]{1,0:T(8,128)(2,1)}, u32[]{:S(2)}) %copy-start.3) | copy-done | bytes 2097176
  11.5 1.6 %copy-done.4 = bf16[512,2048]{1,0:T(8,128)(2,1)S(1)} copy-done((bf16[512,2048]{1,0:T(8,128)(2,1)S(1)}, bf16[512,2048]{1,0:T(8,128)(2,1)}, u32[]{:S(2)}) %copy-start.4) | copy-done | bytes 2097176
  13.1 0.9 copy-done.8
  14.0 0.9 copy-done.9
  14.9 0.9 copy-done.10
  15.8 0.9 copy-done.11
  16.7 1.1 blend_terms.1
  17.8 1.4 copy-done
  19.2 1.7 %all-to-all-done.mine = f32[16,72,128]{2,1,0:T(8,128)S(1)} async-done(((f32[16,72,128]{2,1,0:T(8,128)}), f32[16,72,128]{2,1,0:T(8,128)S(1)}, u32[]{:S(2)}, u32[]{:S(2)}) %all-to-all-start) | async-done | bytes 589856 | tf_op jit(solution)/shard_map/all_to_all | solution.py:28
  20.9 1.9 %collective-permute-start = (f32[16,72,128]{2,1,0:T(8,128)S(1)}, f32[16,72,128]{2,1,0:T(8,128)S(1)}, u32[]{:S(2)}, u32[]{:S(2)}) collective-permute-start(f32[16,72,128]{2,1,0:T(8,128)S(1)} %all-to-all-done.mine), channel_id=1, source_target_pairs={{0,8},{8,0},{16,24},{24,16},{32,40},{40,32},{48,56},{56,48},{64,72... | collective-permute-start | bytes 1769480 | tf_op jit(solution)/shard_map/ppermute | solution.py:24
  22.7 1.6 %collective-permute-done.other = f32[16,72,128]{2,1,0:T(8,128)S(1)} collective-permute-done((f32[16,72,128]{2,1,0:T(8,128)S(1)}, f32[16,72,128]{2,1,0:T(8,128)S(1)}, u32[]{:S(2)}, u32[]{:S(2)}) %collective-permute-start) | collective-permute-done | bytes 589856 | tf_op jit(solution)/shard_map/ppermute | solution.py:24
  24.4 1.7 %copy-done.1 = bf16[512,2304]{1,0:T(8,128)(2,1)S(1)} copy-done((bf16[512,2304]{1,0:T(8,128)(2,1)S(1)}, bf16[512,2304]{1,0:T(8,128)(2,1)}, u32[]{:S(2)}) %copy-start.1) | copy-done | bytes 2359320
  26.0 1.5 partial_rows.1
  27.5 30.4 %all_to_all.25.parts = f32[8,192,128]{2,1,0:T(8,128)S(1)} all-to-all(f32[8,192,128]{2,1,0:T(8,128)S(1)} %partial_rows.1), channel_id=1, replica_groups=mesh['fsdp'=32,'tensor'=8] {'tensor'}, dimensions={0} | all-to-all | bytes 1572864 | tf_op jit(solution)/shard_map/all_to_all | solution.py:36
  58.9 1.9 %collective-permute-start.5 = (f32[192,128]{1,0:T(8,128)S(1)}, f32[192,128]{1,0:T(8,128)S(1)}, u32[]{:S(2)}, u32[]{:S(2)}) collective-permute-start(f32[192,128]{1,0:T(8,128)S(1)} %own_rows.1.r0), channel_id=1, source_target_pairs={{0,5},{1,6},{2,7},{3,0},{4,1},{5,2},{6,3},{7,4},{8,13},{9,14},{10,... | collective-permute-start | bytes 294920 | tf_op jit(solution)/shard_map/ppermute | solution.py:40
  60.8 3.7 %collective-permute-start.4 = (f32[192,128]{1,0:T(8,128)S(1)}, f32[192,128]{1,0:T(8,128)S(1)}, u32[]{:S(2)}, u32[]{:S(2)}) collective-permute-start(f32[192,128]{1,0:T(8,128)S(1)} %own_rows.1.r0), channel_id=1, source_target_pairs={{0,4},{1,5},{2,6},{3,7},{4,0},{5,1},{6,2},{7,3},{8,12},{9,13},{10,... | collective-permute-start | bytes 294920 | tf_op jit(solution)/shard_map/ppermute | solution.py:40
  65.0 2.6 %collective-permute-start.2 = (f32[192,128]{1,0:T(8,128)S(1)}, f32[192,128]{1,0:T(8,128)S(1)}, u32[]{:S(2)}, u32[]{:S(2)}) collective-permute-start(f32[192,128]{1,0:T(8,128)S(1)} %own_rows.1.r0), channel_id=1, source_target_pairs={{0,2},{1,3},{2,4},{3,5},{4,6},{5,7},{6,0},{7,1},{8,10},{9,11},{10,... | collective-permute-start | bytes 294920 | tf_op jit(solution)/shard_map/ppermute | solution.py:40
  67.6 2.1 %collective-permute-done.5.r5 = f32[192,128]{1,0:T(8,128)S(1)} collective-permute-done((f32[192,128]{1,0:T(8,128)S(1)}, f32[192,128]{1,0:T(8,128)S(1)}, u32[]{:S(2)}, u32[]{:S(2)}) %collective-permute-start.5) | collective-permute-done | bytes 98336 | tf_op jit(solution)/shard_map/ppermute | solution.py:40
  69.7 8.8 %collective-permute-done.3.r3 = f32[192,128]{1,0:T(8,128)S(1)} collective-permute-done((f32[192,128]{1,0:T(8,128)S(1)}, f32[192,128]{1,0:T(8,128)S(1)}, u32[]{:S(2)}, u32[]{:S(2)}) %collective-permute-start.3) | collective-permute-done | bytes 98336 | tf_op jit(solution)/shard_map/ppermute | solution.py:40
  78.5 5.4 %collective-permute-done.1.r1 = f32[192,128]{1,0:T(8,128)S(1)} collective-permute-done((f32[192,128]{1,0:T(8,128)S(1)}, f32[192,128]{1,0:T(8,128)S(1)}, u32[]{:S(2)}, u32[]{:S(2)}) %collective-permute-start.1) | collective-permute-done | bytes 98336 | tf_op jit(solution)/shard_map/ppermute | solution.py:40
  83.9 3.4 %right_parts.1 = (f32[11,128,128]{2,1,0:T(8,128)S(1)}, f32[11,128,128]{2,1,0:T(8,128)S(1)}, f32[3,512,128]{2,1,0:T(8,128)S(1)}) custom-call(bf16[512,2304]{1,0:T(8,128)(2,1)S(1)} %get-tuple-element.35.high, bf16[512,2304]{1,0:T(8,128)(2,1)S(1)} %copy-done.2, f32[192,128]{1,0:T(8,128)S(1)} %own_rows.1.r0, f32[192,128]{1,0:T(8,128)S(1)} %collective-permute-done.1.r1, ...), custom_call_target="tpu_custom_call" | custom-call | flops 905969664 | bytes 8000000 | tf_op jit(solution)/shard_map/right_parts/pallas_call | solution.py:201
  88.1 1.8 %collective-permute-done.8.b = f32[11,128,128]{2,1,0:T(8,128)S(1)} collective-permute-done((f32[11,128,128]{2,1,0:T(8,128)S(1)}, f32[11,128,128]{2,1,0:T(8,128)S(1)}, u32[]{:S(2)}, u32[]{:S(2)}) %collective-permute-start.8) | collective-permute-done | bytes 720928 | tf_op jit(solution)/shard_map/ppermute | solution.py:24
  90.0 16.6 %all_to_all.26.parts = f32[16,88,128]{2,1,0:T(8,128)S(1)} all-to-all(f32[16,88,128]{2,1,0:T(8,128)S(1)} %bitcast.4), channel_id=1, replica_groups={{0,16,32,48,64,80,96,112,128,144,160,176,192,208,224,240},{8,24,40,56,7..., dimensions={0} | all-to-all | bytes 1441792 | tf_op jit(solution)/shard_map/all_to_all | solution.py:28
  106.8 15.0 %all_to_all.27 = f32[16,88,128]{2,1,0:T(8,128)S(1)} all-to-all(f32[16,88,128]{2,1,0:T(8,128)S(1)} %own_share.1), channel_id=1, replica_groups={{0,16,32,48,64,80,96,112,128,144,160,176,192,208,224,240},{8,24,40,56,7..., dimensions={0} | all-to-all | bytes 1441792 | tf_op jit(solution)/shard_map/all_to_all | solution.py:28
  121.8 3.0 %collective-permute-start.9 = (f32[11,128,128]{2,1,0:T(8,128)S(1)}, f32[11,128,128]{2,1,0:T(8,128)S(1)}, u32[]{:S(2)}, u32[]{:S(2)}) collective-permute-start(f32[11,128,128]{2,1,0:T(8,128)S(1)} %bitcast.2), channel_id=1, source_target_pairs={{0,8},{8,0},{16,24},{24,16},{32,40},{40,32},{48,56},{56,48},{64,72... | collective-permute-start | bytes 2162696 | tf_op jit(solution)/shard_map/ppermute | solution.py:24
  124.8 1.8 %collective-permute-done.9.other = f32[11,128,128]{2,1,0:T(8,128)S(1)} collective-permute-done((f32[11,128,128]{2,1,0:T(8,128)S(1)}, f32[11,128,128]{2,1,0:T(8,128)S(1)}, u32[]{:S(2)}, u32[]{:S(2)}) %collective-permute-start.9) | collective-permute-done | bytes 720928 | tf_op jit(solution)/shard_map/ppermute | solution.py:24
  126.6 11.6 %factor_and_rotate.1 = (f32[3,512,128]{2,1,0:T(8,128)S(1)}, bf16[128,2304]{1,0:T(8,128)(2,1)S(1)}, bf16[128,2304]{1,0:T(8,128)(2,1)S(1)}, f32[8,8,128]{2,1,0:T(8...) custom-call(f32[11,128,128]{2,1,0:T(8,128)S(1)} %bitcast.3, ...), custom_call_target="tpu_custom_call" | custom-call | tf_op jit(solution)/shard_map/factor_and_rotate/pallas_call | solution.py:298
  138.2 11.0 %all_to_all.28.squares = f32[8,8,128]{2,1,0:T(8,128)S(1)} all-to-all(f32[8,8,128]{2,1,0:T(8,128)S(1)} %get-tuple-element.44), channel_id=1, replica_groups=mesh['fsdp'=32,'tensor'=8] {'tensor'}, dimensions={0} | all-to-all | bytes 65536 | tf_op jit(solution)/shard_map/all_to_all | solution.py:36
  149.2 4.7 %updates.1 = (bf16[512,2048]{1,0:T(8,128)(2,1)}, bf16[512,128]{1,0:T(8,128)(2,1)}, bf16[512,128]{1,0:T(8,128)(2,1)}, bf16[512,2048]{1,0:T(8,128)(2,1)}, bf16[512...) custom-call(bf16[512,2304]{1,0:T(8,128)(2,1)S(1)} %get-tuple-element, ...), custom_call_target="tpu_custom_call" | custom-call | flops 1811939328 | bytes 16000000 | tf_op jit(solution)/shard_map/updates/pallas_call | solution.py:365
  (28 shorter events, 2.4 us)
Async XLA Ops:
  2.3 18.6 %all-to-all-start = ((f32[16,72,128]{2,1,0:T(8,128)}), f32[16,72,128]{2,1,0:T(8,128)S(1)}, u32[]{:S(2)}, u32[]{:S(2)}) async-start(f32[16,72,128]{2,1,0:T(8,128)} %broadcast_in_dim.2), calls=%async_computation | async-start | bytes 1179648 | tf_op jit(solution)/shard_map/all_to_all | solution.py:28
  9.9 1.6 %copy-start.3 = (bf16[512,2048]{1,0:T(8,128)(2,1)S(1)}, bf16[512,2048]{1,0:T(8,128)(2,1)}, u32[]{:S(2)}) copy-start(bf16[512,2048]{1,0:T(8,128)(2,1)} %mq.1) | copy-start | bytes 6291460
  11.5 1.6 %copy-start.4 = (bf16[512,2048]{1,0:T(8,128)(2,1)S(1)}, bf16[512,2048]{1,0:T(8,128)(2,1)}, u32[]{:S(2)}) copy-start(bf16[512,2048]{1,0:T(8,128)(2,1)} %gq.1) | copy-start | bytes 6291460
  13.1 0.9 copy-start.8
  14.0 0.9 copy-start.9
  14.9 0.9 copy-start.10
  15.8 0.9 copy-start.11
  17.8 1.4 copy-start
  20.9 3.5 %collective-permute-start = (f32[16,72,128]{2,1,0:T(8,128)S(1)}, f32[16,72,128]{2,1,0:T(8,128)S(1)}, u32[]{:S(2)}, u32[]{:S(2)}) collective-permute-start(f32[16,72,128]{2,1,0:T(8,128)S(1)} %all-to-all-done.mine), channel_id=1, source_target_pairs={{0,8},{8,0},{16,24},{24,16},{32,40},{40,32},{48,56},{56,48},{64,72... | collective-permute-start | bytes 1769480 | tf_op jit(solution)/shard_map/ppermute | solution.py:24
  24.4 1.7 %copy-start.1 = (bf16[512,2304]{1,0:T(8,128)(2,1)S(1)}, bf16[512,2304]{1,0:T(8,128)(2,1)}, u32[]{:S(2)}) copy-start(bf16[512,2304]{1,0:T(8,128)(2,1)} %copy-done) | copy-start | bytes 7077892
  27.5 56.4 %copy-start.2 = (bf16[512,2304]{1,0:T(8,128)(2,1)S(1)}, bf16[512,2304]{1,0:T(8,128)(2,1)}, u32[]{:S(2)}) copy-start(bf16[512,2304]{1,0:T(8,128)(2,1)} %copy-done) | copy-start | bytes 7077892
  58.0 6.9 %collective-permute-start.7 = (f32[192,128]{1,0:T(8,128)S(1)}, f32[192,128]{1,0:T(8,128)S(1)}, u32[]{:S(2)}, u32[]{:S(2)}) collective-permute-start(f32[192,128]{1,0:T(8,128)S(1)} %own_rows.1.r0), channel_id=1, source_target_pairs={{0,7},{1,0},{2,1},{3,2},{4,3},{5,4},{6,5},{7,6},{8,15},{9,8},{10,9... | collective-permute-start | bytes 294920 | tf_op jit(solution)/shard_map/ppermute | solution.py:40
  58.1 9.5 %collective-permute-start.6 = (f32[192,128]{1,0:T(8,128)S(1)}, f32[192,128]{1,0:T(8,128)S(1)}, u32[]{:S(2)}, u32[]{:S(2)}) collective-permute-start(f32[192,128]{1,0:T(8,128)S(1)} %own_rows.1.r0), channel_id=1, source_target_pairs={{0,6},{1,7},{2,0},{3,1},{4,2},{5,3},{6,4},{7,5},{8,14},{9,15},{10,... | collective-permute-start | bytes 294920 | tf_op jit(solution)/shard_map/ppermute | solution.py:40
  58.9 10.8 %collective-permute-start.5 = (f32[192,128]{1,0:T(8,128)S(1)}, f32[192,128]{1,0:T(8,128)S(1)}, u32[]{:S(2)}, u32[]{:S(2)}) collective-permute-start(f32[192,128]{1,0:T(8,128)S(1)} %own_rows.1.r0), channel_id=1, source_target_pairs={{0,5},{1,6},{2,7},{3,0},{4,1},{5,2},{6,3},{7,4},{8,13},{9,14},{10,... | collective-permute-start | bytes 294920 | tf_op jit(solution)/shard_map/ppermute | solution.py:40
  60.8 8.9 %collective-permute-start.4 = (f32[192,128]{1,0:T(8,128)S(1)}, f32[192,128]{1,0:T(8,128)S(1)}, u32[]{:S(2)}, u32[]{:S(2)}) collective-permute-start(f32[192,128]{1,0:T(8,128)S(1)} %own_rows.1.r0), channel_id=1, source_target_pairs={{0,4},{1,5},{2,6},{3,7},{4,0},{5,1},{6,2},{7,3},{8,12},{9,13},{10,... | collective-permute-start | bytes 294920 | tf_op jit(solution)/shard_map/ppermute | solution.py:40
  64.5 14.1 %collective-permute-start.3 = (f32[192,128]{1,0:T(8,128)S(1)}, f32[192,128]{1,0:T(8,128)S(1)}, u32[]{:S(2)}, u32[]{:S(2)}) collective-permute-start(f32[192,128]{1,0:T(8,128)S(1)} %own_rows.1.r0), channel_id=1, source_target_pairs={{0,3},{1,4},{2,5},{3,6},{4,7},{5,0},{6,1},{7,2},{8,11},{9,12},{10,... | collective-permute-start | bytes 294920 | tf_op jit(solution)/shard_map/ppermute | solution.py:40
  65.0 13.6 %collective-permute-start.2 = (f32[192,128]{1,0:T(8,128)S(1)}, f32[192,128]{1,0:T(8,128)S(1)}, u32[]{:S(2)}, u32[]{:S(2)}) collective-permute-start(f32[192,128]{1,0:T(8,128)S(1)} %own_rows.1.r0), channel_id=1, source_target_pairs={{0,2},{1,3},{2,4},{3,5},{4,6},{5,7},{6,0},{7,1},{8,10},{9,11},{10,... | collective-permute-start | bytes 294920 | tf_op jit(solution)/shard_map/ppermute | solution.py:40
  67.6 16.4 %collective-permute-start.1 = (f32[192,128]{1,0:T(8,128)S(1)}, f32[192,128]{1,0:T(8,128)S(1)}, u32[]{:S(2)}, u32[]{:S(2)}) collective-permute-start(f32[192,128]{1,0:T(8,128)S(1)} %own_rows.1.r0), channel_id=1, source_target_pairs={{0,1},{1,2},{2,3},{3,4},{4,5},{5,6},{6,7},{7,0},{8,9},{9,10},{10,1... | collective-permute-start | bytes 294920 | tf_op jit(solution)/shard_map/ppermute | solution.py:40
  87.4 2.6 %collective-permute-start.8 = (f32[11,128,128]{2,1,0:T(8,128)S(1)}, f32[11,128,128]{2,1,0:T(8,128)S(1)}, u32[]{:S(2)}, u32[]{:S(2)}) collective-permute-start(f32[11,128,128]{2,1,0:T(8,128)S(1)} %get-tuple-element.39), channel_id=1, source_target_pairs={{0,8},{8,0},{16,24},{24,16},{32,40},{40,32},{48,56},{56,48},{64,72... | collective-permute-start | bytes 2162696 | tf_op jit(solution)/shard_map/ppermute | solution.py:24
  106.7 42.4 %copy-start.5 = (bf16[512,2048]{1,0:T(8,128)(2,1)S(1)}, bf16[512,2048]{1,0:T(8,128)(2,1)}, u32[]{:S(2)}) copy-start(bf16[512,2048]{1,0:T(8,128)(2,1)} %wq.1) | copy-start | bytes 6291460
  106.8 42.4 %copy-start.6 = (bf16[512,128]{1,0:T(8,128)(2,1)S(1)}, bf16[512,128]{1,0:T(8,128)(2,1)}, u32[]{:S(2)}) copy-start(bf16[512,128]{1,0:T(8,128)(2,1)} %wk.1) | copy-start | bytes 393220
  106.8 42.4 %copy-start.7 = (bf16[512,128]{1,0:T(8,128)(2,1)S(1)}, bf16[512,128]{1,0:T(8,128)(2,1)}, u32[]{:S(2)}) copy-start(bf16[512,128]{1,0:T(8,128)(2,1)} %wv.1) | copy-start | bytes 393220
  121.8 4.8 %collective-permute-start.9 = (f32[11,128,128]{2,1,0:T(8,128)S(1)}, f32[11,128,128]{2,1,0:T(8,128)S(1)}, u32[]{:S(2)}, u32[]{:S(2)}) collective-permute-start(f32[11,128,128]{2,1,0:T(8,128)S(1)} %bitcast.2), channel_id=1, source_target_pairs={{0,8},{8,0},{16,24},{24,16},{32,40},{40,32},{48,56},{56,48},{64,72... | collective-permute-start | bytes 2162696 | tf_op jit(solution)/shard_map/ppermute | solution.py:24

commit v4 on v3

--- a/solution.py
+++ b/solution.py
@@ -28,16 +28,8 @@
     return lax.all_to_all(x, "fsdp", 0, 0, tiled=True, axis_index_groups=PLANE)
 
 
-def plane_gather(x):
-    return plane_exchange(jnp.broadcast_to(x[None], (16,) + x.shape))
-
-
 def tensor_exchange(x):
     return lax.all_to_all(x, "tensor", 0, 0, tiled=True)
-
-
-def tensor_shift(x, distance):
-    return lax.ppermute(x, "tensor", [(i, (i + distance) % 8) for i in range(8)])
 
 
 def dot(a, b, contract=(1, 0)):
@@ -102,13 +94,26 @@
     )(*operands)
 
 
-def total_kernel(parts, out):
-    out[...] = jnp.sum(parts[...], axis=0)
+def repeat_bases_kernel(q, k, v, out):
+    for i in range(out.shape[0]):
+        out[i, :64] = q[...]
+        out[i, 64:68] = k[...]
+        out[i, 68:72] = v[...]
+
+
+def repeat_bases(bases):
+    return pl.pallas_call(
+        repeat_bases_kernel,
+        in_specs=[VMEM] * 3,
+        out_specs=VMEM,
+        out_shape=jax.ShapeDtypeStruct((16, 72, RANK), F32),
+        name="repeat_bases",
+    )(*bases)
 
 
 def repeat_total_kernel(parts, out):
     total = jnp.sum(parts[...], axis=0)
-    for i in range(16):
+    for i in range(out.shape[0]):
         out[i] = total
 
 
@@ -157,97 +162,132 @@
     )(high, low, mine, other)
 
 
-def right_kernel(
-    high, low, r0, r1, r2, r3, r4, r5, r6, r7, keep, send, projected, lhs
-):
-    core = lax.rem(lax.axis_index("fsdp"), 2)
-    tensor = lax.axis_index("tensor")
-
-    def put(at, value):
-        @pl.when(core == at // HALF)
-        def _():
-            keep[at % HALF] = value
-
-        @pl.when(core != at // HALF)
-        def _():
-            send[at % HALF] = value
-
+def half_of_right(half, high, low, projected, lhs, out):
     def times(m, lo, hi):
         both = dot(lhs[m], high[:, lo:hi])
         return both[:RANK] + both[RANK:] + dot(lhs[m, :RANK], low[:, lo:hi])
 
-    for d, rows in enumerate((r0, r1, r2, r3, r4, r5, r6, r7)):
-        at = pl.multiple_of(lax.rem(tensor + (8 - d), 8) * 64, 64)
+    first = 0 if half == 0 else HALF
+    for lo in range(first, min(first + HALF, 16), 4):
+        hi = min(lo + 4, first + HALF, 16)
+        right = times(0, RANK * lo, RANK * hi)
+        for i in range(hi - lo):
+            out[lo - first + i] = right[:, RANK * i : RANK * i + RANK]
+    if half == 1:
+        out[16 - HALF] = times(1, 2048, 2176)
+        out[17 - HALF] = times(2, 2176, 2304)
         for m in range(3):
-            projected[m, pl.ds(at, 64)] = rows[64 * m : 64 * m + 64]
+            p = projected[m]
+            out[18 - HALF + m] = jnp.dot(p.T, p, precision=HIGHEST, preferred_element_type=F32)
+        out[21 - HALF] = jnp.zeros((RANK, RANK), F32)
+
+
+def send_kernel(high, low, rows, send, projected, lhs):
+    for d in range(8):
+        for m in range(3):
+            projected[m, 64 * d : 64 * d + 64] = rows[d, 64 * m : 64 * m + 64]
     for m in range(3):
-        p = projected[m]
-        turned = p.T
-        h, l = split(turned)
+        h, l = split(projected[m].T)
         lhs[m, :RANK] = h
         lhs[m, RANK:] = l
-        put(18 + m, jnp.dot(turned, p, precision=HIGHEST, preferred_element_type=F32))
-    for lo in range(0, 2048, 512):
-        right = times(0, lo, lo + 512)
-        for i in range(4):
-            put(lo // RANK + i, right[:, RANK * i : RANK * i + RANK])
-    put(16, times(1, 2048, 2176))
-    put(17, times(2, 2176, 2304))
-    put(21, jnp.zeros((RANK, RANK), F32))
-
-
-def right_parts(high, low, rows):
-    half = (HALF, RANK, RANK)
-    return pl.pallas_call(
-        right_kernel,
-        in_specs=[VMEM] * 10,
+    core = lax.rem(lax.axis_index("fsdp"), 2)
+    for half in range(2):
+        pl.when(core != half)(
+            functools.partial(half_of_right, half, high, low, projected, lhs, send)
+        )
+
+
+def keep_kernel(high, low, projected, lhs, keep):
+    core = lax.rem(lax.axis_index("fsdp"), 2)
+    for half in range(2):
+        pl.when(core == half)(
+            functools.partial(half_of_right, half, high, low, projected, lhs, keep)
+        )
+
+
+HALF_SHAPE = jax.ShapeDtypeStruct((HALF, RANK, RANK), F32)
+HALF_COST = pl.CostEstimate(
+    flops=3 * 512 * 2304 * RANK, bytes_accessed=5_000_000, transcendentals=0
+)
+
+
+def part_to_send(high, low, rows):
+    return pl.pallas_call(
+        send_kernel,
+        in_specs=[VMEM] * 3,
         out_specs=[VMEM] * 3,
         out_shape=[
-            jax.ShapeDtypeStruct(half, F32),
-            jax.ShapeDtypeStruct(half, F32),
+            HALF_SHAPE,
             jax.ShapeDtypeStruct((3, 512, RANK), F32),
+            jax.ShapeDtypeStruct((3, 2 * RANK, 512), BF16),
         ],
-        scratch_shapes=[pltpu.VMEM((3, 2 * RANK, 512), BF16)],
-        compiler_params=pltpu.CompilerParams(vmem_limit_bytes=VMEM_LIMIT),
-        cost_estimate=pl.CostEstimate(
-            flops=6 * 512 * 2304 * RANK, bytes_accessed=8_000_000, transcendentals=0
-        ),
-        name="right_parts",
-    )(high, low, *rows)
-
-
-def eliminate(work):
+        compiler_params=pltpu.CompilerParams(vmem_limit_bytes=VMEM_LIMIT),
+        cost_estimate=HALF_COST,
+        name="part_to_send",
+    )(high, low, rows)
+
+
+def part_to_keep(high, low, projected, lhs):
+    return pl.pallas_call(
+        keep_kernel,
+        in_specs=[VMEM] * 4,
+        out_specs=VMEM,
+        out_shape=HALF_SHAPE,
+        compiler_params=pltpu.CompilerParams(vmem_limit_bytes=VMEM_LIMIT),
+        cost_estimate=HALF_COST,
+        name="part_to_keep",
+    )(high, low, projected, lhs)
+
+
+def invert(grams):
     sub = lax.broadcasted_iota(jnp.int32, (8, RANK), 0)
+    lane = lax.broadcasted_iota(jnp.int32, (8, RANK), 1)
+    count = len(grams)
+    rows = [[g[8 * p : 8 * p + 8] for p in range(16)] for g in grams]
+    done = [[] for _ in grams]
     for p in range(16):
         lo = 8 * p
-        for m in range(3):
-            panel = work[m, lo : lo + 8, :]
-            if p > 0:
-                coef = work[m, :lo, :RANK][:, lo : lo + 8]
-                panel = panel - lax.dot_general(
-                    coef,
-                    work[m, :lo, :],
-                    (((0,), (0,)), ((), ())),
-                    precision=HIGHEST,
-                    preferred_element_type=F32,
+        for m in range(count):
+            panel = rows[m][p]
+            cols = [jnp.broadcast_to(panel[:, lo + k : lo + k + 1], (8, RANK)) for k in range(8)]
+            inverse = jnp.zeros((8, RANK), F32)
+            for j in range(8):
+                at = sub == j
+                here = lane == lo + j
+                root = lax.rsqrt(jnp.broadcast_to(cols[j][j : j + 1], (8, RANK)))
+                scale = root * root
+                row = jnp.where(here, 1.0, jnp.broadcast_to(panel[j : j + 1], (8, RANK)))
+                inverse = jnp.where(at, row * root, inverse)
+                row = row * scale
+                panel = jnp.where(at, row, jnp.where(here, 0.0, panel) - cols[j] * row)
+                for k in range(j + 1, 8):
+                    entry = jnp.broadcast_to(cols[k][j : j + 1], (8, RANK)) * scale
+                    cols[k] = jnp.where(at, entry, cols[k] - cols[j] * entry)
+            done[m].append(jnp.where(lane <= sub + lo, inverse, 0.0))
+            inside = (lane >= lo) & (lane < lo + 8)
+            if p < 15:
+                ahead = rows[m][p + 1]
+                total = jnp.where(inside, 0.0, ahead)
+                for k in range(8):
+                    column = jnp.broadcast_to(ahead[:, lo + k : lo + k + 1], (8, RANK))
+                    total -= column * jnp.broadcast_to(panel[k : k + 1], (8, RANK))
+                rows[m][p + 1] = total
+            if p < 14:
+                rest = jnp.concatenate(rows[m][p + 2 :], axis=0)
+                pieces = [panel]
+                if lo > 0:
+                    pieces = [jnp.zeros((lo, RANK), F32)] + pieces
+                pieces = pieces + [jnp.zeros((RANK - lo - 8, RANK), F32)]
+                product = jnp.dot(
+                    rest, jnp.concatenate(pieces, axis=0), precision=HIGHEST, preferred_element_type=F32
                 )
-            cols = [jnp.broadcast_to(panel[:, lo + k : lo + k + 1], (8, RANK)) for k in range(8)]
-            left, right = panel[:, :RANK], panel[:, RANK:]
-            for j in range(8):
-                inv = lax.rsqrt(jnp.broadcast_to(cols[j][j : j + 1, :], (8, RANK)))
-                row_left = jnp.broadcast_to(left[j : j + 1, :], (8, RANK)) * inv
-                row_right = jnp.broadcast_to(right[j : j + 1, :], (8, RANK)) * inv
-                below = jnp.where(sub > j, cols[j] * inv, 0.0)
-                for k in range(j + 1, 8):
-                    cols[k] = cols[k] - below * (jnp.broadcast_to(cols[k][j : j + 1, :], (8, RANK)) * inv)
-                left = jnp.where(sub == j, row_left, left - below * row_left)
-                right = jnp.where(sub == j, row_right, right - below * row_right)
-            work[m, lo : lo + 8, :RANK] = left
-            work[m, lo : lo + 8, RANK:] = right
+                for i in range(p + 2, 16):
+                    rows[m][i] = jnp.where(inside, 0.0, rows[m][i]) - product[8 * (i - p - 2) : 8 * (i - p - 1)]
+    return [jnp.concatenate(d, axis=0) for d in done]
 
 
 def factor_kernel(
-    mine, other, projected, ortho, right_high, right_low, squares, sq, sk, sv, work, turned
+    mine, other, projected, ortho, right_high, right_low, squares, sq, sk, sv, turned
 ):
     fsdp = lax.axis_index("fsdp")
     core = lax.rem(fsdp, 2)
@@ -255,15 +295,9 @@
     def block(j):
         return jnp.where(core == j // HALF, mine[j % HALF], other[j % HALF])
 
-    row = lax.broadcasted_iota(jnp.int32, (RANK, RANK), 0)
-    col = lax.broadcasted_iota(jnp.int32, (RANK, RANK), 1)
-    for m in range(3):
-        work[m, :, :RANK] = block(18 + m)
-        work[m, :, RANK:] = jnp.where(row == col, 1.0, 0.0).astype(F32)
-    eliminate(work)
+    inverses = invert([block(18 + m) for m in range(3)])
     for m, blocks in enumerate((range(16), (16,), (17,))):
-        inverse = work[m, :, RANK:]
-        ih, il = split(inverse)
+        ih, il = split(inverses[m])
         ph, plow = split(projected[m])
         ortho[m] = dot(ph, ih, (1, 1)) + dot(ph, il, (1, 1)) + dot(plow, ih, (1, 1))
         stacked = jnp.concatenate([ih, il], axis=0)
@@ -308,40 +342,35 @@
             jax.ShapeDtypeStruct((4, RANK), F32),
             jax.ShapeDtypeStruct((4, RANK), F32),
         ],
-        scratch_shapes=[pltpu.VMEM((3, RANK, 2 * RANK), F32), pltpu.VMEM((3, RANK, RANK), F32)],
+        scratch_shapes=[pltpu.VMEM((3, RANK, RANK), F32)],
         compiler_params=pltpu.CompilerParams(vmem_limit_bytes=VMEM_LIMIT),
         name="factor_and_rotate",
     )(mine, other, projected)
 
 
-def store_split(lhs, m, value):
-    high, low = split(value)
-    lhs[m, :, :RANK] = high
-    lhs[m, :, RANK:] = low
-
-
-def minus_product(base, lhs, m, high, low):
-    product = dot(lhs[m], jnp.concatenate([high, high], axis=0)) + dot(lhs[m, :, :RANK], low)
-    return (base - product).astype(BF16)
-
-
 def update_kernel(
     factors, high, low, wq, wk, wv, ortho, rh, rl, squares, sq, sk, sv,
-    mq, mk, mv, out_q, out_k, out_v, bq, bk, bv, half, scaled,
+    mq, mk, mv, out_q, out_k, out_v, bq, bk, bv, lhs,
 ):
     step = pl.program_id(0)
 
     def new(m, span, weight, moment_out, weight_out):
-        base = high[:, span].astype(F32) + low[:, span].astype(F32)
-        moment_out[...] = minus_product(base, half, m, rh[:, span], rl[:, span])
-        weight_out[...] = minus_product(weight.astype(F32), scaled, m, rh[:, span], rl[:, span])
+        right = rh[:, span]
+        product = dot(lhs[m], jnp.concatenate([right, right], axis=0))
+        product += dot(lhs[m, :, :RANK], rl[:, span])
+        blend = high[:, span].astype(F32) + low[:, span].astype(F32)
+        moment_out[...] = (blend - product[:512]).astype(BF16)
+        weight_out[...] = (weight.astype(F32) - product[512:]).astype(BF16)
 
     @pl.when(step == 0)
     def _():
         inverse = lax.rsqrt(jnp.sum(squares[...], axis=0) + 1e-06)
         for m in range(3):
-            store_split(half, m, 0.5 * ortho[m])
-            store_split(scaled, m, ortho[m] * (factors[m] * inverse[m : m + 1]))
+            scale = factors[m] * inverse[m : m + 1]
+            for at, left in ((0, 0.5 * ortho[m]), (512, ortho[m] * scale)):
+                h, l = split(left)
+                lhs[m, at : at + 512, :RANK] = h
+                lhs[m, at : at + 512, RANK:] = l
         for m, share, out in ((0, sq, bq), (1, sk, bk), (2, sv, bv)):
             out[...] = share[...] * inverse[m : m + 1]
         new(1, slice(2048, 2176), wk[...], mk, out_k)
@@ -368,7 +397,7 @@
         in_specs=[VMEM] * 12,
         out_specs=WIDE_SPECS + WIDE_SPECS + share_specs,
         out_shape=WIDE_OUT + WIDE_OUT + [jax.ShapeDtypeStruct(s.block_shape, F32) for s in share_specs],
-        scratch_shapes=[pltpu.VMEM((3, 512, 2 * RANK), BF16)] * 2,
+        scratch_shapes=[pltpu.VMEM((3, 1024, 2 * RANK), BF16)],
         compiler_params=pltpu.CompilerParams(vmem_limit_bytes=VMEM_LIMIT),
         cost_estimate=pl.CostEstimate(
             flops=12 * 512 * 2304 * RANK, bytes_accessed=16_000_000, transcendentals=0
@@ -400,14 +429,16 @@
     ]
 
     high, low = blend_terms(moments, grads)
-    mine = plane_gather(jnp.concatenate([basis_q, basis_k, basis_v], axis=0))
+    mine = plane_exchange(repeat_bases((basis_q, basis_k, basis_v)))
     mine, high, low = lax.optimization_barrier((mine, high, low))
     chunks = partial_rows(high, low, mine, swap_core(mine))
-    own = small_kernel(total_kernel, (192, RANK), "own_rows", tensor_exchange(chunks))
-    rows = [own] + [tensor_shift(own, d) for d in range(1, 8)]
-    keep, send, projected = right_parts(high, low, rows)
-
-    paired = small_kernel(pair_kernel, (HALF, RANK, RANK), "pair_sum", keep, swap_core(send))
+    own = small_kernel(repeat_total_kernel, chunks.shape, "own_rows", tensor_exchange(chunks))
+    rows = tensor_exchange(own)
+    send, projected, lhs = part_to_send(high, low, rows)
+    sent = swap_core(send)
+    keep = part_to_keep(high, low, projected, lhs)
+
+    paired = small_kernel(pair_kernel, (HALF, RANK, RANK), "pair_sum", keep, sent)
     share = plane_exchange(paired.reshape(16, 88, RANK))
     share = small_kernel(repeat_total_kernel, (16, 88, RANK), "own_share", share)
     mine = plane_exchange(share).reshape(HALF, RANK, RANK)

time: 154 us -> 148 us (0.961)
  blocking collectives: 73.1 us -> 94.3 us
  waiting for transfers between devices: 23.3 us -> 5.62 us
  starting transfers between devices: 22.7 us -> 16.6 us
  Pallas kernels: 22.4 us -> 19.9 us
    all_to_all x2 -> x3, blocking collectives: 41.4 us -> 62.6 us  [tensor_exchange(): return lax.all_to_all(x, 'tensor', 0, 0, tiled=True)]
    ppermute x7 -> x0, waiting for transfers between devices: 16.4 us -> none  [tensor_shift(): lax.ppermute(x, 'tensor', [(i, (i + distance) % 8) for i in range(8)])]
    ppermute x7 -> x0, starting transfers between devices: 9.54 us -> none  [tensor_shift(): lax.ppermute(x, 'tensor', [(i, (i + distance) % 8) for i in range(8)])]
    ppermute x3, starting transfers between devices: 5.6 us -> 9.05 us  [swap_core(): return lax.ppermute(x, 'fsdp', SIBLING)]
    pallas_call x1, Pallas kernels: 11.6 us -> 8.22 us  [factor_and_rotate(): pl.pallas_call(factor_kernel, in_specs=[VMEM, VMEM, VMEM], out_specs=[VME...]
    pallas_call x1 -> x3, Pallas kernels: 3.4 us -> 4.02 us  [the longest x1 1.63 us: repeat_bases(): pl.pallas_call(repeat_bases_kernel, in_specs=[VMEM] * 3, out_specs=VMEM,...]
  transfers between devices with their start and end apart: 11 -> 4, of which waited for: 7 -> 4; matrix products, arithmetic and copies ran while one was open for 0% -> 0% of each run, Pallas kernels for 1% -> 2%
where the time goes in v4:
time: 148 us; the launch traced here: 147 us
  blocking collectives  94.3 us (64%)
  Pallas kernels  19.9 us (13%)
  starting transfers between devices  16.6 us (11%)
  local copies, waits for them, and re-layouts  9.89 us (7%)
  waiting for transfers between devices  5.62 us (4%)
    all_to_all x3, blocking collectives, tensor_exchange(): return lax.all_to_all(x, 'tensor', 0, 0, tiled=True)  62.6 us
    all_to_all x2, blocking collectives, plane_exchange(): return lax.all_to_all(x, 'fsdp', 0, 0, tiled=True, axis_index_groups=PLANE)  31.7 us
    unnamed x24, local copies, waits for them, and re-layouts  9.89 us
    ppermute x3, starting transfers between devices, swap_core(): return lax.ppermute(x, 'fsdp', SIBLING)  9.05 us
    pallas_call x1, Pallas kernels, factor_and_rotate(): pl.pallas_call(factor_kernel, in_specs=[VMEM, VMEM, VMEM], out_specs=[VME...  8.22 us
    all_to_all x1, starting transfers between devices, plane_exchange(): return lax.all_to_all(x, 'fsdp', 0, 0, tiled=True, axis_index_groups=PLANE)  7.58 us
    pallas_call x1, Pallas kernels, updates(): pl.pallas_call(functools.partial(update_kernel, factors), grid=(STEPS,),...  4.86 us
    ppermute x3, waiting for transfers between devices, swap_core(): return lax.ppermute(x, 'fsdp', SIBLING)  3.91 us
  transfers between devices with their start and end apart: 4, of which 4 were waited for; matrix products, arithmetic and copies ran while one was open for 0% of the time, Pallas kernels for 2%

profile of v4, /device:TPU:1, one launch (start us, length us, event | category | flops | bytes accessed | tf_op | source)
XLA Modules:
  0.0 147.0 jit_solution(8439330058833133887)
XLA Ops:
  0.6 1.6 %repeat_bases.1 = f32[16,72,128]{2,1,0:T(8,128)} custom-call(f32[64,128]{1,0:T(8,128)} %q.1, f32[4,128]{1,0:T(4,128)} %k.1, f32[4,128]{1,0:T(4,128)} %v.1), custom_call_target="tpu_custom_call" | custom-call | tf_op jit(solution)/shard_map/repeat_bases/pallas_call | solution.py:105
  2.3 7.6 %all-to-all-start = ((f32[16,72,128]{2,1,0:T(8,128)}), f32[16,72,128]{2,1,0:T(8,128)S(1)}, u32[]{:S(2)}, u32[]{:S(2)}) async-start(f32[16,72,128]{2,1,0:T(8,128)} %repeat_bases.1), calls=%async_computation | async-start | bytes 1179648 | tf_op jit(solution)/shard_map/all_to_all | solution.py:28
  9.9 0.0 copy-start.3
  9.9 1.6 %copy-done.3 = bf16[512,2048]{1,0:T(8,128)(2,1)S(1)} copy-done((bf16[512,2048]{1,0:T(8,128)(2,1)S(1)}, bf16[512,2048]{1,0:T(8,128)(2,1)}, u32[]{:S(2)}) %copy-start.3) | copy-done | bytes 2097176
  11.5 1.6 %copy-done.4 = bf16[512,2048]{1,0:T(8,128)(2,1)S(1)} copy-done((bf16[512,2048]{1,0:T(8,128)(2,1)S(1)}, bf16[512,2048]{1,0:T(8,128)(2,1)}, u32[]{:S(2)}) %copy-start.4) | copy-done | bytes 2097176
  13.1 0.9 copy-done.8
  14.0 0.9 copy-done.9
  14.9 0.9 copy-done.10
  15.8 0.9 copy-done.11
  16.7 1.1 blend_terms.1
  17.8 1.4 copy-done
  19.2 1.7 %all-to-all-done.mine = f32[16,72,128]{2,1,0:T(8,128)S(1)} async-done(((f32[16,72,128]{2,1,0:T(8,128)}), f32[16,72,128]{2,1,0:T(8,128)S(1)}, u32[]{:S(2)}, u32[]{:S(2)}) %all-to-all-start) | async-done | bytes 589856 | tf_op jit(solution)/shard_map/all_to_all | solution.py:28
  20.9 1.9 %collective-permute-start = (f32[16,72,128]{2,1,0:T(8,128)S(1)}, f32[16,72,128]{2,1,0:T(8,128)S(1)}, u32[]{:S(2)}, u32[]{:S(2)}) collective-permute-start(f32[16,72,128]{2,1,0:T(8,128)S(1)} %all-to-all-done.mine), channel_id=1, source_target_pairs={{0,8},{8,0},{16,24},{24,16},{32,40},{40,32},{48,56},{56,48},{64,72... | collective-permute-start | bytes 1769480 | tf_op jit(solution)/shard_map/ppermute | solution.py:24
  22.7 1.6 %collective-permute-done.other = f32[16,72,128]{2,1,0:T(8,128)S(1)} collective-permute-done((f32[16,72,128]{2,1,0:T(8,128)S(1)}, f32[16,72,128]{2,1,0:T(8,128)S(1)}, u32[]{:S(2)}, u32[]{:S(2)}) %collective-permute-start) | collective-permute-done | bytes 589856 | tf_op jit(solution)/shard_map/ppermute | solution.py:24
  24.4 1.7 %copy-done.1 = bf16[512,2304]{1,0:T(8,128)(2,1)S(1)} copy-done((bf16[512,2304]{1,0:T(8,128)(2,1)S(1)}, bf16[512,2304]{1,0:T(8,128)(2,1)}, u32[]{:S(2)}) %copy-start.1) | copy-done | bytes 2359320
  26.0 1.5 %partial_rows.1 = f32[8,192,128]{2,1,0:T(8,128)S(1)} custom-call(bf16[512,2304]{1,0:T(8,128)(2,1)S(1)} %get-tuple-element.35.high, bf16[512,2304]{1,0:T(8,128)(2,1)S(1)} %copy-done.1, f32[16,72,128]{2,1,0:T(8,128)S(1)} %all-to-all-done.mine, f32[16,72,128]{2,1,0:T(8,128)S(1)} %collective-permute-done.other), custom_call_target="tpu_custom_call" | custom-call | flops 905969664 | bytes 7000000 | tf_op jit(solution)/shard_map/partial_rows/pallas_call | solution.py:151
  27.5 30.4 %all_to_all.30.parts = f32[8,192,128]{2,1,0:T(8,128)S(1)} all-to-all(f32[8,192,128]{2,1,0:T(8,128)S(1)} %partial_rows.1), channel_id=1, replica_groups=mesh['fsdp'=32,'tensor'=8] {'tensor'}, dimensions={0} | all-to-all | bytes 1572864 | tf_op jit(solution)/shard_map/all_to_all | solution.py:32
  58.0 0.1 own_rows.1
  58.0 22.9 %all_to_all.31.rows = f32[8,192,128]{2,1,0:T(8,128)S(1)} all-to-all(f32[8,192,128]{2,1,0:T(8,128)S(1)} %own_rows.1), channel_id=1, replica_groups=mesh['fsdp'=32,'tensor'=8] {'tensor'}, dimensions={0} | all-to-all | bytes 1572864 | tf_op jit(solution)/shard_map/all_to_all | solution.py:32
  81.0 1.0 part_to_send.1
  82.0 4.2 %collective-permute-start.1 = (f32[11,128,128]{2,1,0:T(8,128)S(1)}, f32[11,128,128]{2,1,0:T(8,128)S(1)}, u32[]{:S(2)}, u32[]{:S(2)}) collective-permute-start(f32[11,128,128]{2,1,0:T(8,128)S(1)} %get-tuple-element.40), channel_id=1, source_target_pairs={{0,8},{8,0},{16,24},{24,16},{32,40},{40,32},{48,56},{56,48},{64,72... | collective-permute-start | bytes 2162696 | tf_op jit(solution)/shard_map/ppermute | solution.py:24
  86.2 1.4 part_to_keep.1.a
  87.6 0.5 collective-permute-done.1.b
  88.1 0.1 pair_sum.1
  88.1 16.6 %all_to_all.32.parts = f32[16,88,128]{2,1,0:T(8,128)S(1)} all-to-all(f32[16,88,128]{2,1,0:T(8,128)S(1)} %bitcast.4), channel_id=1, replica_groups={{0,16,32,48,64,80,96,112,128,144,160,176,192,208,224,240},{8,24,40,56,7..., dimensions={0} | all-to-all | bytes 1441792 | tf_op jit(solution)/shard_map/all_to_all | solution.py:28
  104.8 0.1 own_share.1
  104.9 15.0 %all_to_all.33 = f32[16,88,128]{2,1,0:T(8,128)S(1)} all-to-all(f32[16,88,128]{2,1,0:T(8,128)S(1)} %own_share.1), channel_id=1, replica_groups={{0,16,32,48,64,80,96,112,128,144,160,176,192,208,224,240},{8,24,40,56,7..., dimensions={0} | all-to-all | bytes 1441792 | tf_op jit(solution)/shard_map/all_to_all | solution.py:28
  119.9 3.0 %collective-permute-start.2 = (f32[11,128,128]{2,1,0:T(8,128)S(1)}, f32[11,128,128]{2,1,0:T(8,128)S(1)}, u32[]{:S(2)}, u32[]{:S(2)}) collective-permute-start(f32[11,128,128]{2,1,0:T(8,128)S(1)} %bitcast.2), channel_id=1, source_target_pairs={{0,8},{8,0},{16,24},{24,16},{32,40},{40,32},{48,56},{56,48},{64,72... | collective-permute-start | bytes 2162696 | tf_op jit(solution)/shard_map/ppermute | solution.py:24
  122.9 1.8 %collective-permute-done.2.other = f32[11,128,128]{2,1,0:T(8,128)S(1)} collective-permute-done((f32[11,128,128]{2,1,0:T(8,128)S(1)}, f32[11,128,128]{2,1,0:T(8,128)S(1)}, u32[]{:S(2)}, u32[]{:S(2)}) %collective-permute-start.2) | collective-permute-done | bytes 720928 | tf_op jit(solution)/shard_map/ppermute | solution.py:24
  124.7 8.2 %factor_and_rotate.1 = (f32[3,512,128]{2,1,0:T(8,128)S(1)}, bf16[128,2304]{1,0:T(8,128)(2,1)S(1)}, bf16[128,2304]{1,0:T(8,128)(2,1)S(1)}, f32[8,8,128]{2,1,0:T(8...) custom-call(f32[11,128,128]{2,1,0:T(8,128)S(1)} %bitcast.3, ...), custom_call_target="tpu_custom_call" | custom-call | tf_op jit(solution)/shard_map/factor_and_rotate/pallas_call | solution.py:332
  132.9 9.2 %all_to_all.34.squares = f32[8,8,128]{2,1,0:T(8,128)S(1)} all-to-all(f32[8,8,128]{2,1,0:T(8,128)S(1)} %get-tuple-element.44), channel_id=1, replica_groups=mesh['fsdp'=32,'tensor'=8] {'tensor'}, dimensions={0} | all-to-all | bytes 65536 | tf_op jit(solution)/shard_map/all_to_all | solution.py:32
  142.2 4.9 %updates.1 = (bf16[512,2048]{1,0:T(8,128)(2,1)}, bf16[512,128]{1,0:T(8,128)(2,1)}, bf16[512,128]{1,0:T(8,128)(2,1)}, bf16[512,2048]{1,0:T(8,128)(2,1)}, bf16[512...) custom-call(bf16[512,2304]{1,0:T(8,128)(2,1)S(1)} %get-tuple-element, ...), custom_call_target="tpu_custom_call" | custom-call | flops 1811939328 | bytes 16000000 | tf_op jit(solution)/shard_map/updates/pallas_call | solution.py:394
  (15 shorter events, 0.0 us)
Async XLA Ops:
  2.3 18.6 %all-to-all-start = ((f32[16,72,128]{2,1,0:T(8,128)}), f32[16,72,128]{2,1,0:T(8,128)S(1)}, u32[]{:S(2)}, u32[]{:S(2)}) async-start(f32[16,72,128]{2,1,0:T(8,128)} %repeat_bases.1), calls=%async_computation | async-start | bytes 1179648 | tf_op jit(solution)/shard_map/all_to_all | solution.py:28
  9.9 1.6 %copy-start.3 = (bf16[512,2048]{1,0:T(8,128)(2,1)S(1)}, bf16[512,2048]{1,0:T(8,128)(2,1)}, u32[]{:S(2)}) copy-start(bf16[512,2048]{1,0:T(8,128)(2,1)} %mq.1) | copy-start | bytes 6291460
  11.5 1.6 %copy-start.4 = (bf16[512,2048]{1,0:T(8,128)(2,1)S(1)}, bf16[512,2048]{1,0:T(8,128)(2,1)}, u32[]{:S(2)}) copy-start(bf16[512,2048]{1,0:T(8,128)(2,1)} %gq.1) | copy-start | bytes 6291460
  13.1 0.9 copy-start.8
  14.0 0.9 copy-start.9
  14.9 0.9 copy-start.10
  15.8 0.9 copy-start.11
  17.7 1.4 copy-start
  20.9 3.5 %collective-permute-start = (f32[16,72,128]{2,1,0:T(8,128)S(1)}, f32[16,72,128]{2,1,0:T(8,128)S(1)}, u32[]{:S(2)}, u32[]{:S(2)}) collective-permute-start(f32[16,72,128]{2,1,0:T(8,128)S(1)} %all-to-all-done.mine), channel_id=1, source_target_pairs={{0,8},{8,0},{16,24},{24,16},{32,40},{40,32},{48,56},{56,48},{64,72... | collective-permute-start | bytes 1769480 | tf_op jit(solution)/shard_map/ppermute | solution.py:24
  24.4 1.7 %copy-start.1 = (bf16[512,2304]{1,0:T(8,128)(2,1)S(1)}, bf16[512,2304]{1,0:T(8,128)(2,1)}, u32[]{:S(2)}) copy-start(bf16[512,2304]{1,0:T(8,128)(2,1)} %copy-done) | copy-start | bytes 7077892
  27.5 53.4 %copy-start.2 = (bf16[512,2304]{1,0:T(8,128)(2,1)S(1)}, bf16[512,2304]{1,0:T(8,128)(2,1)}, u32[]{:S(2)}) copy-start(bf16[512,2304]{1,0:T(8,128)(2,1)} %copy-done) | copy-start | bytes 7077892
  82.0 6.0 %collective-permute-start.1 = (f32[11,128,128]{2,1,0:T(8,128)S(1)}, f32[11,128,128]{2,1,0:T(8,128)S(1)}, u32[]{:S(2)}, u32[]{:S(2)}) collective-permute-start(f32[11,128,128]{2,1,0:T(8,128)S(1)} %get-tuple-element.40), channel_id=1, source_target_pairs={{0,8},{8,0},{16,24},{24,16},{32,40},{40,32},{48,56},{56,48},{64,72... | collective-permute-start | bytes 2162696 | tf_op jit(solution)/shard_map/ppermute | solution.py:24
  104.8 37.3 %copy-start.5 = (bf16[512,2048]{1,0:T(8,128)(2,1)S(1)}, bf16[512,2048]{1,0:T(8,128)(2,1)}, u32[]{:S(2)}) copy-start(bf16[512,2048]{1,0:T(8,128)(2,1)} %wq.1) | copy-start | bytes 6291460
  104.8 37.3 %copy-start.6 = (bf16[512,128]{1,0:T(8,128)(2,1)S(1)}, bf16[512,128]{1,0:T(8,128)(2,1)}, u32[]{:S(2)}) copy-start(bf16[512,128]{1,0:T(8,128)(2,1)} %wk.1) | copy-start | bytes 393220
  104.9 37.3 %copy-start.7 = (bf16[512,128]{1,0:T(8,128)(2,1)S(1)}, bf16[512,128]{1,0:T(8,128)(2,1)}, u32[]{:S(2)}) copy-start(bf16[512,128]{1,0:T(8,128)(2,1)} %wv.1) | copy-start | bytes 393220
  119.9 4.8 %collective-permute-start.2 = (f32[11,128,128]{2,1,0:T(8,128)S(1)}, f32[11,128,128]{2,1,0:T(8,128)S(1)}, u32[]{:S(2)}, u32[]{:S(2)}) collective-permute-start(f32[11,128,128]{2,1,0:T(8,128)S(1)} %bitcast.2), channel_id=1, source_target_pairs={{0,8},{8,0},{16,24},{24,16},{32,40},{40,32},{48,56},{56,48},{64,72... | collective-permute-start | bytes 2162696 | tf_op jit(solution)/shard_map/ppermute | solution.py:24

commit v5 on v4

--- a/solution.py
+++ b/solution.py
@@ -14,9 +14,9 @@
 BF16 = jnp.bfloat16
 PLANE = [[2 * i + c for i in range(16)] for c in range(2)]
 SIBLING = [(i, i ^ 1) for i in range(32)]
-STEPS = 4
-BLOCKS = 22
-HALF = BLOCKS // 2
+STEPS = 2
+HALF = 9
+SUMMED = HALF + 2
 VMEM_LIMIT = 24 * 1024 * 1024
 
 
@@ -94,21 +94,9 @@
     )(*operands)
 
 
-def repeat_bases_kernel(q, k, v, out):
+def repeat_kernel(block, out):
     for i in range(out.shape[0]):
-        out[i, :64] = q[...]
-        out[i, 64:68] = k[...]
-        out[i, 68:72] = v[...]
-
-
-def repeat_bases(bases):
-    return pl.pallas_call(
-        repeat_bases_kernel,
-        in_specs=[VMEM] * 3,
-        out_specs=VMEM,
-        out_shape=jax.ShapeDtypeStruct((16, 72, RANK), F32),
-        name="repeat_bases",
-    )(*bases)
+        out[i] = block[...]
 
 
 def repeat_total_kernel(parts, out):
@@ -162,50 +150,74 @@
     )(high, low, mine, other)
 
 
-def half_of_right(half, high, low, projected, lhs, out):
+def grid_of_indices():
+    row = lax.broadcasted_iota(jnp.int32, (RANK, RANK), 0)
+    return row, lax.broadcasted_iota(jnp.int32, (RANK, RANK), 1)
+
+
+def pack_symmetric(a, b, c):
+    row, col = grid_of_indices()
+    diagonal = jnp.sum(jnp.where(row == col, b, 0.0), axis=0, keepdims=True)
+    first = jnp.where(row >= col, a, b.T)
+    upper = jnp.where((row == 0) & (col > 0), diagonal, 0.0)
+    upper = jnp.where((row == 1) & (col == RANK - 1), b[:1, :1], upper)
+    return first, jnp.where(row >= col, c, upper)
+
+
+def unpack_symmetric(first, second):
+    row, col = grid_of_indices()
+    turned = first.T
+    diagonal = jnp.where(col[:1] == 0, second[1:2, RANK - 1 :], second[:1])
+    a = jnp.where(row >= col, first, turned)
+    b = jnp.where(row < col, first, jnp.where(row > col, turned, diagonal))
+    return a, b, jnp.where(row >= col, second, second.T)
+
+
+def half_of_right(half, high, low, lhs, out):
     def times(m, lo, hi):
         both = dot(lhs[m], high[:, lo:hi])
         return both[:RANK] + both[RANK:] + dot(lhs[m, :RANK], low[:, lo:hi])
 
-    first = 0 if half == 0 else HALF
-    for lo in range(first, min(first + HALF, 16), 4):
-        hi = min(lo + 4, first + HALF, 16)
+    first = HALF * half
+    for lo in range(first, min(first + HALF, 16), 3):
+        hi = min(lo + 3, first + HALF, 16)
         right = times(0, RANK * lo, RANK * hi)
         for i in range(hi - lo):
             out[lo - first + i] = right[:, RANK * i : RANK * i + RANK]
     if half == 1:
         out[16 - HALF] = times(1, 2048, 2176)
         out[17 - HALF] = times(2, 2176, 2304)
-        for m in range(3):
-            p = projected[m]
-            out[18 - HALF + m] = jnp.dot(p.T, p, precision=HIGHEST, preferred_element_type=F32)
-        out[21 - HALF] = jnp.zeros((RANK, RANK), F32)
-
-
-def send_kernel(high, low, rows, send, projected, lhs):
+
+
+def send_kernel(high, low, rows, send, projected, lhs, grams):
     for d in range(8):
         for m in range(3):
             projected[m, 64 * d : 64 * d + 64] = rows[d, 64 * m : 64 * m + 64]
+    squares = []
     for m in range(3):
-        h, l = split(projected[m].T)
+        p = projected[m]
+        turned = p.T
+        h, l = split(turned)
         lhs[m, :RANK] = h
         lhs[m, RANK:] = l
+        squares.append(jnp.dot(turned, p, precision=HIGHEST, preferred_element_type=F32))
     core = lax.rem(lax.axis_index("fsdp"), 2)
     for half in range(2):
-        pl.when(core != half)(
-            functools.partial(half_of_right, half, high, low, projected, lhs, send)
-        )
-
-
-def keep_kernel(high, low, projected, lhs, keep):
+        pl.when(core != half)(functools.partial(half_of_right, half, high, low, lhs, send))
+    for i, block in enumerate(pack_symmetric(*squares)):
+        send[HALF + i] = block
+        grams[i] = block
+
+
+def keep_kernel(high, low, lhs, grams, keep):
     core = lax.rem(lax.axis_index("fsdp"), 2)
     for half in range(2):
-        pl.when(core == half)(
-            functools.partial(half_of_right, half, high, low, projected, lhs, keep)
-        )
-
-
-HALF_SHAPE = jax.ShapeDtypeStruct((HALF, RANK, RANK), F32)
+        pl.when(core == half)(functools.partial(half_of_right, half, high, low, lhs, keep))
+    for i in range(2):
+        keep[HALF + i] = grams[i]
+
+
+HALF_SHAPE = jax.ShapeDtypeStruct((SUMMED, RANK, RANK), F32)
 HALF_COST = pl.CostEstimate(
     flops=3 * 512 * 2304 * RANK, bytes_accessed=5_000_000, transcendentals=0
 )
@@ -215,11 +227,12 @@
     return pl.pallas_call(
         send_kernel,
         in_specs=[VMEM] * 3,
-        out_specs=[VMEM] * 3,
+        out_specs=[VMEM] * 4,
         out_shape=[
             HALF_SHAPE,
             jax.ShapeDtypeStruct((3, 512, RANK), F32),
             jax.ShapeDtypeStruct((3, 2 * RANK, 512), BF16),
+            jax.ShapeDtypeStruct((2, RANK, RANK), F32),
         ],
         compiler_params=pltpu.CompilerParams(vmem_limit_bytes=VMEM_LIMIT),
         cost_estimate=HALF_COST,
@@ -227,7 +240,7 @@
     )(high, low, rows)
 
 
-def part_to_keep(high, low, projected, lhs):
+def part_to_keep(high, low, lhs, grams):
     return pl.pallas_call(
         keep_kernel,
         in_specs=[VMEM] * 4,
@@ -236,7 +249,7 @@
         compiler_params=pltpu.CompilerParams(vmem_limit_bytes=VMEM_LIMIT),
         cost_estimate=HALF_COST,
         name="part_to_keep",
-    )(high, low, projected, lhs)
+    )(high, low, lhs, grams)
 
 
 def invert(grams):
@@ -286,41 +299,61 @@
     return [jnp.concatenate(d, axis=0) for d in done]
 
 
-def factor_kernel(
-    mine, other, projected, ortho, right_high, right_low, squares, sq, sk, sv, turned
-):
+def factor_kernel(mine, projected, inverses, ortho):
+    for m, inverse in enumerate(invert(unpack_symmetric(mine[HALF], mine[HALF + 1]))):
+        inverses[m] = inverse
+        ih, il = split(inverse)
+        ph, plow = split(projected[m])
+        ortho[m] = dot(ph, ih, (1, 1)) + dot(ph, il, (1, 1)) + dot(plow, ih, (1, 1))
+
+
+def factor(mine, projected):
+    return pl.pallas_call(
+        factor_kernel,
+        in_specs=[VMEM] * 2,
+        out_specs=[VMEM] * 2,
+        out_shape=[
+            jax.ShapeDtypeStruct((3, RANK, RANK), F32),
+            jax.ShapeDtypeStruct((3, 512, RANK), F32),
+        ],
+        compiler_params=pltpu.CompilerParams(vmem_limit_bytes=VMEM_LIMIT),
+        cost_estimate=pl.CostEstimate(
+            flops=6_000_000_000, bytes_accessed=3_000_000, transcendentals=0
+        ),
+        name="factor",
+    )(mine, projected)
+
+
+def rotate_kernel(mine, other, inverses, right_high, right_low, squares, sq, sk, sv, turned):
     fsdp = lax.axis_index("fsdp")
     core = lax.rem(fsdp, 2)
 
     def block(j):
         return jnp.where(core == j // HALF, mine[j % HALF], other[j % HALF])
 
-    inverses = invert([block(18 + m) for m in range(3)])
-    for m, blocks in enumerate((range(16), (16,), (17,))):
-        ih, il = split(inverses[m])
-        ph, plow = split(projected[m])
-        ortho[m] = dot(ph, ih, (1, 1)) + dot(ph, il, (1, 1)) + dot(plow, ih, (1, 1))
-        stacked = jnp.concatenate([ih, il], axis=0)
-        total = jnp.zeros((RANK, RANK), F32)
-        for j in blocks:
-            zh, zl = split(block(j))
-            both = dot(stacked, zh)
-            right = both[:RANK] + both[RANK:] + dot(ih, zl)
-            total += right * right
-            high, low = split(right)
-            right_high[:, RANK * j : RANK * j + RANK] = high
-            right_low[:, RANK * j : RANK * j + RANK] = low
-            if m == 0:
-                @pl.when(lax.div(fsdp, 2) == j)
-                def _():
-                    turned[0] = right.T
-            else:
-                turned[m] = right.T
-        sums = jnp.sum(total.T, axis=0, keepdims=True)
+    groups = ((0, range(0, 4)), (0, range(4, 8)), (0, range(8, 12)), (0, range(12, 16)))
+    terms = [split(inverses[m]) for m in range(3)]
+    stacked = [jnp.concatenate(pair, axis=0) for pair in terms]
+    totals = [jnp.zeros((RANK, RANK), F32)] * 3
+    for m, blocks in groups + ((1, (16,)), (2, (17,))):
+        zh, zl = split(jnp.concatenate([block(j) for j in blocks], axis=1))
+        both = dot(stacked[m], zh)
+        right = both[:RANK] + both[RANK:] + dot(terms[m][0], zl)
+        span = slice(RANK * blocks[0], RANK * blocks[-1] + RANK)
+        right_high[:, span], right_low[:, span] = split(right)
+        for i, j in enumerate(blocks):
+            piece = right[:, RANK * i : RANK * i + RANK]
+            totals[m] += piece * piece
+            turned[j] = piece
+    for m in range(3):
+        sums = jnp.sum(totals[m].T, axis=0, keepdims=True)
         for d in range(8):
             squares[d, m : m + 1, :] = sums
     for d in range(8):
         squares[d, 3:, :] = jnp.zeros((5, RANK), F32)
+    turned[0] = turned[lax.div(fsdp, 2)].T
+    turned[1] = turned[16].T
+    turned[2] = turned[17].T
     odd = lax.rem(fsdp, 2)
     sq[...] = turned[0, pl.ds(pl.multiple_of(odd * 64, 64), 64)]
     for m, out in ((1, sk), (2, sv)):
@@ -328,13 +361,12 @@
         out[...] = jnp.where(odd == 0, tile[:4], tile[4:])
 
 
-def factor_and_rotate(mine, other, projected):
-    return pl.pallas_call(
-        factor_kernel,
-        in_specs=[VMEM, VMEM, VMEM],
-        out_specs=[VMEM] * 7,
+def rotate(mine, other, inverses):
+    return pl.pallas_call(
+        rotate_kernel,
+        in_specs=[VMEM] * 3,
+        out_specs=[VMEM] * 6,
         out_shape=[
-            jax.ShapeDtypeStruct((3, 512, RANK), F32),
             jax.ShapeDtypeStruct((RANK, 2304), BF16),
             jax.ShapeDtypeStruct((RANK, 2304), BF16),
             jax.ShapeDtypeStruct((8, 8, RANK), F32),
@@ -342,10 +374,10 @@
             jax.ShapeDtypeStruct((4, RANK), F32),
             jax.ShapeDtypeStruct((4, RANK), F32),
         ],
-        scratch_shapes=[pltpu.VMEM((3, RANK, RANK), F32)],
-        compiler_params=pltpu.CompilerParams(vmem_limit_bytes=VMEM_LIMIT),
-        name="factor_and_rotate",
-    )(mine, other, projected)
+        scratch_shapes=[pltpu.VMEM((18, RANK, RANK), F32)],
+        compiler_params=pltpu.CompilerParams(vmem_limit_bytes=VMEM_LIMIT),
+        name="rotate",
+    )(mine, other, inverses)
 
 
 def update_kernel(
@@ -355,12 +387,17 @@
     step = pl.program_id(0)
 
     def new(m, span, weight, moment_out, weight_out):
-        right = rh[:, span]
-        product = dot(lhs[m], jnp.concatenate([right, right], axis=0))
-        product += dot(lhs[m, :, :RANK], rl[:, span])
-        blend = high[:, span].astype(F32) + low[:, span].astype(F32)
-        moment_out[...] = (blend - product[:512]).astype(BF16)
-        weight_out[...] = (weight.astype(F32) - product[512:]).astype(BF16)
+        right = jnp.concatenate([rh[:, span], rh[:, span]], axis=0)
+        low_right = rl[:, span]
+
+        def product(at):
+            return dot(lhs[m, at : at + 256], right) + dot(lhs[m, at : at + 256, :RANK], low_right)
+
+        for at in (0, 256):
+            part = slice(at, at + 256)
+            blend = high[part, span].astype(F32) + low[part, span].astype(F32)
+            moment_out[part] = (blend - product(at)).astype(BF16)
+            weight_out[part] = (weight[part].astype(F32) - product(512 + at)).astype(BF16)
 
     @pl.when(step == 0)
     def _():
@@ -429,20 +466,24 @@
     ]
 
     high, low = blend_terms(moments, grads)
-    mine = plane_exchange(repeat_bases((basis_q, basis_k, basis_v)))
+    bases = jnp.concatenate([basis_q, basis_k, basis_v], axis=0)
+    bases = small_kernel(repeat_kernel, (16,) + bases.shape, "repeat_bases", bases)
+    mine = plane_exchange(bases)
     mine, high, low = lax.optimization_barrier((mine, high, low))
     chunks = partial_rows(high, low, mine, swap_core(mine))
     own = small_kernel(repeat_total_kernel, chunks.shape, "own_rows", tensor_exchange(chunks))
     rows = tensor_exchange(own)
-    send, projected, lhs = part_to_send(high, low, rows)
+    send, projected, lhs, grams = part_to_send(high, low, rows)
     sent = swap_core(send)
-    keep = part_to_keep(high, low, projected, lhs)
-
-    paired = small_kernel(pair_kernel, (HALF, RANK, RANK), "pair_sum", keep, sent)
+    keep = part_to_keep(high, low, lhs, grams)
+
+    paired = small_kernel(pair_kernel, send.shape, "pair_sum", keep, sent)
     share = plane_exchange(paired.reshape(16, 88, RANK))
     share = small_kernel(repeat_total_kernel, (16, 88, RANK), "own_share", share)
-    mine = plane_exchange(share).reshape(HALF, RANK, RANK)
-    ortho, rh, rl, squares, *shares = factor_and_rotate(mine, swap_core(mine), projected)
+    mine = plane_exchange(share).reshape(send.shape)
+    other = swap_core(mine)
+    inverses, ortho = factor(mine, projected)
+    rh, rl, squares, *shares = rotate(mine, other, inverses)
     squares = tensor_exchange(squares)
     out = updates(factors, high, low, weights, ortho, rh, rl, squares, shares)
     return tuple(out[3 * j + i] for i in range(3) for j in (1, 0, 2))

time: 148 us -> 143 us (0.966)
  Pallas kernels: 19.9 us -> 16.8 us
    pallas_call x3, Pallas kernels: 10.9 us -> 7.66 us  [the longest x1 5.05 us: factor(): pl.pallas_call(factor_kernel, in_specs=[VMEM] * 2, out_specs=[VMEM] * 2,...]
  transfers between devices with their start and end apart: 4 -> 4, of which waited for: 4 -> 3; matrix products, arithmetic and copies ran while one was open for 0% -> 0% of each run, Pallas kernels for 2% -> 5%
where the time goes in v5:
time: 143 us
  blocking collectives  94.1 us (66%)
  Pallas kernels  16.8 us (12%)
  starting transfers between devices  16.2 us (11%)
  local copies, waits for them, and re-layouts  9.9 us (7%)
  waiting for transfers between devices  4.26 us (3%)
    all_to_all x3, blocking collectives, tensor_exchange(): return lax.all_to_all(x, 'tensor', 0, 0, tiled=True)  62.6 us
    all_to_all x2, blocking collectives, plane_exchange(): return lax.all_to_all(x, 'fsdp', 0, 0, tiled=True, axis_index_groups=PLANE)  31.5 us
    unnamed x24, local copies, waits for them, and re-layouts  9.9 us
    ppermute x3, starting transfers between devices, swap_core(): return lax.ppermute(x, 'fsdp', SIBLING)  8.59 us
    all_to_all x1, starting transfers between devices, plane_exchange(): return lax.all_to_all(x, 'fsdp', 0, 0, tiled=True, axis_index_groups=PLANE)  7.58 us
    pallas_call x1, Pallas kernels, factor(): pl.pallas_call(factor_kernel, in_specs=[VMEM] * 2, out_specs=[VMEM] * 2,...  5.05 us
    pallas_call x1, Pallas kernels, updates(): pl.pallas_call(functools.partial(update_kernel, factors), grid=(STEPS,),...  4.65 us
  transfers between devices with their start and end apart: 4, of which 3 were waited for; matrix products, arithmetic and copies ran while one was open for 0% of the time, Pallas kernels for 5%

profile of v5, /device:TPU:1, one launch (start us, length us, event | category | flops | bytes accessed | tf_op | source)
XLA Modules:
  0.0 142.8 jit_solution(13402523001918915814)
XLA Ops:
  0.6 0.8 pad_maximum_fusion.block
  1.4 0.9 repeat_bases.1
  2.3 7.6 %all-to-all-start = ((f32[16,72,128]{2,1,0:T(8,128)}), f32[16,72,128]{2,1,0:T(8,128)S(1)}, u32[]{:S(2)}, u32[]{:S(2)}) async-start(f32[16,72,128]{2,1,0:T(8,128)} %repeat_bases.1), calls=%async_computation | async-start | bytes 1179648 | tf_op jit(solution)/shard_map/all_to_all | solution.py:28
  9.9 1.6 %copy-done.3 = bf16[512,2048]{1,0:T(8,128)(2,1)S(1)} copy-done((bf16[512,2048]{1,0:T(8,128)(2,1)S(1)}, bf16[512,2048]{1,0:T(8,128)(2,1)}, u32[]{:S(2)}) %copy-start.3) | copy-done | bytes 2097176
  11.5 1.6 %copy-done.4 = bf16[512,2048]{1,0:T(8,128)(2,1)S(1)} copy-done((bf16[512,2048]{1,0:T(8,128)(2,1)S(1)}, bf16[512,2048]{1,0:T(8,128)(2,1)}, u32[]{:S(2)}) %copy-start.4) | copy-done | bytes 2097176
  13.1 0.9 copy-done.8
  14.0 0.9 copy-done.9
  14.9 0.9 copy-done.10
  15.8 0.9 copy-done.11
  16.7 1.1 blend_terms.1
  17.8 1.4 copy-done
  19.2 1.7 %all-to-all-done.mine = f32[16,72,128]{2,1,0:T(8,128)S(1)} async-done(((f32[16,72,128]{2,1,0:T(8,128)}), f32[16,72,128]{2,1,0:T(8,128)S(1)}, u32[]{:S(2)}, u32[]{:S(2)}) %all-to-all-start) | async-done | bytes 589856 | tf_op jit(solution)/shard_map/all_to_all | solution.py:28
  20.9 1.9 %collective-permute-start = (f32[16,72,128]{2,1,0:T(8,128)S(1)}, f32[16,72,128]{2,1,0:T(8,128)S(1)}, u32[]{:S(2)}, u32[]{:S(2)}) collective-permute-start(f32[16,72,128]{2,1,0:T(8,128)S(1)} %all-to-all-done.mine), channel_id=1, source_target_pairs={{0,8},{8,0},{16,24},{24,16},{32,40},{40,32},{48,56},{56,48},{64,72... | collective-permute-start | bytes 1769480 | tf_op jit(solution)/shard_map/ppermute | solution.py:24
  22.7 1.6 %collective-permute-done.other = f32[16,72,128]{2,1,0:T(8,128)S(1)} collective-permute-done((f32[16,72,128]{2,1,0:T(8,128)S(1)}, f32[16,72,128]{2,1,0:T(8,128)S(1)}, u32[]{:S(2)}, u32[]{:S(2)}) %collective-permute-start) | collective-permute-done | bytes 589856 | tf_op jit(solution)/shard_map/ppermute | solution.py:24
  24.4 1.7 %copy-done.1 = bf16[512,2304]{1,0:T(8,128)(2,1)S(1)} copy-done((bf16[512,2304]{1,0:T(8,128)(2,1)S(1)}, bf16[512,2304]{1,0:T(8,128)(2,1)}, u32[]{:S(2)}) %copy-start.1) | copy-done | bytes 2359320
  26.0 1.5 %partial_rows.1 = f32[8,192,128]{2,1,0:T(8,128)S(1)} custom-call(bf16[512,2304]{1,0:T(8,128)(2,1)S(1)} %get-tuple-element.37.high, bf16[512,2304]{1,0:T(8,128)(2,1)S(1)} %copy-done.1, f32[16,72,128]{2,1,0:T(8,128)S(1)} %all-to-all-done.mine, f32[16,72,128]{2,1,0:T(8,128)S(1)} %collective-permute-done.other), custom_call_target="tpu_custom_call" | custom-call | flops 905969664 | bytes 7000000 | tf_op jit(solution)/shard_map/partial_rows/pallas_call | solution.py:139
  27.5 30.4 %all_to_all.30.parts = f32[8,192,128]{2,1,0:T(8,128)S(1)} all-to-all(f32[8,192,128]{2,1,0:T(8,128)S(1)} %partial_rows.1), channel_id=1, replica_groups=mesh['fsdp'=32,'tensor'=8] {'tensor'}, dimensions={0} | all-to-all | bytes 1572864 | tf_op jit(solution)/shard_map/all_to_all | solution.py:32
  58.0 0.1 own_rows.1
  58.0 22.9 %all_to_all.31.rows = f32[8,192,128]{2,1,0:T(8,128)S(1)} all-to-all(f32[8,192,128]{2,1,0:T(8,128)S(1)} %own_rows.1), channel_id=1, replica_groups=mesh['fsdp'=32,'tensor'=8] {'tensor'}, dimensions={0} | all-to-all | bytes 1572864 | tf_op jit(solution)/shard_map/all_to_all | solution.py:32
  81.0 1.8 %part_to_send.1 = (f32[11,128,128]{2,1,0:T(8,128)S(1)}, f32[3,512,128]{2,1,0:T(8,128)S(1)}, bf16[3,256,512]{2,1,0:T(8,128)(2,1)S(1)}, f32[2,128,128]{2,1,0:T(8,128)S(1)}) custom-call(bf16[512,2304]{1,0:T(8,128)(2,1)S(1)} %get-tuple-element.37.high, bf16[512,2304]{1,0:T(8,128)(2,1)S(1)} %copy-done.2, f32[8,192,128]{2,1,0:T(8,128)S(1)} %all_to_all.31.rows), custom_call_target="tpu_custom_call" | custom-call | flops 452984832 | bytes 5000000 | tf_op jit(solution)/shard_map/part_to_send/pallas_call | solution.py:227
  82.7 3.8 %collective-permute-start.1 = (f32[11,128,128]{2,1,0:T(8,128)S(1)}, f32[11,128,128]{2,1,0:T(8,128)S(1)}, u32[]{:S(2)}, u32[]{:S(2)}) collective-permute-start(f32[11,128,128]{2,1,0:T(8,128)S(1)} %get-tuple-element.42), channel_id=1, source_target_pairs={{0,8},{8,0},{16,24},{24,16},{32,40},{40,32},{48,56},{56,48},{64,72... | collective-permute-start | bytes 2162696 | tf_op jit(solution)/shard_map/ppermute | solution.py:24
  86.5 0.9 part_to_keep.1.a
  87.4 0.9 collective-permute-done.1.b
  88.3 0.1 pair_sum.1
  88.4 16.6 %all_to_all.32.parts = f32[16,88,128]{2,1,0:T(8,128)S(1)} all-to-all(f32[16,88,128]{2,1,0:T(8,128)S(1)} %bitcast.5), channel_id=1, replica_groups={{0,16,32,48,64,80,96,112,128,144,160,176,192,208,224,240},{8,24,40,56,7..., dimensions={0} | all-to-all | bytes 1441792 | tf_op jit(solution)/shard_map/all_to_all | solution.py:28
  105.0 0.1 own_share.1
  105.1 14.9 %all_to_all.33 = f32[16,88,128]{2,1,0:T(8,128)S(1)} all-to-all(f32[16,88,128]{2,1,0:T(8,128)S(1)} %own_share.1), channel_id=1, replica_groups={{0,16,32,48,64,80,96,112,128,144,160,176,192,208,224,240},{8,24,40,56,7..., dimensions={0} | all-to-all | bytes 1441792 | tf_op jit(solution)/shard_map/all_to_all | solution.py:28
  120.0 3.0 %collective-permute-start.2 = (f32[11,128,128]{2,1,0:T(8,128)S(1)}, f32[11,128,128]{2,1,0:T(8,128)S(1)}, u32[]{:S(2)}, u32[]{:S(2)}) collective-permute-start(f32[11,128,128]{2,1,0:T(8,128)S(1)} %bitcast.2), channel_id=1, source_target_pairs={{0,8},{8,0},{16,24},{24,16},{32,40},{40,32},{48,56},{56,48},{64,72... | collective-permute-start | bytes 2162696 | tf_op jit(solution)/shard_map/ppermute | solution.py:24
  123.0 5.1 %factor.1 = (f32[3,128,128]{2,1,0:T(8,128)S(1)}, f32[3,512,128]{2,1,0:T(8,128)S(1)}) custom-call(f32[11,128,128]{2,1,0:T(8,128)S(1)} %bitcast.3, f32[3,512,128]{2,1,0:T(8,128)S(1)} %get-tuple-element.43.projected), custom_call_target="tpu_custom_call" | custom-call | flops 6000000000 | bytes 3000000 | tf_op jit(solution)/shard_map/factor/pallas_call | solution.py:311
  128.0 0.8 rotate.1
  128.9 9.2 %all_to_all.34.squares = f32[8,8,128]{2,1,0:T(8,128)S(1)} all-to-all(f32[8,8,128]{2,1,0:T(8,128)S(1)} %get-tuple-element.48), channel_id=1, replica_groups=mesh['fsdp'=32,'tensor'=8] {'tensor'}, dimensions={0} | all-to-all | bytes 65536 | tf_op jit(solution)/shard_map/all_to_all | solution.py:32
  138.1 4.6 %updates.1 = (bf16[512,2048]{1,0:T(8,128)(2,1)}, bf16[512,128]{1,0:T(8,128)(2,1)}, bf16[512,128]{1,0:T(8,128)(2,1)}, bf16[512,2048]{1,0:T(8,128)(2,1)}, bf16[512...) custom-call(bf16[512,2304]{1,0:T(8,128)(2,1)S(1)} %get-tuple-element, ...), custom_call_target="tpu_custom_call" | custom-call | flops 1811939328 | bytes 16000000 | tf_op jit(solution)/shard_map/updates/pallas_call | solution.py:431
  (17 shorter events, 0.0 us)
Async XLA Ops:
  2.3 18.6 %all-to-all-start = ((f32[16,72,128]{2,1,0:T(8,128)}), f32[16,72,128]{2,1,0:T(8,128)S(1)}, u32[]{:S(2)}, u32[]{:S(2)}) async-start(f32[16,72,128]{2,1,0:T(8,128)} %repeat_bases.1), calls=%async_computation | async-start | bytes 1179648 | tf_op jit(solution)/shard_map/all_to_all | solution.py:28
  9.9 1.6 %copy-start.3 = (bf16[512,2048]{1,0:T(8,128)(2,1)S(1)}, bf16[512,2048]{1,0:T(8,128)(2,1)}, u32[]{:S(2)}) copy-start(bf16[512,2048]{1,0:T(8,128)(2,1)} %mq.1) | copy-start | bytes 6291460
  11.5 1.6 %copy-start.4 = (bf16[512,2048]{1,0:T(8,128)(2,1)S(1)}, bf16[512,2048]{1,0:T(8,128)(2,1)}, u32[]{:S(2)}) copy-start(bf16[512,2048]{1,0:T(8,128)(2,1)} %gq.1) | copy-start | bytes 6291460
  13.1 0.9 copy-start.8
  14.0 0.9 copy-start.9
  14.9 0.9 copy-start.10
  15.8 0.9 copy-start.11
  17.8 1.4 %copy-start = (bf16[512,2304]{1,0:T(8,128)(2,1)}, bf16[512,2304]{1,0:T(8,128)(2,1)S(1)}, u32[]{:S(2)}) copy-start(bf16[512,2304]{1,0:T(8,128)(2,1)S(1)} %get-tuple-element.38.low) | copy-start | bytes 7077892
  20.9 3.5 %collective-permute-start = (f32[16,72,128]{2,1,0:T(8,128)S(1)}, f32[16,72,128]{2,1,0:T(8,128)S(1)}, u32[]{:S(2)}, u32[]{:S(2)}) collective-permute-start(f32[16,72,128]{2,1,0:T(8,128)S(1)} %all-to-all-done.mine), channel_id=1, source_target_pairs={{0,8},{8,0},{16,24},{24,16},{32,40},{40,32},{48,56},{56,48},{64,72... | collective-permute-start | bytes 1769480 | tf_op jit(solution)/shard_map/ppermute | solution.py:24
  24.4 1.7 %copy-start.1 = (bf16[512,2304]{1,0:T(8,128)(2,1)S(1)}, bf16[512,2304]{1,0:T(8,128)(2,1)}, u32[]{:S(2)}) copy-start(bf16[512,2304]{1,0:T(8,128)(2,1)} %copy-done) | copy-start | bytes 7077892
  27.5 53.4 %copy-start.2 = (bf16[512,2304]{1,0:T(8,128)(2,1)S(1)}, bf16[512,2304]{1,0:T(8,128)(2,1)}, u32[]{:S(2)}) copy-start(bf16[512,2304]{1,0:T(8,128)(2,1)} %copy-done) | copy-start | bytes 7077892
  82.7 5.6 %collective-permute-start.1 = (f32[11,128,128]{2,1,0:T(8,128)S(1)}, f32[11,128,128]{2,1,0:T(8,128)S(1)}, u32[]{:S(2)}, u32[]{:S(2)}) collective-permute-start(f32[11,128,128]{2,1,0:T(8,128)S(1)} %get-tuple-element.42), channel_id=1, source_target_pairs={{0,8},{8,0},{16,24},{24,16},{32,40},{40,32},{48,56},{56,48},{64,72... | collective-permute-start | bytes 2162696 | tf_op jit(solution)/shard_map/ppermute | solution.py:24
  120.0 8.0 %collective-permute-start.2 = (f32[11,128,128]{2,1,0:T(8,128)S(1)}, f32[11,128,128]{2,1,0:T(8,128)S(1)}, u32[]{:S(2)}, u32[]{:S(2)}) collective-permute-start(f32[11,128,128]{2,1,0:T(8,128)S(1)} %bitcast.2), channel_id=1, source_target_pairs={{0,8},{8,0},{16,24},{24,16},{32,40},{40,32},{48,56},{56,48},{64,72... | collective-permute-start | bytes 2162696 | tf_op jit(solution)/shard_map/ppermute | solution.py:24
  123.0 15.1 %copy-start.5 = (bf16[512,2048]{1,0:T(8,128)(2,1)S(1)}, bf16[512,2048]{1,0:T(8,128)(2,1)}, u32[]{:S(2)}) copy-start(bf16[512,2048]{1,0:T(8,128)(2,1)} %wq.1) | copy-start | bytes 6291460
  123.0 15.1 %copy-start.6 = (bf16[512,128]{1,0:T(8,128)(2,1)S(1)}, bf16[512,128]{1,0:T(8,128)(2,1)}, u32[]{:S(2)}) copy-start(bf16[512,128]{1,0:T(8,128)(2,1)} %wk.1) | copy-start | bytes 393220
  123.0 15.1 %copy-start.7 = (bf16[512,128]{1,0:T(8,128)(2,1)S(1)}, bf16[512,128]{1,0:T(8,128)(2,1)}, u32[]{:S(2)}) copy-start(bf16[512,128]{1,0:T(8,128)(2,1)} %wv.1) | copy-start | bytes 393220

commit v6 on v5

--- a/solution.py
+++ b/solution.py
@@ -18,6 +18,8 @@
 HALF = 9
 SUMMED = HALF + 2
 VMEM_LIMIT = 24 * 1024 * 1024
+EARLY_LIMIT = 60 * 1024 * 1024
+BLEND_LIMIT = 50 * 1024 * 1024
 
 
 def swap_core(x):
@@ -57,30 +59,81 @@
 VMEM = pl.BlockSpec(memory_space=pltpu.VMEM)
 
 
-def blend_kernel(mq, gq, mk, gk, mv, gv, high, low):
-    for at, moment, grad in ((0, mq, gq), (2048, mk, gk), (2048 + RANK, mv, gv)):
-        h, l = split(moment[...].astype(F32) + grad[...].astype(F32))
-        span = slice(at, at + h.shape[1])
-        high[:, span] = h
-        low[:, span] = l
-
-
-def blend_terms(moments, grads):
+SPLITS = ((0, 2048), (2048, 2176), (2176, 2304))
+TERMS = [jax.ShapeDtypeStruct((512, 2304), BF16)] * 2
+
+
+def early_blend_kernel(
+    mq, gq, mk, gk, mv, gv, high_out, low_out, moments, grads, high, low, sems, out_sems
+):
+    @pl.when(lax.rem(lax.axis_index("fsdp"), 2) == 0)
+    def _():
+        fetches = []
+        for i, ((lo, hi), moment, grad) in enumerate(zip(SPLITS, (mq, mk, mv), (gq, gk, gv))):
+            fetches.append(pltpu.make_async_copy(moment, moments.at[:, lo:hi], sems.at[i, 0]))
+            fetches.append(pltpu.make_async_copy(grad, grads.at[:, lo:hi], sems.at[i, 1]))
+        for copy in fetches:
+            copy.start()
+        for copy in fetches:
+            copy.wait()
+        for at in range(0, 512, 64):
+            part = slice(at, at + 64)
+            high[part], low[part] = split(moments[part].astype(F32) + grads[part].astype(F32))
+        stores = [
+            pltpu.make_async_copy(high, high_out, out_sems.at[0]),
+            pltpu.make_async_copy(low, low_out, out_sems.at[1]),
+        ]
+        for copy in stores:
+            copy.start()
+        for copy in stores:
+            copy.wait()
+
+
+def early_blend_terms(moments, grads):
+    anywhere = pl.BlockSpec(memory_space=pl.ANY)
+    return pl.pallas_call(
+        early_blend_kernel,
+        in_specs=[anywhere] * 6,
+        out_specs=[anywhere] * 2,
+        out_shape=TERMS,
+        scratch_shapes=[pltpu.VMEM((512, 2304), BF16)] * 4
+        + [pltpu.SemaphoreType.DMA((3, 2)), pltpu.SemaphoreType.DMA((2,))],
+        compiler_params=pltpu.CompilerParams(vmem_limit_bytes=EARLY_LIMIT),
+        name="early_blend_terms",
+    )(*(x for group in zip(moments, grads) for x in group))
+
+
+def blend_kernel(mq, gq, mk, gk, mv, gv, early_high, early_low, high, low):
+    core = lax.rem(lax.axis_index("fsdp"), 2)
+
+    @pl.when(core == 0)
+    def _():
+        high[...] = early_high[...]
+        low[...] = early_low[...]
+
+    @pl.when(core == 1)
+    def _():
+        for (lo, hi), moment, grad in zip(SPLITS, (mq, mk, mv), (gq, gk, gv)):
+            blend = moment[...].astype(F32) + grad[...].astype(F32)
+            high[:, lo:hi], low[:, lo:hi] = split(blend)
+
+
+def blend_terms(moments, grads, early):
     def rows(width):
         return pl.BlockSpec((128, width), lambda i: (i, 0))
 
     return pl.pallas_call(
         blend_kernel,
         grid=(4,),
-        in_specs=[rows(2048)] * 2 + [rows(RANK)] * 4,
+        in_specs=[rows(2048)] * 2 + [rows(RANK)] * 4 + [rows(2304)] * 2,
         out_specs=[rows(2304)] * 2,
-        out_shape=[jax.ShapeDtypeStruct((512, 2304), BF16)] * 2,
-        compiler_params=pltpu.CompilerParams(vmem_limit_bytes=VMEM_LIMIT),
+        out_shape=TERMS,
+        compiler_params=pltpu.CompilerParams(vmem_limit_bytes=BLEND_LIMIT),
         cost_estimate=pl.CostEstimate(
-            flops=4 * 512 * 2304, bytes_accessed=9_400_000, transcendentals=0
+            flops=4 * 512 * 2304, bytes_accessed=14_000_000, transcendentals=0
         ),
         name="blend_terms",
-    )(*(x for group in zip(moments, grads) for x in group))
+    )(*(x for group in zip(moments, grads) for x in group), *early)
 
 
 def small_kernel(kernel, shape, name, *operands):
@@ -94,9 +147,13 @@
     )(*operands)
 
 
-def repeat_kernel(block, out):
+def repeat_kernel(own, sibling, out):
+    first = lax.rem(lax.axis_index("fsdp"), 2) == 0
+    a, b = own[...], sibling[...]
+    low, high = jnp.where(first, a, b), jnp.where(first, b, a)
     for i in range(out.shape[0]):
-        out[i] = block[...]
+        out[i, :72] = low
+        out[i, 72:] = high
 
 
 def repeat_total_kernel(parts, out):
@@ -109,11 +166,9 @@
     out[...] = a[...] + b[...]
 
 
-def rows_kernel(high, low, mine, other, out, basis, small):
-    first = lax.rem(lax.axis_index("fsdp"), 2) == 0
+def rows_kernel(high, low, gathered, out, basis, small):
     for i in range(16):
-        a, b = mine[i], other[i]
-        pair = (jnp.where(first, a, b), jnp.where(first, b, a))
+        pair = (gathered[i, :72], gathered[i, 72:])
         for c in range(2):
             at = 128 * i + 64 * c
             qh, ql = split(pair[c][:64])
@@ -135,10 +190,10 @@
                 out[4 * half + d, 64 * m : 64 * m + 64] = rows[64 * d : 64 * d + 64]
 
 
-def partial_rows(high, low, mine, other):
+def partial_rows(high, low, gathered):
     return pl.pallas_call(
         rows_kernel,
-        in_specs=[VMEM] * 4,
+        in_specs=[VMEM] * 3,
         out_specs=VMEM,
         out_shape=jax.ShapeDtypeStruct((8, 192, RANK), F32),
         scratch_shapes=[pltpu.VMEM((2304, 2 * RANK), BF16), pltpu.VMEM((2, RANK, RANK), F32)],
@@ -147,7 +202,7 @@
             flops=6 * 512 * 2304 * RANK, bytes_accessed=7_000_000, transcendentals=0
         ),
         name="partial_rows",
-    )(high, low, mine, other)
+    )(high, low, gathered)
 
 
 def grid_of_indices():
@@ -465,12 +520,15 @@
         for w in weights
     ]
 
-    high, low = blend_terms(moments, grads)
     bases = jnp.concatenate([basis_q, basis_k, basis_v], axis=0)
-    bases = small_kernel(repeat_kernel, (16,) + bases.shape, "repeat_bases", bases)
-    mine = plane_exchange(bases)
-    mine, high, low = lax.optimization_barrier((mine, high, low))
-    chunks = partial_rows(high, low, mine, swap_core(mine))
+    sibling, momentum_q = lax.optimization_barrier((swap_core(bases), momentum_q))
+    early = early_blend_terms((momentum_q, momentum_k, momentum_v), grads)
+    bases = small_kernel(repeat_kernel, (16, 144, RANK), "repeat_bases", bases, sibling)
+    bases, early = lax.optimization_barrier((bases, early))
+    gathered = plane_exchange(bases)
+    high, low = blend_terms(moments, grads, early)
+    gathered, high, low = lax.optimization_barrier((gathered, high, low))
+    chunks = partial_rows(high, low, gathered)
     own = small_kernel(repeat_total_kernel, chunks.shape, "own_rows", tensor_exchange(chunks))
     rows = tensor_exchange(own)
     send, projected, lhs, grams = part_to_send(high, low, rows)

time: 143 us -> 140 us (0.979)
  blocking collectives: 94.1 us -> 83.5 us
  starting transfers between devices: 16.2 us -> 20.7 us
  Pallas kernels: 16.8 us -> 20.8 us
  local copies, waits for them, and re-layouts: 9.9 us -> 6.18 us
  waiting for transfers between devices: 4.26 us -> 6.86 us
    all_to_all x3, blocking collectives: 62.6 us -> 51.1 us  [tensor_exchange(): return lax.all_to_all(x, 'tensor', 0, 0, tiled=True)]
    ppermute x3, starting transfers between devices: 8.59 us -> 15.5 us  [swap_core(): return lax.ppermute(x, 'fsdp', SIBLING)]
    pallas_call x1, Pallas kernels: 1.06 us -> 5.81 us  [blend_terms(): pl.pallas_call(blend_kernel, grid=(4,), in_specs=[rows(2048)] * 2 + [rows...]
    unnamed x24 -> x26, local copies, waits for them, and re-layouts: 9.9 us -> 6.18 us
    all_to_all x1, waiting for transfers between devices: 1.69 us -> 5.06 us  [plane_exchange(): return lax.all_to_all(x, 'fsdp', 0, 0, tiled=True, axis_index_groups=PLANE)]
    all_to_all x1, starting transfers between devices: 7.58 us -> 5.16 us  [plane_exchange(): return lax.all_to_all(x, 'fsdp', 0, 0, tiled=True, axis_index_groups=PLANE)]
  transfers between devices with their start and end apart: 4 -> 4, of which waited for: 3 -> 3; matrix products, arithmetic and copies ran while one was open for 0% -> 0% of each run, Pallas kernels for 5% -> 8%
where the time goes in v6:
time: 140 us
  blocking collectives  83.5 us (60%)
  Pallas kernels  20.8 us (15%)
  starting transfers between devices  20.7 us (15%)
  waiting for transfers between devices  6.86 us (5%)
  local copies, waits for them, and re-layouts  6.18 us (4%)
    all_to_all x3, blocking collectives, tensor_exchange(): return lax.all_to_all(x, 'tensor', 0, 0, tiled=True)  51.1 us
    all_to_all x2, blocking collectives, plane_exchange(): return lax.all_to_all(x, 'fsdp', 0, 0, tiled=True, axis_index_groups=PLANE)  32.4 us
    ppermute x3, starting transfers between devices, swap_core(): return lax.ppermute(x, 'fsdp', SIBLING)  15.5 us
    unnamed x26, local copies, waits for them, and re-layouts  6.18 us
    pallas_call x1, Pallas kernels, blend_terms(): pl.pallas_call(blend_kernel, grid=(4,), in_specs=[rows(2048)] * 2 + [rows...  5.81 us
    all_to_all x1, starting transfers between devices, plane_exchange(): return lax.all_to_all(x, 'fsdp', 0, 0, tiled=True, axis_index_groups=PLANE)  5.16 us
    all_to_all x1, waiting for transfers between devices, plane_exchange(): return lax.all_to_all(x, 'fsdp', 0, 0, tiled=True, axis_index_groups=PLANE)  5.06 us
    pallas_call x1, Pallas kernels, factor(): pl.pallas_call(factor_kernel, in_specs=[VMEM] * 2, out_specs=[VMEM] * 2,...  5.06 us
  transfers between devices with their start and end apart: 4, of which 3 were waited for; matrix products, arithmetic and copies ran while one was open for 0% of the time, Pallas kernels for 8%

profile of v6, /device:TPU:1, one launch (start us, length us, event | category | flops | bytes accessed | tf_op | source)
XLA Modules:
  0.0 139.6 jit_solution(14151775768615393534)
XLA Ops:
  0.6 0.8 pad_maximum_fusion.own
  1.4 3.2 %collective-permute-start = (f32[72,128]{1,0:T(8,128)S(1)}, f32[72,128]{1,0:T(8,128)S(1)}, u32[]{:S(2)}, u32[]{:S(2)}) collective-permute-start(f32[72,128]{1,0:T(8,128)S(1)} %pad_maximum_fusion.own), channel_id=1, source_target_pairs={{0,8},{8,0},{16,24},{24,16},{32,40},{40,32},{48,56},{56,48},{64,72... | collective-permute-start | bytes 110600 | tf_op jit(solution)/shard_map/ppermute | solution.py:26
  4.7 0.9 collective-permute-done.sibling
  5.5 0.1 repeat_bases.1
  5.6 0.0 copy-start.5
  5.6 1.0 copy-done.5
  6.6 0.1 early_blend_terms.1
  6.7 0.0 copy-start.7
  6.8 5.2 %all-to-all-start = ((f32[16,144,128]{2,1,0:T(8,128)}), f32[16,144,128]{2,1,0:T(8,128)S(1)}, u32[]{:S(2)}, u32[]{:S(2)}) async-start(f32[16,144,128]{2,1,0:T(8,128)} %copy-done.5), calls=%async_computation | async-start | bytes 2359296 | tf_op jit(solution)/shard_map/all_to_all | solution.py:30
  12.0 0.9 copy-done.9
  12.9 0.9 copy-done.10
  13.8 5.8 %blend_terms.1 = (bf16[512,2304]{1,0:T(8,128)(2,1)}, bf16[512,2304]{1,0:T(8,128)(2,1)}) custom-call(bf16[512,2048]{1,0:T(8,128)(2,1)S(1)} %copy-done.4, bf16[512,2048]{1,0:T(8,128)(2,1)} %gq.3, bf16[512,128]{1,0:T(8,128)(2,1)S(1)} %copy-done.7, bf16[512,128]{1,0:T(8,128)(2,1)S(1)} %copy-done.8, bf16[512,128]{1,0:T(8,128)(2,1)S(1)} %copy-done.9, ...), custom_call_target="tpu_custom_call" | custom-call | flops 4718592 | bytes 14000000 | tf_op jit(solution)/shard_map/blend_terms/pallas_call | solution.py:125
  19.6 5.1 %all-to-all-done.gathered = f32[16,144,128]{2,1,0:T(8,128)S(1)} async-done(((f32[16,144,128]{2,1,0:T(8,128)}), f32[16,144,128]{2,1,0:T(8,128)S(1)}, u32[]{:S(2)}, u32[]{:S(2)}) %all-to-all-start) | async-done | bytes 1179680 | tf_op jit(solution)/shard_map/all_to_all | solution.py:30
  24.7 1.7 %copy-done = bf16[512,2304]{1,0:T(8,128)(2,1)S(1)} copy-done((bf16[512,2304]{1,0:T(8,128)(2,1)S(1)}, bf16[512,2304]{1,0:T(8,128)(2,1)}, u32[]{:S(2)}) %copy-start) | copy-done | bytes 2359320
  26.3 1.7 %copy-done.2 = bf16[512,2304]{1,0:T(8,128)(2,1)S(1)} copy-done((bf16[512,2304]{1,0:T(8,128)(2,1)S(1)}, bf16[512,2304]{1,0:T(8,128)(2,1)}, u32[]{:S(2)}) %copy-start.2) | copy-done | bytes 2359320
  28.0 1.5 %partial_rows.1 = f32[8,192,128]{2,1,0:T(8,128)S(1)} custom-call(bf16[512,2304]{1,0:T(8,128)(2,1)S(1)} %copy-done, bf16[512,2304]{1,0:T(8,128)(2,1)S(1)} %copy-done.2, f32[16,144,128]{2,1,0:T(8,128)S(1)} %all-to-all-done.gathered), custom_call_target="tpu_custom_call" | custom-call | flops 905969664 | bytes 7000000 | tf_op jit(solution)/shard_map/partial_rows/pallas_call | solution.py:194
  29.5 23.6 %all_to_all.30.parts = f32[8,192,128]{2,1,0:T(8,128)S(1)} all-to-all(f32[8,192,128]{2,1,0:T(8,128)S(1)} %partial_rows.1), channel_id=1, replica_groups=mesh['fsdp'=32,'tensor'=8] {'tensor'}, dimensions={0} | all-to-all | bytes 1572864 | tf_op jit(solution)/shard_map/all_to_all | solution.py:34
  53.1 0.1 own_rows.1
  53.2 18.2 %all_to_all.31.rows = f32[8,192,128]{2,1,0:T(8,128)S(1)} all-to-all(f32[8,192,128]{2,1,0:T(8,128)S(1)} %own_rows.1), channel_id=1, replica_groups=mesh['fsdp'=32,'tensor'=8] {'tensor'}, dimensions={0} | all-to-all | bytes 1572864 | tf_op jit(solution)/shard_map/all_to_all | solution.py:34
  71.4 1.8 %part_to_send.1 = (f32[11,128,128]{2,1,0:T(8,128)S(1)}, f32[3,512,128]{2,1,0:T(8,128)S(1)}, bf16[3,256,512]{2,1,0:T(8,128)(2,1)S(1)}, f32[2,128,128]{2,1,0:T(8,128)S(1)}) custom-call(bf16[512,2304]{1,0:T(8,128)(2,1)S(1)} %copy-done.1, bf16[512,2304]{1,0:T(8,128)(2,1)S(1)} %copy-done.2, f32[8,192,128]{2,1,0:T(8,128)S(1)} %all_to_all.31.rows), custom_call_target="tpu_custom_call" | custom-call | flops 452984832 | bytes 5000000 | tf_op jit(solution)/shard_map/part_to_send/pallas_call | solution.py:282
  73.2 9.3 %collective-permute-start.1 = (f32[11,128,128]{2,1,0:T(8,128)S(1)}, f32[11,128,128]{2,1,0:T(8,128)S(1)}, u32[]{:S(2)}, u32[]{:S(2)}) collective-permute-start(f32[11,128,128]{2,1,0:T(8,128)S(1)} %get-tuple-element.56), channel_id=1, source_target_pairs={{0,8},{8,0},{16,24},{24,16},{32,40},{40,32},{48,56},{56,48},{64,72... | collective-permute-start | bytes 2162696 | tf_op jit(solution)/shard_map/ppermute | solution.py:26
  82.5 0.9 part_to_keep.1.a
  83.4 0.9 collective-permute-done.1.b
  84.3 0.1 pair_sum.1
  84.4 17.5 %all_to_all.32.parts = f32[16,88,128]{2,1,0:T(8,128)S(1)} all-to-all(f32[16,88,128]{2,1,0:T(8,128)S(1)} %bitcast.5), channel_id=1, replica_groups={{0,16,32,48,64,80,96,112,128,144,160,176,192,208,224,240},{8,24,40,56,7..., dimensions={0} | all-to-all | bytes 1441792 | tf_op jit(solution)/shard_map/all_to_all | solution.py:30
  101.9 0.1 own_share.1
  102.0 14.9 %all_to_all.33 = f32[16,88,128]{2,1,0:T(8,128)S(1)} all-to-all(f32[16,88,128]{2,1,0:T(8,128)S(1)} %own_share.1), channel_id=1, replica_groups={{0,16,32,48,64,80,96,112,128,144,160,176,192,208,224,240},{8,24,40,56,7..., dimensions={0} | all-to-all | bytes 1441792 | tf_op jit(solution)/shard_map/all_to_all | solution.py:30
  116.9 3.0 %collective-permute-start.2 = (f32[11,128,128]{2,1,0:T(8,128)S(1)}, f32[11,128,128]{2,1,0:T(8,128)S(1)}, u32[]{:S(2)}, u32[]{:S(2)}) collective-permute-start(f32[11,128,128]{2,1,0:T(8,128)S(1)} %bitcast.2), channel_id=1, source_target_pairs={{0,8},{8,0},{16,24},{24,16},{32,40},{40,32},{48,56},{56,48},{64,72... | collective-permute-start | bytes 2162696 | tf_op jit(solution)/shard_map/ppermute | solution.py:26
  119.9 5.1 %factor.1 = (f32[3,128,128]{2,1,0:T(8,128)S(1)}, f32[3,512,128]{2,1,0:T(8,128)S(1)}) custom-call(f32[11,128,128]{2,1,0:T(8,128)S(1)} %bitcast.3, f32[3,512,128]{2,1,0:T(8,128)S(1)} %get-tuple-element.57.projected), custom_call_target="tpu_custom_call" | custom-call | flops 6000000000 | bytes 3000000 | tf_op jit(solution)/shard_map/factor/pallas_call | solution.py:366
  124.9 0.8 rotate.1
  125.8 9.2 %all_to_all.34.squares = f32[8,8,128]{2,1,0:T(8,128)S(1)} all-to-all(f32[8,8,128]{2,1,0:T(8,128)S(1)} %get-tuple-element.62), channel_id=1, replica_groups=mesh['fsdp'=32,'tensor'=8] {'tensor'}, dimensions={0} | all-to-all | bytes 65536 | tf_op jit(solution)/shard_map/all_to_all | solution.py:34
  135.0 4.6 %updates.1 = (bf16[512,2048]{1,0:T(8,128)(2,1)}, bf16[512,128]{1,0:T(8,128)(2,1)}, bf16[512,128]{1,0:T(8,128)(2,1)}, bf16[512,2048]{1,0:T(8,128)(2,1)}, bf16[512...) custom-call(bf16[512,2304]{1,0:T(8,128)(2,1)S(1)} %copy-done.1, ...), custom_call_target="tpu_custom_call" | custom-call | flops 1811939328 | bytes 16000000 | tf_op jit(solution)/shard_map/updates/pallas_call | solution.py:486
  (20 shorter events, 0.0 us)
Async XLA Ops:
  1.4 4.1 %collective-permute-start = (f32[72,128]{1,0:T(8,128)S(1)}, f32[72,128]{1,0:T(8,128)S(1)}, u32[]{:S(2)}, u32[]{:S(2)}) collective-permute-start(f32[72,128]{1,0:T(8,128)S(1)} %pad_maximum_fusion.own), channel_id=1, source_target_pairs={{0,8},{8,0},{16,24},{24,16},{32,40},{40,32},{48,56},{56,48},{64,72... | collective-permute-start | bytes 110600 | tf_op jit(solution)/shard_map/ppermute | solution.py:26
  5.6 1.0 copy-start.5
  6.7 5.2 %copy-start.4 = (bf16[512,2048]{1,0:T(8,128)(2,1)S(1)}, bf16[512,2048]{1,0:T(8,128)(2,1)}, u32[]{:S(2)}) copy-start(bf16[512,2048]{1,0:T(8,128)(2,1)} %mq.2) | copy-start | bytes 6291460
  6.7 5.2 %copy-start.7 = (bf16[512,128]{1,0:T(8,128)(2,1)S(1)}, bf16[512,128]{1,0:T(8,128)(2,1)}, u32[]{:S(2)}) copy-start(bf16[512,128]{1,0:T(8,128)(2,1)} %mk.3) | copy-start | bytes 393220
  6.8 5.2 %copy-start.8 = (bf16[512,128]{1,0:T(8,128)(2,1)S(1)}, bf16[512,128]{1,0:T(8,128)(2,1)}, u32[]{:S(2)}) copy-start(bf16[512,128]{1,0:T(8,128)(2,1)} %gk.3) | copy-start | bytes 393220
  6.8 17.9 %all-to-all-start = ((f32[16,144,128]{2,1,0:T(8,128)}), f32[16,144,128]{2,1,0:T(8,128)S(1)}, u32[]{:S(2)}, u32[]{:S(2)}) async-start(f32[16,144,128]{2,1,0:T(8,128)} %copy-done.5), calls=%async_computation | async-start | bytes 2359296 | tf_op jit(solution)/shard_map/all_to_all | solution.py:30
  12.0 0.9 copy-start.9
  12.9 0.9 copy-start.10
  24.7 1.7 %copy-start = (bf16[512,2304]{1,0:T(8,128)(2,1)S(1)}, bf16[512,2304]{1,0:T(8,128)(2,1)}, u32[]{:S(2)}) copy-start(bf16[512,2304]{1,0:T(8,128)(2,1)} %get-tuple-element.51.high) | copy-start | bytes 7077892
  26.3 1.7 %copy-start.2 = (bf16[512,2304]{1,0:T(8,128)(2,1)S(1)}, bf16[512,2304]{1,0:T(8,128)(2,1)}, u32[]{:S(2)}) copy-start(bf16[512,2304]{1,0:T(8,128)(2,1)} %get-tuple-element.52.low) | copy-start | bytes 7077892
  29.5 41.9 %copy-start.1 = (bf16[512,2304]{1,0:T(8,128)(2,1)S(1)}, bf16[512,2304]{1,0:T(8,128)(2,1)}, u32[]{:S(2)}) copy-start(bf16[512,2304]{1,0:T(8,128)(2,1)} %get-tuple-element.51.high) | copy-start | bytes 7077892
  73.2 11.1 %collective-permute-start.1 = (f32[11,128,128]{2,1,0:T(8,128)S(1)}, f32[11,128,128]{2,1,0:T(8,128)S(1)}, u32[]{:S(2)}, u32[]{:S(2)}) collective-permute-start(f32[11,128,128]{2,1,0:T(8,128)S(1)} %get-tuple-element.56), channel_id=1, source_target_pairs={{0,8},{8,0},{16,24},{24,16},{32,40},{40,32},{48,56},{56,48},{64,72... | collective-permute-start | bytes 2162696 | tf_op jit(solution)/shard_map/ppermute | solution.py:26
  116.9 8.0 %collective-permute-start.2 = (f32[11,128,128]{2,1,0:T(8,128)S(1)}, f32[11,128,128]{2,1,0:T(8,128)S(1)}, u32[]{:S(2)}, u32[]{:S(2)}) collective-permute-start(f32[11,128,128]{2,1,0:T(8,128)S(1)} %bitcast.2), channel_id=1, source_target_pairs={{0,8},{8,0},{16,24},{24,16},{32,40},{40,32},{48,56},{56,48},{64,72... | collective-permute-start | bytes 2162696 | tf_op jit(solution)/shard_map/ppermute | solution.py:26
  119.9 15.2 %copy-start.3 = (bf16[512,2304]{1,0:T(8,128)(2,1)S(1)}, bf16[512,2304]{1,0:T(8,128)(2,1)}, u32[]{:S(2)}) copy-start(bf16[512,2304]{1,0:T(8,128)(2,1)} %get-tuple-element.52.low) | copy-start | bytes 7077892
  119.9 15.2 %copy-start.6 = (bf16[512,2048]{1,0:T(8,128)(2,1)S(1)}, bf16[512,2048]{1,0:T(8,128)(2,1)}, u32[]{:S(2)}) copy-start(bf16[512,2048]{1,0:T(8,128)(2,1)} %wq.1) | copy-start | bytes 6291460
  119.9 15.2 %copy-start.11 = (bf16[512,128]{1,0:T(8,128)(2,1)S(1)}, bf16[512,128]{1,0:T(8,128)(2,1)}, u32[]{:S(2)}) copy-start(bf16[512,128]{1,0:T(8,128)(2,1)} %wk.1) | copy-start | bytes 393220
  119.9 15.2 %copy-start.12 = (bf16[512,128]{1,0:T(8,128)(2,1)S(1)}, bf16[512,128]{1,0:T(8,128)(2,1)}, u32[]{:S(2)}) copy-start(bf16[512,128]{1,0:T(8,128)(2,1)} %wv.1) | copy-start | bytes 393220

commit v7 on v6

--- a/solution.py
+++ b/solution.py
@@ -19,7 +19,7 @@
 SUMMED = HALF + 2
 VMEM_LIMIT = 24 * 1024 * 1024
 EARLY_LIMIT = 60 * 1024 * 1024
-BLEND_LIMIT = 50 * 1024 * 1024
+BLEND_LIMIT = 46 * 1024 * 1024
 
 
 def swap_core(x):
@@ -103,31 +103,36 @@
     )(*(x for group in zip(moments, grads) for x in group))
 
 
-def blend_kernel(mq, gq, mk, gk, mv, gv, early_high, early_low, high, low):
+def blend_kernel(mq, gq, mk, gk, mv, gv, early_high, early_low, high, low, sems):
     core = lax.rem(lax.axis_index("fsdp"), 2)
 
     @pl.when(core == 0)
     def _():
-        high[...] = early_high[...]
-        low[...] = early_low[...]
+        copies = [
+            pltpu.make_async_copy(early_high, high, sems.at[0]),
+            pltpu.make_async_copy(early_low, low, sems.at[1]),
+        ]
+        for copy in copies:
+            copy.start()
+        for copy in copies:
+            copy.wait()
 
     @pl.when(core == 1)
     def _():
         for (lo, hi), moment, grad in zip(SPLITS, (mq, mk, mv), (gq, gk, gv)):
-            blend = moment[...].astype(F32) + grad[...].astype(F32)
-            high[:, lo:hi], low[:, lo:hi] = split(blend)
+            for at in range(0, 512, 64):
+                part = slice(at, at + 64)
+                blend = moment[part].astype(F32) + grad[part].astype(F32)
+                high[part, lo:hi], low[part, lo:hi] = split(blend)
 
 
 def blend_terms(moments, grads, early):
-    def rows(width):
-        return pl.BlockSpec((128, width), lambda i: (i, 0))
-
     return pl.pallas_call(
         blend_kernel,
-        grid=(4,),
-        in_specs=[rows(2048)] * 2 + [rows(RANK)] * 4 + [rows(2304)] * 2,
-        out_specs=[rows(2304)] * 2,
+        in_specs=[VMEM] * 6 + [pl.BlockSpec(memory_space=pl.ANY)] * 2,
+        out_specs=[VMEM] * 2,
         out_shape=TERMS,
+        scratch_shapes=[pltpu.SemaphoreType.DMA((2,))],
         compiler_params=pltpu.CompilerParams(vmem_limit_bytes=BLEND_LIMIT),
         cost_estimate=pl.CostEstimate(
             flops=4 * 512 * 2304, bytes_accessed=14_000_000, transcendentals=0

time: 140 us -> 138 us (0.986)
  Pallas kernels: 20.8 us -> 18.5 us
  local copies, waits for them, and re-layouts: 6.18 us -> 8.47 us
  waiting for transfers between devices: 6.86 us -> 5.23 us
    pallas_call x1, Pallas kernels: 5.81 us -> 2.48 us  [blend_terms(): pl.pallas_call(blend_kernel, in_specs=[VMEM] * 6 + [pl.BlockSpec(memory_s...]
    unnamed x26 -> x22, local copies, waits for them, and re-layouts: 6.18 us -> 8.47 us
    all_to_all x1, waiting for transfers between devices: 5.06 us -> 3.43 us  [plane_exchange(): return lax.all_to_all(x, 'fsdp', 0, 0, tiled=True, axis_index_groups=PLANE)]
  transfers between devices with their start and end apart: 4 -> 4, of which waited for: 3 -> 3; matrix products, arithmetic and copies ran while one was open for 0% -> 0% of each run, Pallas kernels for 8% -> 6%
where the time goes in v7:
time: 138 us
  blocking collectives  83.5 us (61%)
  starting transfers between devices  20.6 us (15%)
  Pallas kernels  18.5 us (13%)
  local copies, waits for them, and re-layouts  8.47 us (6%)
  waiting for transfers between devices  5.23 us (4%)
    all_to_all x3, blocking collectives, tensor_exchange(): return lax.all_to_all(x, 'tensor', 0, 0, tiled=True)  51.1 us
    all_to_all x2, blocking collectives, plane_exchange(): return lax.all_to_all(x, 'fsdp', 0, 0, tiled=True, axis_index_groups=PLANE)  32.4 us
    ppermute x3, starting transfers between devices, swap_core(): return lax.ppermute(x, 'fsdp', SIBLING)  15.5 us
    unnamed x22, local copies, waits for them, and re-layouts  8.47 us
    pallas_call x1, Pallas kernels, factor(): pl.pallas_call(factor_kernel, in_specs=[VMEM] * 2, out_specs=[VMEM] * 2,...  5.05 us
    all_to_all x1, starting transfers between devices, plane_exchange(): return lax.all_to_all(x, 'fsdp', 0, 0, tiled=True, axis_index_groups=PLANE)  5.03 us
    pallas_call x1, Pallas kernels, updates(): pl.pallas_call(functools.partial(update_kernel, factors), grid=(STEPS,),...  4.65 us
    all_to_all x1, waiting for transfers between devices, plane_exchange(): return lax.all_to_all(x, 'fsdp', 0, 0, tiled=True, axis_index_groups=PLANE)  3.43 us
  transfers between devices with their start and end apart: 4, of which 3 were waited for; matrix products, arithmetic and copies ran while one was open for 0% of the time, Pallas kernels for 6%

profile of v7, /device:TPU:1, one launch (start us, length us, event | category | flops | bytes accessed | tf_op | source)
XLA Modules:
  0.0 137.8 jit_solution(18060239280642619829)
XLA Ops:
  0.6 0.8 pad_maximum_fusion.own
  1.4 3.2 %collective-permute-start = (f32[72,128]{1,0:T(8,128)S(1)}, f32[72,128]{1,0:T(8,128)S(1)}, u32[]{:S(2)}, u32[]{:S(2)}) collective-permute-start(f32[72,128]{1,0:T(8,128)S(1)} %pad_maximum_fusion.own), channel_id=1, source_target_pairs={{0,8},{8,0},{16,24},{24,16},{32,40},{40,32},{48,56},{56,48},{64,72... | collective-permute-start | bytes 110600 | tf_op jit(solution)/shard_map/ppermute | solution.py:26
  4.7 0.9 collective-permute-done.sibling
  5.5 1.1 repeat_bases.1
  6.6 0.1 early_blend_terms.1
  6.7 5.0 %all-to-all-start = ((f32[16,144,128]{2,1,0:T(8,128)}), f32[16,144,128]{2,1,0:T(8,128)S(1)}, u32[]{:S(2)}, u32[]{:S(2)}) async-start(f32[16,144,128]{2,1,0:T(8,128)} %repeat_bases.1), calls=%async_computation | async-start | bytes 2359296 | tf_op jit(solution)/shard_map/all_to_all | solution.py:30
  11.8 1.6 %copy-done.2 = bf16[512,2048]{1,0:T(8,128)(2,1)S(1)} copy-done((bf16[512,2048]{1,0:T(8,128)(2,1)S(1)}, bf16[512,2048]{1,0:T(8,128)(2,1)}, u32[]{:S(2)}) %copy-start.2) | copy-done | bytes 2097176
  13.4 1.6 %copy-done.3 = bf16[512,2048]{1,0:T(8,128)(2,1)S(1)} copy-done((bf16[512,2048]{1,0:T(8,128)(2,1)S(1)}, bf16[512,2048]{1,0:T(8,128)(2,1)}, u32[]{:S(2)}) %copy-start.3) | copy-done | bytes 2097176
  15.0 0.9 copy-done.5
  15.9 0.9 copy-done.6
  16.8 0.9 copy-done.7
  17.7 0.9 copy-done.8
  18.6 2.5 %blend_terms.1 = (bf16[512,2304]{1,0:T(8,128)(2,1)S(1)}, bf16[512,2304]{1,0:T(8,128)(2,1)}) custom-call(bf16[512,2048]{1,0:T(8,128)(2,1)S(1)} %copy-done.2, bf16[512,2048]{1,0:T(8,128)(2,1)S(1)} %copy-done.3, bf16[512,128]{1,0:T(8,128)(2,1)S(1)} %copy-done.5, bf16[512,128]{1,0:T(8,128)(2,1)S(1)} %copy-done.6, bf16[512,128]{1,0:T(8,128)(2,1)S(1)} %copy-done.7, ...), custom_call_target="tpu_custom_call" | custom-call | flops 4718592 | bytes 14000000 | tf_op jit(solution)/shard_map/blend_terms/pallas_call | solution.py:130
  21.1 3.4 %all-to-all-done.gathered = f32[16,144,128]{2,1,0:T(8,128)S(1)} async-done(((f32[16,144,128]{2,1,0:T(8,128)}), f32[16,144,128]{2,1,0:T(8,128)S(1)}, u32[]{:S(2)}, u32[]{:S(2)}) %all-to-all-start) | async-done | bytes 1179680 | tf_op jit(solution)/shard_map/all_to_all | solution.py:30
  24.5 1.7 %copy-done = bf16[512,2304]{1,0:T(8,128)(2,1)S(1)} copy-done((bf16[512,2304]{1,0:T(8,128)(2,1)S(1)}, bf16[512,2304]{1,0:T(8,128)(2,1)}, u32[]{:S(2)}) %copy-start) | copy-done | bytes 2359320
  26.2 1.5 %partial_rows.1 = f32[8,192,128]{2,1,0:T(8,128)S(1)} custom-call(bf16[512,2304]{1,0:T(8,128)(2,1)S(1)} %get-tuple-element.51.high, bf16[512,2304]{1,0:T(8,128)(2,1)S(1)} %copy-done, f32[16,144,128]{2,1,0:T(8,128)S(1)} %all-to-all-done.gathered), custom_call_target="tpu_custom_call" | custom-call | flops 905969664 | bytes 7000000 | tf_op jit(solution)/shard_map/partial_rows/pallas_call | solution.py:199
  27.7 23.6 %all_to_all.30.parts = f32[8,192,128]{2,1,0:T(8,128)S(1)} all-to-all(f32[8,192,128]{2,1,0:T(8,128)S(1)} %partial_rows.1), channel_id=1, replica_groups=mesh['fsdp'=32,'tensor'=8] {'tensor'}, dimensions={0} | all-to-all | bytes 1572864 | tf_op jit(solution)/shard_map/all_to_all | solution.py:34
  51.3 0.1 own_rows.1
  51.4 18.2 %all_to_all.31.rows = f32[8,192,128]{2,1,0:T(8,128)S(1)} all-to-all(f32[8,192,128]{2,1,0:T(8,128)S(1)} %own_rows.1), channel_id=1, replica_groups=mesh['fsdp'=32,'tensor'=8] {'tensor'}, dimensions={0} | all-to-all | bytes 1572864 | tf_op jit(solution)/shard_map/all_to_all | solution.py:34
  69.6 1.8 %part_to_send.1 = (f32[11,128,128]{2,1,0:T(8,128)S(1)}, f32[3,512,128]{2,1,0:T(8,128)S(1)}, bf16[3,256,512]{2,1,0:T(8,128)(2,1)S(1)}, f32[2,128,128]{2,1,0:T(8,128)S(1)}) custom-call(bf16[512,2304]{1,0:T(8,128)(2,1)S(1)} %get-tuple-element.51.high, bf16[512,2304]{1,0:T(8,128)(2,1)S(1)} %copy-done.1, f32[8,192,128]{2,1,0:T(8,128)S(1)} %all_to_all.31.rows), custom_call_target="tpu_custom_call" | custom-call | flops 452984832 | bytes 5000000 | tf_op jit(solution)/shard_map/part_to_send/pallas_call | solution.py:287
  71.4 9.3 %collective-permute-start.1 = (f32[11,128,128]{2,1,0:T(8,128)S(1)}, f32[11,128,128]{2,1,0:T(8,128)S(1)}, u32[]{:S(2)}, u32[]{:S(2)}) collective-permute-start(f32[11,128,128]{2,1,0:T(8,128)S(1)} %get-tuple-element.56), channel_id=1, source_target_pairs={{0,8},{8,0},{16,24},{24,16},{32,40},{40,32},{48,56},{56,48},{64,72... | collective-permute-start | bytes 2162696 | tf_op jit(solution)/shard_map/ppermute | solution.py:26
  80.7 0.9 part_to_keep.1.a
  81.6 0.9 collective-permute-done.1.b
  82.5 0.1 pair_sum.1
  82.6 17.5 %all_to_all.32.parts = f32[16,88,128]{2,1,0:T(8,128)S(1)} all-to-all(f32[16,88,128]{2,1,0:T(8,128)S(1)} %bitcast.5), channel_id=1, replica_groups={{0,16,32,48,64,80,96,112,128,144,160,176,192,208,224,240},{8,24,40,56,7..., dimensions={0} | all-to-all | bytes 1441792 | tf_op jit(solution)/shard_map/all_to_all | solution.py:30
  100.1 0.1 own_share.1
  100.1 14.9 %all_to_all.33 = f32[16,88,128]{2,1,0:T(8,128)S(1)} all-to-all(f32[16,88,128]{2,1,0:T(8,128)S(1)} %own_share.1), channel_id=1, replica_groups={{0,16,32,48,64,80,96,112,128,144,160,176,192,208,224,240},{8,24,40,56,7..., dimensions={0} | all-to-all | bytes 1441792 | tf_op jit(solution)/shard_map/all_to_all | solution.py:30
  115.0 3.0 %collective-permute-start.2 = (f32[11,128,128]{2,1,0:T(8,128)S(1)}, f32[11,128,128]{2,1,0:T(8,128)S(1)}, u32[]{:S(2)}, u32[]{:S(2)}) collective-permute-start(f32[11,128,128]{2,1,0:T(8,128)S(1)} %bitcast.2), channel_id=1, source_target_pairs={{0,8},{8,0},{16,24},{24,16},{32,40},{40,32},{48,56},{56,48},{64,72... | collective-permute-start | bytes 2162696 | tf_op jit(solution)/shard_map/ppermute | solution.py:26
  118.0 5.1 %factor.1 = (f32[3,128,128]{2,1,0:T(8,128)S(1)}, f32[3,512,128]{2,1,0:T(8,128)S(1)}) custom-call(f32[11,128,128]{2,1,0:T(8,128)S(1)} %bitcast.3, f32[3,512,128]{2,1,0:T(8,128)S(1)} %get-tuple-element.57.projected), custom_call_target="tpu_custom_call" | custom-call | flops 6000000000 | bytes 3000000 | tf_op jit(solution)/shard_map/factor/pallas_call | solution.py:371
  123.1 0.8 rotate.1
  123.9 9.2 %all_to_all.34.squares = f32[8,8,128]{2,1,0:T(8,128)S(1)} all-to-all(f32[8,8,128]{2,1,0:T(8,128)S(1)} %get-tuple-element.62), channel_id=1, replica_groups=mesh['fsdp'=32,'tensor'=8] {'tensor'}, dimensions={0} | all-to-all | bytes 65536 | tf_op jit(solution)/shard_map/all_to_all | solution.py:34
  133.2 4.6 %updates.1 = (bf16[512,2048]{1,0:T(8,128)(2,1)}, bf16[512,128]{1,0:T(8,128)(2,1)}, bf16[512,128]{1,0:T(8,128)(2,1)}, bf16[512,2048]{1,0:T(8,128)(2,1)}, bf16[512...) custom-call(bf16[512,2304]{1,0:T(8,128)(2,1)S(1)} %get-tuple-element, ...), custom_call_target="tpu_custom_call" | custom-call | flops 1811939328 | bytes 16000000 | tf_op jit(solution)/shard_map/updates/pallas_call | solution.py:491
  (16 shorter events, 0.0 us)
Async XLA Ops:
  1.4 4.1 %collective-permute-start = (f32[72,128]{1,0:T(8,128)S(1)}, f32[72,128]{1,0:T(8,128)S(1)}, u32[]{:S(2)}, u32[]{:S(2)}) collective-permute-start(f32[72,128]{1,0:T(8,128)S(1)} %pad_maximum_fusion.own), channel_id=1, source_target_pairs={{0,8},{8,0},{16,24},{24,16},{32,40},{40,32},{48,56},{56,48},{64,72... | collective-permute-start | bytes 110600 | tf_op jit(solution)/shard_map/ppermute | solution.py:26
  6.7 17.8 %all-to-all-start = ((f32[16,144,128]{2,1,0:T(8,128)}), f32[16,144,128]{2,1,0:T(8,128)S(1)}, u32[]{:S(2)}, u32[]{:S(2)}) async-start(f32[16,144,128]{2,1,0:T(8,128)} %repeat_bases.1), calls=%async_computation | async-start | bytes 2359296 | tf_op jit(solution)/shard_map/all_to_all | solution.py:30
  11.8 1.6 %copy-start.2 = (bf16[512,2048]{1,0:T(8,128)(2,1)S(1)}, bf16[512,2048]{1,0:T(8,128)(2,1)}, u32[]{:S(2)}) copy-start(bf16[512,2048]{1,0:T(8,128)(2,1)} %mq.2) | copy-start | bytes 6291460
  13.4 1.6 %copy-start.3 = (bf16[512,2048]{1,0:T(8,128)(2,1)S(1)}, bf16[512,2048]{1,0:T(8,128)(2,1)}, u32[]{:S(2)}) copy-start(bf16[512,2048]{1,0:T(8,128)(2,1)} %gq.3) | copy-start | bytes 6291460
  14.9 0.9 copy-start.5
  15.9 0.9 copy-start.6
  16.8 0.9 copy-start.7
  17.7 0.9 copy-start.8
  24.5 1.7 %copy-start = (bf16[512,2304]{1,0:T(8,128)(2,1)S(1)}, bf16[512,2304]{1,0:T(8,128)(2,1)}, u32[]{:S(2)}) copy-start(bf16[512,2304]{1,0:T(8,128)(2,1)} %get-tuple-element.52.low) | copy-start | bytes 7077892
  27.6 41.9 %copy-start.1 = (bf16[512,2304]{1,0:T(8,128)(2,1)S(1)}, bf16[512,2304]{1,0:T(8,128)(2,1)}, u32[]{:S(2)}) copy-start(bf16[512,2304]{1,0:T(8,128)(2,1)} %get-tuple-element.52.low) | copy-start | bytes 7077892
  71.4 11.1 %collective-permute-start.1 = (f32[11,128,128]{2,1,0:T(8,128)S(1)}, f32[11,128,128]{2,1,0:T(8,128)S(1)}, u32[]{:S(2)}, u32[]{:S(2)}) collective-permute-start(f32[11,128,128]{2,1,0:T(8,128)S(1)} %get-tuple-element.56), channel_id=1, source_target_pairs={{0,8},{8,0},{16,24},{24,16},{32,40},{40,32},{48,56},{56,48},{64,72... | collective-permute-start | bytes 2162696 | tf_op jit(solution)/shard_map/ppermute | solution.py:26
  115.0 8.0 %collective-permute-start.2 = (f32[11,128,128]{2,1,0:T(8,128)S(1)}, f32[11,128,128]{2,1,0:T(8,128)S(1)}, u32[]{:S(2)}, u32[]{:S(2)}) collective-permute-start(f32[11,128,128]{2,1,0:T(8,128)S(1)} %bitcast.2), channel_id=1, source_target_pairs={{0,8},{8,0},{16,24},{24,16},{32,40},{40,32},{48,56},{56,48},{64,72... | collective-permute-start | bytes 2162696 | tf_op jit(solution)/shard_map/ppermute | solution.py:26
  118.0 15.1 %copy-start.4 = (bf16[512,2048]{1,0:T(8,128)(2,1)S(1)}, bf16[512,2048]{1,0:T(8,128)(2,1)}, u32[]{:S(2)}) copy-start(bf16[512,2048]{1,0:T(8,128)(2,1)} %wq.1) | copy-start | bytes 6291460
  118.0 15.1 %copy-start.9 = (bf16[512,128]{1,0:T(8,128)(2,1)S(1)}, bf16[512,128]{1,0:T(8,128)(2,1)}, u32[]{:S(2)}) copy-start(bf16[512,128]{1,0:T(8,128)(2,1)} %wk.1) | copy-start | bytes 393220
  118.0 15.1 %copy-start.10 = (bf16[512,128]{1,0:T(8,128)(2,1)S(1)}, bf16[512,128]{1,0:T(8,128)(2,1)}, u32[]{:S(2)}) copy-start(bf16[512,128]{1,0:T(8,128)(2,1)} %wv.1) | copy-start | bytes 393220

commit v8 on v7

--- a/solution.py
+++ b/solution.py
@@ -171,7 +171,7 @@
     out[...] = a[...] + b[...]
 
 
-def rows_kernel(high, low, gathered, out, basis, small):
+def high_rows_kernel(high, gathered, out, basis, small):
     for i in range(16):
         pair = (gathered[i, :72], gathered[i, 72:])
         for c in range(2):
@@ -186,28 +186,51 @@
         qh, ql = split(small[n])
         basis[2048 + RANK * n : 2048 + RANK * n + RANK, :RANK] = qh
         basis[2048 + RANK * n : 2048 + RANK * n + RANK, RANK:] = ql
-    for m, (lo, hi) in enumerate(((0, 2048), (2048, 2176), (2176, 2304))):
+    for m, (lo, hi) in enumerate(SPLITS):
         for half in range(2):
-            at = slice(256 * half, 256 * half + 256)
-            both = dot(high[at, lo:hi], basis[lo:hi])
-            rows = both[:, :RANK] + both[:, RANK:] + dot(low[at, lo:hi], basis[lo:hi, :RANK])
+            both = dot(high[256 * half : 256 * half + 256, lo:hi], basis[lo:hi])
+            rows = both[:, :RANK] + both[:, RANK:]
             for d in range(4):
                 out[4 * half + d, 64 * m : 64 * m + 64] = rows[64 * d : 64 * d + 64]
 
 
+def low_rows_kernel(low, basis, part, out):
+    for m, (lo, hi) in enumerate(SPLITS):
+        for half in range(2):
+            rows = dot(low[256 * half : 256 * half + 256, lo:hi], basis[lo:hi, :RANK])
+            for d in range(4):
+                at = (4 * half + d, slice(64 * m, 64 * m + 64))
+                out[at] = part[at] + rows[64 * d : 64 * d + 64]
+
+
+ROWS_SHAPE = jax.ShapeDtypeStruct((8, 192, RANK), F32)
+
+
 def partial_rows(high, low, gathered):
-    return pl.pallas_call(
-        rows_kernel,
+    params = pltpu.CompilerParams(vmem_limit_bytes=VMEM_LIMIT)
+    part, basis = pl.pallas_call(
+        high_rows_kernel,
+        in_specs=[VMEM] * 2,
+        out_specs=[VMEM] * 2,
+        out_shape=[ROWS_SHAPE, jax.ShapeDtypeStruct((2304, 2 * RANK), BF16)],
+        scratch_shapes=[pltpu.VMEM((2, RANK, RANK), F32)],
+        compiler_params=params,
+        cost_estimate=pl.CostEstimate(
+            flops=4 * 512 * 2304 * RANK, bytes_accessed=7_000_000, transcendentals=0
+        ),
+        name="high_rows",
+    )(high, gathered)
+    return pl.pallas_call(
+        low_rows_kernel,
         in_specs=[VMEM] * 3,
         out_specs=VMEM,
-        out_shape=jax.ShapeDtypeStruct((8, 192, RANK), F32),
-        scratch_shapes=[pltpu.VMEM((2304, 2 * RANK), BF16), pltpu.VMEM((2, RANK, RANK), F32)],
-        compiler_params=pltpu.CompilerParams(vmem_limit_bytes=VMEM_LIMIT),
+        out_shape=ROWS_SHAPE,
+        compiler_params=params,
         cost_estimate=pl.CostEstimate(
-            flops=6 * 512 * 2304 * RANK, bytes_accessed=7_000_000, transcendentals=0
+            flops=2 * 512 * 2304 * RANK, bytes_accessed=4_000_000, transcendentals=0
         ),
-        name="partial_rows",
-    )(high, low, gathered)
+        name="low_rows",
+    )(low, basis, part)
 
 
 def grid_of_indices():

time: 138 us -> 138 us (level)
    unnamed x22 -> x20, local copies, waits for them, and re-layouts: 8.47 us -> 7.59 us
where the time goes in v8:
time: 138 us; the launch traced here: 137 us
  blocking collectives  83.4 us (60%)
  starting transfers between devices  20.6 us (15%)
  Pallas kernels  18.7 us (14%)
  local copies, waits for them, and re-layouts  7.59 us (6%)
  waiting for transfers between devices  5.23 us (4%)
    all_to_all x3, blocking collectives, tensor_exchange(): return lax.all_to_all(x, 'tensor', 0, 0, tiled=True)  50.9 us
    all_to_all x2, blocking collectives, plane_exchange(): return lax.all_to_all(x, 'fsdp', 0, 0, tiled=True, axis_index_groups=PLANE)  32.4 us
    ppermute x3, starting transfers between devices, swap_core(): return lax.ppermute(x, 'fsdp', SIBLING)  15.5 us
    unnamed x20, local copies, waits for them, and re-layouts  7.59 us
    pallas_call x1, Pallas kernels, factor(): pl.pallas_call(factor_kernel, in_specs=[VMEM] * 2, out_specs=[VMEM] * 2,...  5.06 us
    all_to_all x1, starting transfers between devices, plane_exchange(): return lax.all_to_all(x, 'fsdp', 0, 0, tiled=True, axis_index_groups=PLANE)  5.03 us
    pallas_call x1, Pallas kernels, updates(): pl.pallas_call(functools.partial(update_kernel, factors), grid=(STEPS,),...  4.65 us
    all_to_all x1, waiting for transfers between devices, plane_exchange(): return lax.all_to_all(x, 'fsdp', 0, 0, tiled=True, axis_index_groups=PLANE)  3.43 us
  transfers between devices with their start and end apart: 4, of which 3 were waited for; matrix products, arithmetic and copies ran while one was open for 0% of the time, Pallas kernels for 6%

profile of v8, /device:TPU:1, one launch (start us, length us, event | category | flops | bytes accessed | tf_op | source)
XLA Modules:
  0.0 137.0 jit_solution(488547687124841030)
XLA Ops:
  0.6 0.8 pad_maximum_fusion.own
  1.4 3.2 %collective-permute-start = (f32[72,128]{1,0:T(8,128)S(1)}, f32[72,128]{1,0:T(8,128)S(1)}, u32[]{:S(2)}, u32[]{:S(2)}) collective-permute-start(f32[72,128]{1,0:T(8,128)S(1)} %pad_maximum_fusion.own), channel_id=1, source_target_pairs={{0,8},{8,0},{16,24},{24,16},{32,40},{40,32},{48,56},{56,48},{64,72... | collective-permute-start | bytes 110600 | tf_op jit(solution)/shard_map/ppermute | solution.py:26
  4.7 0.9 collective-permute-done.sibling
  5.5 1.1 repeat_bases.1
  6.6 0.1 early_blend_terms.1
  6.7 5.0 %all-to-all-start = ((f32[16,144,128]{2,1,0:T(8,128)}), f32[16,144,128]{2,1,0:T(8,128)S(1)}, u32[]{:S(2)}, u32[]{:S(2)}) async-start(f32[16,144,128]{2,1,0:T(8,128)} %repeat_bases.1), calls=%async_computation | async-start | bytes 2359296 | tf_op jit(solution)/shard_map/all_to_all | solution.py:30
  11.8 1.6 %copy-done.1 = bf16[512,2048]{1,0:T(8,128)(2,1)S(1)} copy-done((bf16[512,2048]{1,0:T(8,128)(2,1)S(1)}, bf16[512,2048]{1,0:T(8,128)(2,1)}, u32[]{:S(2)}) %copy-start.1) | copy-done | bytes 2097176
  13.4 1.6 %copy-done.2 = bf16[512,2048]{1,0:T(8,128)(2,1)S(1)} copy-done((bf16[512,2048]{1,0:T(8,128)(2,1)S(1)}, bf16[512,2048]{1,0:T(8,128)(2,1)}, u32[]{:S(2)}) %copy-start.2) | copy-done | bytes 2097176
  15.0 0.9 copy-done.4
  15.9 0.9 copy-done.5
  16.8 0.9 copy-done.6
  17.7 0.9 copy-done.7
  18.6 2.5 %blend_terms.1 = (bf16[512,2304]{1,0:T(8,128)(2,1)S(1)}, bf16[512,2304]{1,0:T(8,128)(2,1)}) custom-call(bf16[512,2048]{1,0:T(8,128)(2,1)S(1)} %copy-done.1, bf16[512,2048]{1,0:T(8,128)(2,1)S(1)} %copy-done.2, bf16[512,128]{1,0:T(8,128)(2,1)S(1)} %copy-done.4, bf16[512,128]{1,0:T(8,128)(2,1)S(1)} %copy-done.5, bf16[512,128]{1,0:T(8,128)(2,1)S(1)} %copy-done.6, ...), custom_call_target="tpu_custom_call" | custom-call | flops 4718592 | bytes 14000000 | tf_op jit(solution)/shard_map/blend_terms/pallas_call | solution.py:130
  21.1 3.4 %all-to-all-done.gathered = f32[16,144,128]{2,1,0:T(8,128)S(1)} async-done(((f32[16,144,128]{2,1,0:T(8,128)}), f32[16,144,128]{2,1,0:T(8,128)S(1)}, u32[]{:S(2)}, u32[]{:S(2)}) %all-to-all-start) | async-done | bytes 1179680 | tf_op jit(solution)/shard_map/all_to_all | solution.py:30
  24.5 0.9 high_rows.1
  25.4 0.8 copy-done
  26.2 0.8 low_rows.1
  26.9 23.5 %all_to_all.30.parts = f32[8,192,128]{2,1,0:T(8,128)S(1)} all-to-all(f32[8,192,128]{2,1,0:T(8,128)S(1)} %low_rows.1), channel_id=1, replica_groups=mesh['fsdp'=32,'tensor'=8] {'tensor'}, dimensions={0} | all-to-all | bytes 1572864 | tf_op jit(solution)/shard_map/all_to_all | solution.py:34
  50.5 18.2 %all_to_all.31.rows = f32[8,192,128]{2,1,0:T(8,128)S(1)} all-to-all(f32[8,192,128]{2,1,0:T(8,128)S(1)} %own_rows.1), channel_id=1, replica_groups=mesh['fsdp'=32,'tensor'=8] {'tensor'}, dimensions={0} | all-to-all | bytes 1572864 | tf_op jit(solution)/shard_map/all_to_all | solution.py:34
  68.7 1.8 %part_to_send.1 = (f32[11,128,128]{2,1,0:T(8,128)S(1)}, f32[3,512,128]{2,1,0:T(8,128)S(1)}, bf16[3,256,512]{2,1,0:T(8,128)(2,1)S(1)}, f32[2,128,128]{2,1,0:T(8,128)S(1)}) custom-call(bf16[512,2304]{1,0:T(8,128)(2,1)S(1)} %get-tuple-element.53.high, bf16[512,2304]{1,0:T(8,128)(2,1)S(1)} %copy-done, f32[8,192,128]{2,1,0:T(8,128)S(1)} %all_to_all.31.rows), custom_call_target="tpu_custom_call" | custom-call | flops 452984832 | bytes 5000000 | tf_op jit(solution)/shard_map/part_to_send/pallas_call | solution.py:310
  70.5 9.3 %collective-permute-start.1 = (f32[11,128,128]{2,1,0:T(8,128)S(1)}, f32[11,128,128]{2,1,0:T(8,128)S(1)}, u32[]{:S(2)}, u32[]{:S(2)}) collective-permute-start(f32[11,128,128]{2,1,0:T(8,128)S(1)} %get-tuple-element.60), channel_id=1, source_target_pairs={{0,8},{8,0},{16,24},{24,16},{32,40},{40,32},{48,56},{56,48},{64,72... | collective-permute-start | bytes 2162696 | tf_op jit(solution)/shard_map/ppermute | solution.py:26
  79.8 0.9 part_to_keep.1.a
  80.7 0.9 collective-permute-done.1.b
  81.6 0.1 pair_sum.1
  81.7 17.5 %all_to_all.32.parts = f32[16,88,128]{2,1,0:T(8,128)S(1)} all-to-all(f32[16,88,128]{2,1,0:T(8,128)S(1)} %bitcast.5), channel_id=1, replica_groups={{0,16,32,48,64,80,96,112,128,144,160,176,192,208,224,240},{8,24,40,56,7..., dimensions={0} | all-to-all | bytes 1441792 | tf_op jit(solution)/shard_map/all_to_all | solution.py:30
  99.2 0.1 own_share.1
  99.3 14.9 %all_to_all.33 = f32[16,88,128]{2,1,0:T(8,128)S(1)} all-to-all(f32[16,88,128]{2,1,0:T(8,128)S(1)} %own_share.1), channel_id=1, replica_groups={{0,16,32,48,64,80,96,112,128,144,160,176,192,208,224,240},{8,24,40,56,7..., dimensions={0} | all-to-all | bytes 1441792 | tf_op jit(solution)/shard_map/all_to_all | solution.py:30
  114.2 3.0 %collective-permute-start.2 = (f32[11,128,128]{2,1,0:T(8,128)S(1)}, f32[11,128,128]{2,1,0:T(8,128)S(1)}, u32[]{:S(2)}, u32[]{:S(2)}) collective-permute-start(f32[11,128,128]{2,1,0:T(8,128)S(1)} %bitcast.2), channel_id=1, source_target_pairs={{0,8},{8,0},{16,24},{24,16},{32,40},{40,32},{48,56},{56,48},{64,72... | collective-permute-start | bytes 2162696 | tf_op jit(solution)/shard_map/ppermute | solution.py:26
  117.2 5.1 %factor.1 = (f32[3,128,128]{2,1,0:T(8,128)S(1)}, f32[3,512,128]{2,1,0:T(8,128)S(1)}) custom-call(f32[11,128,128]{2,1,0:T(8,128)S(1)} %bitcast.3, f32[3,512,128]{2,1,0:T(8,128)S(1)} %get-tuple-element.61.projected), custom_call_target="tpu_custom_call" | custom-call | flops 6000000000 | bytes 3000000 | tf_op jit(solution)/shard_map/factor/pallas_call | solution.py:394
  122.2 0.8 rotate.1
  123.1 9.2 %all_to_all.34.squares = f32[8,8,128]{2,1,0:T(8,128)S(1)} all-to-all(f32[8,8,128]{2,1,0:T(8,128)S(1)} %get-tuple-element.66), channel_id=1, replica_groups=mesh['fsdp'=32,'tensor'=8] {'tensor'}, dimensions={0} | all-to-all | bytes 65536 | tf_op jit(solution)/shard_map/all_to_all | solution.py:34
  132.3 4.6 %updates.1 = (bf16[512,2048]{1,0:T(8,128)(2,1)}, bf16[512,128]{1,0:T(8,128)(2,1)}, bf16[512,128]{1,0:T(8,128)(2,1)}, bf16[512,2048]{1,0:T(8,128)(2,1)}, bf16[512...) custom-call(bf16[512,2304]{1,0:T(8,128)(2,1)S(1)} %get-tuple-element, ...), custom_call_target="tpu_custom_call" | custom-call | flops 1811939328 | bytes 16000000 | tf_op jit(solution)/shard_map/updates/pallas_call | solution.py:514
  (15 shorter events, 0.1 us)
Async XLA Ops:
  1.4 4.1 %collective-permute-start = (f32[72,128]{1,0:T(8,128)S(1)}, f32[72,128]{1,0:T(8,128)S(1)}, u32[]{:S(2)}, u32[]{:S(2)}) collective-permute-start(f32[72,128]{1,0:T(8,128)S(1)} %pad_maximum_fusion.own), channel_id=1, source_target_pairs={{0,8},{8,0},{16,24},{24,16},{32,40},{40,32},{48,56},{56,48},{64,72... | collective-permute-start | bytes 110600 | tf_op jit(solution)/shard_map/ppermute | solution.py:26
  6.7 17.8 %all-to-all-start = ((f32[16,144,128]{2,1,0:T(8,128)}), f32[16,144,128]{2,1,0:T(8,128)S(1)}, u32[]{:S(2)}, u32[]{:S(2)}) async-start(f32[16,144,128]{2,1,0:T(8,128)} %repeat_bases.1), calls=%async_computation | async-start | bytes 2359296 | tf_op jit(solution)/shard_map/all_to_all | solution.py:30
  11.8 1.6 %copy-start.1 = (bf16[512,2048]{1,0:T(8,128)(2,1)S(1)}, bf16[512,2048]{1,0:T(8,128)(2,1)}, u32[]{:S(2)}) copy-start(bf16[512,2048]{1,0:T(8,128)(2,1)} %mq.2) | copy-start | bytes 6291460
  13.4 1.6 %copy-start.2 = (bf16[512,2048]{1,0:T(8,128)(2,1)S(1)}, bf16[512,2048]{1,0:T(8,128)(2,1)}, u32[]{:S(2)}) copy-start(bf16[512,2048]{1,0:T(8,128)(2,1)} %gq.3) | copy-start | bytes 6291460
  14.9 0.9 copy-start.4
  15.9 0.9 copy-start.5
  16.8 0.9 copy-start.6
  17.7 0.9 copy-start.7
  24.5 1.7 %copy-start = (bf16[512,2304]{1,0:T(8,128)(2,1)S(1)}, bf16[512,2304]{1,0:T(8,128)(2,1)}, u32[]{:S(2)}) copy-start(bf16[512,2304]{1,0:T(8,128)(2,1)} %get-tuple-element.54.low) | copy-start | bytes 7077892
  70.5 11.1 %collective-permute-start.1 = (f32[11,128,128]{2,1,0:T(8,128)S(1)}, f32[11,128,128]{2,1,0:T(8,128)S(1)}, u32[]{:S(2)}, u32[]{:S(2)}) collective-permute-start(f32[11,128,128]{2,1,0:T(8,128)S(1)} %get-tuple-element.60), channel_id=1, source_target_pairs={{0,8},{8,0},{16,24},{24,16},{32,40},{40,32},{48,56},{56,48},{64,72... | collective-permute-start | bytes 2162696 | tf_op jit(solution)/shard_map/ppermute | solution.py:26
  114.2 8.0 %collective-permute-start.2 = (f32[11,128,128]{2,1,0:T(8,128)S(1)}, f32[11,128,128]{2,1,0:T(8,128)S(1)}, u32[]{:S(2)}, u32[]{:S(2)}) collective-permute-start(f32[11,128,128]{2,1,0:T(8,128)S(1)} %bitcast.2), channel_id=1, source_target_pairs={{0,8},{8,0},{16,24},{24,16},{32,40},{40,32},{48,56},{56,48},{64,72... | collective-permute-start | bytes 2162696 | tf_op jit(solution)/shard_map/ppermute | solution.py:26
  117.2 15.1 %copy-start.3 = (bf16[512,2048]{1,0:T(8,128)(2,1)S(1)}, bf16[512,2048]{1,0:T(8,128)(2,1)}, u32[]{:S(2)}) copy-start(bf16[512,2048]{1,0:T(8,128)(2,1)} %wq.1) | copy-start | bytes 6291460
  117.2 15.1 %copy-start.8 = (bf16[512,128]{1,0:T(8,128)(2,1)S(1)}, bf16[512,128]{1,0:T(8,128)(2,1)}, u32[]{:S(2)}) copy-start(bf16[512,128]{1,0:T(8,128)(2,1)} %wk.1) | copy-start | bytes 393220
  117.2 15.1 %copy-start.9 = (bf16[512,128]{1,0:T(8,128)(2,1)S(1)}, bf16[512,128]{1,0:T(8,128)(2,1)}, u32[]{:S(2)}) copy-start(bf16[512,128]{1,0:T(8,128)(2,1)} %wv.1) | copy-start | bytes 393220

commit v9 on v8

--- a/solution.py
+++ b/solution.py
@@ -68,23 +68,27 @@
 ):
     @pl.when(lax.rem(lax.axis_index("fsdp"), 2) == 0)
     def _():
-        fetches = []
-        for i, ((lo, hi), moment, grad) in enumerate(zip(SPLITS, (mq, mk, mv), (gq, gk, gv))):
-            fetches.append(pltpu.make_async_copy(moment, moments.at[:, lo:hi], sems.at[i, 0]))
-            fetches.append(pltpu.make_async_copy(grad, grads.at[:, lo:hi], sems.at[i, 1]))
-        for copy in fetches:
-            copy.start()
-        for copy in fetches:
-            copy.wait()
-        for at in range(0, 512, 64):
-            part = slice(at, at + 64)
-            high[part], low[part] = split(moments[part].astype(F32) + grads[part].astype(F32))
-        stores = [
-            pltpu.make_async_copy(high, high_out, out_sems.at[0]),
-            pltpu.make_async_copy(low, low_out, out_sems.at[1]),
-        ]
-        for copy in stores:
-            copy.start()
+        halves = (slice(0, 256), slice(256, 512))
+        fetches = [[], []]
+        for h, rows in enumerate(halves):
+            for i, ((lo, hi), moment, grad) in enumerate(zip(SPLITS, (mq, mk, mv), (gq, gk, gv))):
+                for j, (source, target) in enumerate(((moment, moments), (grad, grads))):
+                    copy = pltpu.make_async_copy(
+                        source.at[rows], target.at[rows, lo:hi], sems.at[h, i, j]
+                    )
+                    copy.start()
+                    fetches[h].append(copy)
+        stores = []
+        for h, rows in enumerate(halves):
+            for copy in fetches[h]:
+                copy.wait()
+            for at in range(rows.start, rows.stop, 64):
+                part = slice(at, at + 64)
+                high[part], low[part] = split(moments[part].astype(F32) + grads[part].astype(F32))
+            for j, (source, target) in enumerate(((high, high_out), (low, low_out))):
+                copy = pltpu.make_async_copy(source.at[rows], target.at[rows], out_sems.at[h, j])
+                copy.start()
+                stores.append(copy)
         for copy in stores:
             copy.wait()
 
@@ -97,7 +101,7 @@
         out_specs=[anywhere] * 2,
         out_shape=TERMS,
         scratch_shapes=[pltpu.VMEM((512, 2304), BF16)] * 4
-        + [pltpu.SemaphoreType.DMA((3, 2)), pltpu.SemaphoreType.DMA((2,))],
+        + [pltpu.SemaphoreType.DMA((2, 3, 2)), pltpu.SemaphoreType.DMA((2, 2))],
         compiler_params=pltpu.CompilerParams(vmem_limit_bytes=EARLY_LIMIT),
         name="early_blend_terms",
     )(*(x for group in zip(moments, grads) for x in group))

time: 138 us -> 139 us (level)
  no operation moved by 1% of the time
where the time goes in v9:
time: 139 us
  blocking collectives  84.5 us (61%)
  starting transfers between devices  20.6 us (15%)
  Pallas kernels  18.7 us (13%)
  local copies, waits for them, and re-layouts  7.59 us (5%)
  waiting for transfers between devices  5.62 us (4%)
    all_to_all x3, blocking collectives, tensor_exchange(): return lax.all_to_all(x, 'tensor', 0, 0, tiled=True)  51 us
    all_to_all x2, blocking collectives, plane_exchange(): return lax.all_to_all(x, 'fsdp', 0, 0, tiled=True, axis_index_groups=PLANE)  33.5 us
    ppermute x3, starting transfers between devices, swap_core(): return lax.ppermute(x, 'fsdp', SIBLING)  15.6 us
    unnamed x20, local copies, waits for them, and re-layouts  7.59 us
    pallas_call x1, Pallas kernels, factor(): pl.pallas_call(factor_kernel, in_specs=[VMEM] * 2, out_specs=[VMEM] * 2,...  5.05 us
    all_to_all x1, starting transfers between devices, plane_exchange(): return lax.all_to_all(x, 'fsdp', 0, 0, tiled=True, axis_index_groups=PLANE)  5.03 us
    pallas_call x1, Pallas kernels, updates(): pl.pallas_call(functools.partial(update_kernel, factors), grid=(STEPS,),...  4.65 us
    all_to_all x1, waiting for transfers between devices, plane_exchange(): return lax.all_to_all(x, 'fsdp', 0, 0, tiled=True, axis_index_groups=PLANE)  3.82 us
  transfers between devices with their start and end apart: 4, of which 3 were waited for; matrix products, arithmetic and copies ran while one was open for 0% of the time, Pallas kernels for 6%

profile of v9, /device:TPU:1, one launch (start us, length us, event | category | flops | bytes accessed | tf_op | source)
XLA Modules:
  0.0 138.6 jit_solution(10550840449194831627)
XLA Ops:
  0.6 0.8 pad_maximum_fusion.own
  1.4 3.2 %collective-permute-start = (f32[72,128]{1,0:T(8,128)S(1)}, f32[72,128]{1,0:T(8,128)S(1)}, u32[]{:S(2)}, u32[]{:S(2)}) collective-permute-start(f32[72,128]{1,0:T(8,128)S(1)} %pad_maximum_fusion.own), channel_id=1, source_target_pairs={{0,8},{8,0},{16,24},{24,16},{32,40},{40,32},{48,56},{56,48},{64,72... | collective-permute-start | bytes 110600 | tf_op jit(solution)/shard_map/ppermute | solution.py:26
  4.7 0.9 collective-permute-done.sibling
  5.5 1.1 repeat_bases.1
  6.6 0.1 early_blend_terms.1
  6.8 5.0 %all-to-all-start = ((f32[16,144,128]{2,1,0:T(8,128)}), f32[16,144,128]{2,1,0:T(8,128)S(1)}, u32[]{:S(2)}, u32[]{:S(2)}) async-start(f32[16,144,128]{2,1,0:T(8,128)} %repeat_bases.1), calls=%async_computation | async-start | bytes 2359296 | tf_op jit(solution)/shard_map/all_to_all | solution.py:30
  11.8 1.6 %copy-done.1 = bf16[512,2048]{1,0:T(8,128)(2,1)S(1)} copy-done((bf16[512,2048]{1,0:T(8,128)(2,1)S(1)}, bf16[512,2048]{1,0:T(8,128)(2,1)}, u32[]{:S(2)}) %copy-start.1) | copy-done | bytes 2097176
  13.4 1.6 %copy-done.2 = bf16[512,2048]{1,0:T(8,128)(2,1)S(1)} copy-done((bf16[512,2048]{1,0:T(8,128)(2,1)S(1)}, bf16[512,2048]{1,0:T(8,128)(2,1)}, u32[]{:S(2)}) %copy-start.2) | copy-done | bytes 2097176
  15.0 0.9 copy-done.4
  15.9 0.9 copy-done.5
  16.8 0.9 copy-done.6
  17.7 0.9 copy-done.7
  18.6 2.5 %blend_terms.1 = (bf16[512,2304]{1,0:T(8,128)(2,1)S(1)}, bf16[512,2304]{1,0:T(8,128)(2,1)}) custom-call(bf16[512,2048]{1,0:T(8,128)(2,1)S(1)} %copy-done.1, bf16[512,2048]{1,0:T(8,128)(2,1)S(1)} %copy-done.2, bf16[512,128]{1,0:T(8,128)(2,1)S(1)} %copy-done.4, bf16[512,128]{1,0:T(8,128)(2,1)S(1)} %copy-done.5, bf16[512,128]{1,0:T(8,128)(2,1)S(1)} %copy-done.6, ...), custom_call_target="tpu_custom_call" | custom-call | flops 4718592 | bytes 14000000 | tf_op jit(solution)/shard_map/blend_terms/pallas_call | solution.py:134
  21.1 3.8 %all-to-all-done.gathered = f32[16,144,128]{2,1,0:T(8,128)S(1)} async-done(((f32[16,144,128]{2,1,0:T(8,128)}), f32[16,144,128]{2,1,0:T(8,128)S(1)}, u32[]{:S(2)}, u32[]{:S(2)}) %all-to-all-start) | async-done | bytes 1179680 | tf_op jit(solution)/shard_map/all_to_all | solution.py:30
  24.9 0.9 high_rows.1
  25.8 0.8 copy-done
  26.6 0.8 low_rows.1
  27.4 23.9 %all_to_all.30.parts = f32[8,192,128]{2,1,0:T(8,128)S(1)} all-to-all(f32[8,192,128]{2,1,0:T(8,128)S(1)} %low_rows.1), channel_id=1, replica_groups=mesh['fsdp'=32,'tensor'=8] {'tensor'}, dimensions={0} | all-to-all | bytes 1572864 | tf_op jit(solution)/shard_map/all_to_all | solution.py:34
  51.4 17.9 %all_to_all.31.rows = f32[8,192,128]{2,1,0:T(8,128)S(1)} all-to-all(f32[8,192,128]{2,1,0:T(8,128)S(1)} %own_rows.1), channel_id=1, replica_groups=mesh['fsdp'=32,'tensor'=8] {'tensor'}, dimensions={0} | all-to-all | bytes 1572864 | tf_op jit(solution)/shard_map/all_to_all | solution.py:34
  69.2 1.8 %part_to_send.1 = (f32[11,128,128]{2,1,0:T(8,128)S(1)}, f32[3,512,128]{2,1,0:T(8,128)S(1)}, bf16[3,256,512]{2,1,0:T(8,128)(2,1)S(1)}, f32[2,128,128]{2,1,0:T(8,128)S(1)}) custom-call(bf16[512,2304]{1,0:T(8,128)(2,1)S(1)} %get-tuple-element.53.high, bf16[512,2304]{1,0:T(8,128)(2,1)S(1)} %copy-done, f32[8,192,128]{2,1,0:T(8,128)S(1)} %all_to_all.31.rows), custom_call_target="tpu_custom_call" | custom-call | flops 452984832 | bytes 5000000 | tf_op jit(solution)/shard_map/part_to_send/pallas_call | solution.py:314
  71.0 9.4 %collective-permute-start.1 = (f32[11,128,128]{2,1,0:T(8,128)S(1)}, f32[11,128,128]{2,1,0:T(8,128)S(1)}, u32[]{:S(2)}, u32[]{:S(2)}) collective-permute-start(f32[11,128,128]{2,1,0:T(8,128)S(1)} %get-tuple-element.60), channel_id=1, source_target_pairs={{0,8},{8,0},{16,24},{24,16},{32,40},{40,32},{48,56},{56,48},{64,72... | collective-permute-start | bytes 2162696 | tf_op jit(solution)/shard_map/ppermute | solution.py:26
  80.4 0.9 part_to_keep.1.a
  81.3 0.9 collective-permute-done.1.b
  82.2 0.1 pair_sum.1
  82.3 18.6 %all_to_all.32.parts = f32[16,88,128]{2,1,0:T(8,128)S(1)} all-to-all(f32[16,88,128]{2,1,0:T(8,128)S(1)} %bitcast.5), channel_id=1, replica_groups={{0,16,32,48,64,80,96,112,128,144,160,176,192,208,224,240},{8,24,40,56,7..., dimensions={0} | all-to-all | bytes 1441792 | tf_op jit(solution)/shard_map/all_to_all | solution.py:30
  100.8 0.1 own_share.1
  100.9 14.9 %all_to_all.33 = f32[16,88,128]{2,1,0:T(8,128)S(1)} all-to-all(f32[16,88,128]{2,1,0:T(8,128)S(1)} %own_share.1), channel_id=1, replica_groups={{0,16,32,48,64,80,96,112,128,144,160,176,192,208,224,240},{8,24,40,56,7..., dimensions={0} | all-to-all | bytes 1441792 | tf_op jit(solution)/shard_map/all_to_all | solution.py:30
  115.8 3.0 %collective-permute-start.2 = (f32[11,128,128]{2,1,0:T(8,128)S(1)}, f32[11,128,128]{2,1,0:T(8,128)S(1)}, u32[]{:S(2)}, u32[]{:S(2)}) collective-permute-start(f32[11,128,128]{2,1,0:T(8,128)S(1)} %bitcast.2), channel_id=1, source_target_pairs={{0,8},{8,0},{16,24},{24,16},{32,40},{40,32},{48,56},{56,48},{64,72... | collective-permute-start | bytes 2162696 | tf_op jit(solution)/shard_map/ppermute | solution.py:26
  118.8 5.1 %factor.1 = (f32[3,128,128]{2,1,0:T(8,128)S(1)}, f32[3,512,128]{2,1,0:T(8,128)S(1)}) custom-call(f32[11,128,128]{2,1,0:T(8,128)S(1)} %bitcast.3, f32[3,512,128]{2,1,0:T(8,128)S(1)} %get-tuple-element.61.projected), custom_call_target="tpu_custom_call" | custom-call | flops 6000000000 | bytes 3000000 | tf_op jit(solution)/shard_map/factor/pallas_call | solution.py:398
  123.9 0.8 rotate.1
  124.7 9.2 %all_to_all.34.squares = f32[8,8,128]{2,1,0:T(8,128)S(1)} all-to-all(f32[8,8,128]{2,1,0:T(8,128)S(1)} %get-tuple-element.66), channel_id=1, replica_groups=mesh['fsdp'=32,'tensor'=8] {'tensor'}, dimensions={0} | all-to-all | bytes 65536 | tf_op jit(solution)/shard_map/all_to_all | solution.py:34
  133.9 4.7 %updates.1 = (bf16[512,2048]{1,0:T(8,128)(2,1)}, bf16[512,128]{1,0:T(8,128)(2,1)}, bf16[512,128]{1,0:T(8,128)(2,1)}, bf16[512,2048]{1,0:T(8,128)(2,1)}, bf16[512...) custom-call(bf16[512,2304]{1,0:T(8,128)(2,1)S(1)} %get-tuple-element, ...), custom_call_target="tpu_custom_call" | custom-call | flops 1811939328 | bytes 16000000 | tf_op jit(solution)/shard_map/updates/pallas_call | solution.py:518
  (15 shorter events, 0.1 us)
Async XLA Ops:
  1.4 4.1 %collective-permute-start = (f32[72,128]{1,0:T(8,128)S(1)}, f32[72,128]{1,0:T(8,128)S(1)}, u32[]{:S(2)}, u32[]{:S(2)}) collective-permute-start(f32[72,128]{1,0:T(8,128)S(1)} %pad_maximum_fusion.own), channel_id=1, source_target_pairs={{0,8},{8,0},{16,24},{24,16},{32,40},{40,32},{48,56},{56,48},{64,72... | collective-permute-start | bytes 110600 | tf_op jit(solution)/shard_map/ppermute | solution.py:26
  6.8 18.1 %all-to-all-start = ((f32[16,144,128]{2,1,0:T(8,128)}), f32[16,144,128]{2,1,0:T(8,128)S(1)}, u32[]{:S(2)}, u32[]{:S(2)}) async-start(f32[16,144,128]{2,1,0:T(8,128)} %repeat_bases.1), calls=%async_computation | async-start | bytes 2359296 | tf_op jit(solution)/shard_map/all_to_all | solution.py:30
  11.8 1.6 %copy-start.1 = (bf16[512,2048]{1,0:T(8,128)(2,1)S(1)}, bf16[512,2048]{1,0:T(8,128)(2,1)}, u32[]{:S(2)}) copy-start(bf16[512,2048]{1,0:T(8,128)(2,1)} %mq.2) | copy-start | bytes 6291460
  13.4 1.6 %copy-start.2 = (bf16[512,2048]{1,0:T(8,128)(2,1)S(1)}, bf16[512,2048]{1,0:T(8,128)(2,1)}, u32[]{:S(2)}) copy-start(bf16[512,2048]{1,0:T(8,128)(2,1)} %gq.3) | copy-start | bytes 6291460
  15.0 0.9 copy-start.4
  15.9 0.9 copy-start.5
  16.8 0.9 copy-start.6
  17.7 0.9 copy-start.7
  24.9 1.7 %copy-start = (bf16[512,2304]{1,0:T(8,128)(2,1)S(1)}, bf16[512,2304]{1,0:T(8,128)(2,1)}, u32[]{:S(2)}) copy-start(bf16[512,2304]{1,0:T(8,128)(2,1)} %get-tuple-element.54.low) | copy-start | bytes 7077892
  71.0 11.2 %collective-permute-start.1 = (f32[11,128,128]{2,1,0:T(8,128)S(1)}, f32[11,128,128]{2,1,0:T(8,128)S(1)}, u32[]{:S(2)}, u32[]{:S(2)}) collective-permute-start(f32[11,128,128]{2,1,0:T(8,128)S(1)} %get-tuple-element.60), channel_id=1, source_target_pairs={{0,8},{8,0},{16,24},{24,16},{32,40},{40,32},{48,56},{56,48},{64,72... | collective-permute-start | bytes 2162696 | tf_op jit(solution)/shard_map/ppermute | solution.py:26
  115.8 8.0 %collective-permute-start.2 = (f32[11,128,128]{2,1,0:T(8,128)S(1)}, f32[11,128,128]{2,1,0:T(8,128)S(1)}, u32[]{:S(2)}, u32[]{:S(2)}) collective-permute-start(f32[11,128,128]{2,1,0:T(8,128)S(1)} %bitcast.2), channel_id=1, source_target_pairs={{0,8},{8,0},{16,24},{24,16},{32,40},{40,32},{48,56},{56,48},{64,72... | collective-permute-start | bytes 2162696 | tf_op jit(solution)/shard_map/ppermute | solution.py:26
  118.8 15.1 %copy-start.3 = (bf16[512,2048]{1,0:T(8,128)(2,1)S(1)}, bf16[512,2048]{1,0:T(8,128)(2,1)}, u32[]{:S(2)}) copy-start(bf16[512,2048]{1,0:T(8,128)(2,1)} %wq.1) | copy-start | bytes 6291460
  118.8 15.1 %copy-start.8 = (bf16[512,128]{1,0:T(8,128)(2,1)S(1)}, bf16[512,128]{1,0:T(8,128)(2,1)}, u32[]{:S(2)}) copy-start(bf16[512,128]{1,0:T(8,128)(2,1)} %wk.1) | copy-start | bytes 393220
  118.8 15.1 %copy-start.9 = (bf16[512,128]{1,0:T(8,128)(2,1)S(1)}, bf16[512,128]{1,0:T(8,128)(2,1)}, u32[]{:S(2)}) copy-start(bf16[512,128]{1,0:T(8,128)(2,1)} %wv.1) | copy-start | bytes 393220
